TPU v7x, 32 devices: a whole 2x2x4 slice. The times are simulated.
32 devices in a mesh: grp: 2 (over y), chan: 8 (over z, core), bl: 2 (over x).
Axes of the slice: x: 2, y: 2, z: 4, core: 2. Of those that a mesh axis runs over, the one named last changes fastest.
Arguments:
- patches: bfloat16 [32, 2, 2, 64, 8192], P(None, None, None, ('grp', 'chan'), 'bl'), parts along dimension 3, may hold values from -1.5 to 1.5
- visibilities: float32 [2, 2, 64, 8192], P(None, None, ('grp', 'chan'), 'bl'), parts along dimension 2, may hold values from -6 to 6
- valid: int32 [64, 8192], P(('grp', 'chan'), 'bl'), parts along dimension 0, may hold values 0 or 1
- baseline_stations: int32 [2, 8192], P(None, 'bl'), may hold values from 0 to 511, as said below
- cluster: int32 [32, 1], replicated, may hold values from 0 to 15
- gains: float32 [2, 16, 64, 512], P(None, None, ('grp', 'chan'), 'bl'), parts along dimension 2, may hold values from -1 to 1
Outputs:
- new_gains: float32 [2, 16, 64, 512], P(None, None, ('grp', 'chan'), 'bl'), parts along dimension 2
There are 2 independent parts, one for each index of `grp`. A program takes and returns all parts, laid end to end along the dimension named above; an argument that names none is the same for every part. Nothing has to cross between parts.
Inputs may be any that keep to these rules, and one draw needn't show every extreme that they name: `baseline_stations`: row 0 holds each baseline's lower station and row 1 its higher one; the two always differ. `cluster`: every direction has at least one patch.
All inputs are finite; a program needn't handle non-finite values. No bound on the sum of `valid` on one device may be relied on, other than what follows from the above.
Results may differ from a plain program's by a relative error of at most 0.0015.
Values may be sent and summed in bfloat16 or wider, within the bound.
No kernel may reach another device: no remote copies, remote signals or barrier semaphores. Data moves between devices by JAX's collectives and lax.ppermute only.
A program may use at most 64 MiB of HBM per device.

v0:
```python
from functools import partial

import jax
import jax.numpy as jnp
from jax import lax
from jax.experimental import pallas as pl
from jax.experimental.pallas import tpu as pltpu
from jax.sharding import PartitionSpec as P

DIRECTIONS = 16
SKY_PATCHES = 32
TIME_SLOTS = 2
ITERS = 2
LANES = 128
PREP_CHUNK = 1024
SWEEP_CHUNK = 1024
HALF = DIRECTIONS // 2
HIGHEST = lax.Precision.HIGHEST
F32, BF16 = jnp.float32, jnp.bfloat16


def basis_at(channel, total):
    ratio = 1.0 + channel.astype(F32) / total
    inverse = 4.0 / ratio - 3.0
    return jnp.ones_like(inverse), inverse, 2.0 * inverse * inverse - 1.0


def iotas(shape):
    return lax.broadcasted_iota(jnp.int32, shape, 0), lax.broadcasted_iota(jnp.int32, shape, 1)


def pick(index, values):
    out = values[-1]
    for k in range(len(values) - 2, -1, -1):
        out = jnp.where(index == k, values[k], out)
    return out


def moment_matrix(terms, channels, total, chan):
    row, col = iotas((2 * terms * HALF, DIRECTIONS * channels))
    block = row // HALF
    half = (block >= terms).astype(jnp.int32)
    term = block - half * terms
    direction = jnp.bitwise_xor(half, lax.rem(chan, 2)) * HALF + row % HALF
    one, first, second = basis_at(chan * channels + col % channels, total)
    if terms == 6:
        values = (one, first, second, first * first, first * second, second * second)
    else:
        values = (one, first, second)
    return jnp.where(direction == col // channels, pick(term, values), 0.0)


def fit_matrix(half, channels, total, chan):
    per = DIRECTIONS * channels
    row, col = iotas((2 * per, 6 * HALF))
    place = row % per
    block = col // HALF
    direction = jnp.bitwise_xor(half, lax.rem(chan, 2)) * HALF + col % HALF
    basis = basis_at(chan * channels + place % channels, total)
    same = (direction == place // channels) & (row // per == block // 3)
    return jnp.where(same, pick(block % 3, basis), 0.0)


def prep_kernel(total, channels, cluster_ref, patches_ref, valid_ref, model_ref, power_ref,
                normal_ref, right_ref, fit_ref, order_ref, start_ref):
    chan = lax.axis_index("chan")

    @pl.when(pl.program_id(0) == 0)
    def _():
        for d in range(DIRECTIONS + 1):
            start_ref[d] = 0

        @pl.loop(0, SKY_PATCHES)
        def _(q):
            d = cluster_ref[q]
            start_ref[d + 1] = start_ref[d + 1] + 1

        for d in range(DIRECTIONS):
            start_ref[d + 1] = start_ref[d + 1] + start_ref[d]
        for d in range(DIRECTIONS):
            start_ref[DIRECTIONS + 1 + d] = start_ref[d]

        @pl.loop(0, SKY_PATCHES)
        def _(q):
            d = cluster_ref[q]
            place = start_ref[DIRECTIONS + 1 + d]
            order_ref[place] = q
            start_ref[DIRECTIONS + 1 + d] = place + 1

        normal_ref[...] = moment_matrix(6, channels, total, chan)
        right_ref[...] = moment_matrix(3, channels, total, chan)
        fit_ref[0] = fit_matrix(0, channels, total, chan)
        fit_ref[1] = fit_matrix(1, channels, total, chan)

    width = valid_ref.shape[1]
    validity = valid_ref[...].astype(F32)
    parts = [(x, t) for x in range(2) for t in range(TIME_SLOTS)]
    for d in range(DIRECTIONS):

        def add(i, sums):
            q = order_ref[i]
            return tuple(
                s + patches_ref[q, x, t].astype(F32) for s, (x, t) in zip(sums, parts)
            )

        zero = jnp.zeros((channels, width), F32)
        sums = lax.fori_loop(start_ref[d], start_ref[d + 1], add, (zero,) * len(parts))
        power = sums[0] * sums[0]
        for s in sums[1:]:
            power = power + s * s
        rows = slice(d * channels, (d + 1) * channels)
        for s, (x, t) in zip(sums, parts):
            model_ref[x, t, rows, :] = s
        power_ref[rows, :] = power * validity


def prepare(cluster, patches, valid, total):
    channels, baselines = valid.shape
    chunk = min(PREP_CHUNK, baselines)
    per = DIRECTIONS * channels
    whole = lambda shape: pl.BlockSpec(shape, lambda i: (0,) * len(shape))
    return pl.pallas_call(
        partial(prep_kernel, total, channels),
        grid=(baselines // chunk,),
        in_specs=[
            pl.BlockSpec(memory_space=pltpu.SMEM),
            pl.BlockSpec((SKY_PATCHES, 2, TIME_SLOTS, channels, chunk), lambda i: (0, 0, 0, 0, i)),
            pl.BlockSpec((channels, chunk), lambda i: (0, i)),
        ],
        out_specs=[
            pl.BlockSpec((2, TIME_SLOTS, per, chunk), lambda i: (0, 0, 0, i)),
            pl.BlockSpec((per, chunk), lambda i: (0, i)),
            whole((12 * HALF, per)),
            whole((6 * HALF, per)),
            whole((2, 2 * per, 6 * HALF)),
        ],
        out_shape=[
            jax.ShapeDtypeStruct((2, TIME_SLOTS, per, baselines), F32),
            jax.ShapeDtypeStruct((per, baselines), F32),
            jax.ShapeDtypeStruct((12 * HALF, per), F32),
            jax.ShapeDtypeStruct((6 * HALF, per), F32),
            jax.ShapeDtypeStruct((2, 2 * per, 6 * HALF), F32),
        ],
        scratch_shapes=[
            pltpu.SMEM((SKY_PATCHES,), jnp.int32),
            pltpu.SMEM((2 * DIRECTIONS + 1,), jnp.int32),
        ],
        compiler_params=pltpu.CompilerParams(vmem_limit_bytes=32 << 20),
        name="prepare",
    )(cluster, patches, valid)


def fitted_values(fit_ref, coefs):
    out = jnp.dot(fit_ref[0], coefs[0], precision=HIGHEST, preferred_element_type=F32)
    return out + jnp.dot(fit_ref[1], coefs[1], precision=HIGHEST, preferred_element_type=F32)


def sweep_kernel(first, blocks, owned, *refs):
    if first:
        gain_refs, refs = refs[:blocks], refs[blocks:]
    else:
        (before_ref, fit_ref, own_coef_ref, other_coef_ref), refs = refs[:4], refs[4:]
    (stations_ref, model_ref, power_ref, valid_ref, visible_ref, normal_ref, right_ref,
     own_ref, other_ref, current_ref, rounded_ref, sums_ref, near_ref, far_ref,
     upper_ref, lower_ref) = refs
    step = pl.program_id(0)
    channels, width = valid_ref.shape
    per = DIRECTIONS * channels
    stations = blocks * owned

    @pl.when(step == 0)
    def _():
        if first:
            for k in range(blocks):
                for x in range(2):
                    for d in range(DIRECTIONS):
                        row = x * per + d * channels
                        current_ref[row:row + channels, k * owned:(k + 1) * owned] = gain_refs[k][x, d]
        else:
            fitted = fitted_values(fit_ref, (own_coef_ref[...], other_coef_ref[...]))
            current_ref[...] = 0.5 * (before_ref[...] + fitted)
        rounded_ref[...] = current_ref[...].astype(BF16)
        sums_ref[...] = jnp.zeros_like(sums_ref)

    shift = lax.axis_index("bl") * owned
    place = stations_ref[...] - shift
    place = jnp.where(place < 0, place + stations, place)
    ids = lax.broadcasted_iota(jnp.int32, (stations, width), 0)
    first_pick = (ids == place[0:1, :]).astype(BF16)
    second_pick = (ids == place[1:2, :]).astype(BF16)
    rounded = rounded_ref[...]
    near_ref[...] = jnp.dot(rounded, first_pick, preferred_element_type=F32)
    far_ref[...] = jnp.dot(rounded, second_pick, preferred_element_type=F32)

    fold = 8 // channels
    for tile in range(width // LANES):
        lanes = slice(tile * LANES, (tile + 1) * LANES)
        pred = [jnp.zeros((8, LANES), F32) for _ in range(2 * TIME_SLOTS)]
        for row in range(0, per, 8):
            re, im = slice(row, row + 8), slice(per + row, per + row + 8)
            pr, pi, qr, qi = near_ref[re, lanes], near_ref[im, lanes], far_ref[re, lanes], far_ref[im, lanes]
            gr = pr * qr + pi * qi
            gi = pi * qr - pr * qi
            for t in range(TIME_SLOTS):
                mr, mi = model_ref[0, t, re, lanes], model_ref[1, t, re, lanes]
                pred[2 * t] = pred[2 * t] + (gr * mr - gi * mi)
                pred[2 * t + 1] = pred[2 * t + 1] + (gr * mi + gi * mr)
        validity = valid_ref[:, lanes].astype(F32)
        resid = []
        for t in range(TIME_SLOTS):
            for x in range(2):
                p = pred[2 * t + x]
                total = p[0:channels]
                for k in range(1, fold):
                    total = total + p[k * channels:(k + 1) * channels]
                r = (visible_ref[x, t, :, lanes] - total) * validity
                resid.append(jnp.concatenate([r] * fold, axis=0))
        for row in range(0, per, 8):
            re, im = slice(row, row + 8), slice(per + row, per + row + 8)
            third = slice(2 * per + row, 2 * per + row + 8)
            pr, pi, qr, qi = near_ref[re, lanes], near_ref[im, lanes], far_ref[re, lanes], far_ref[im, lanes]
            ar = ai = None
            for t in range(TIME_SLOTS):
                mr, mi = model_ref[0, t, re, lanes], model_ref[1, t, re, lanes]
                rr, ri = resid[2 * t], resid[2 * t + 1]
                br = mr * rr + mi * ri
                bi = mr * ri - mi * rr
                ar, ai = (br, bi) if ar is None else (ar + br, ai + bi)
            power = power_ref[re, lanes]
            upper_ref[re, lanes] = qr * ar - qi * ai
            upper_ref[im, lanes] = qr * ai + qi * ar
            upper_ref[third, lanes] = power * (qr * qr + qi * qi)
            lower_ref[re, lanes] = pr * ar + pi * ai
            lower_ref[im, lanes] = pi * ar - pr * ai
            lower_ref[third, lanes] = power * (pr * pr + pi * pi)
    over = (((1,), (1,)), ((), ()))
    sums_ref[...] += lax.dot_general(
        upper_ref[...].astype(BF16), first_pick, over, preferred_element_type=F32
    ) + lax.dot_general(
        lower_ref[...].astype(BF16), second_pick, over, preferred_element_type=F32
    )

    @pl.when(step == pl.num_programs(0) - 1)
    def _():
        weight = sums_ref[2 * per:3 * per, :] + 1.0 / blocks
        product = partial(jnp.dot, precision=HIGHEST, preferred_element_type=F32)
        normal = product(normal_ref[...], weight)
        right = [
            product(right_ref[...], weight * current_ref[x * per:(x + 1) * per, :] + sums_ref[x * per:(x + 1) * per, :])
            for x in range(2)
        ]
        for half, out in enumerate((own_ref, other_ref)):
            out[0:6 * HALF, :] = normal[half * 6 * HALF:(half + 1) * 6 * HALF, :]
            for x in range(2):
                out[(6 + 3 * x) * HALF:(9 + 3 * x) * HALF, :] = right[x][half * 3 * HALF:(half + 1) * 3 * HALF, :]


def sweep(first, gains, stations, model, power, valid, visible, normal, right, owned, blocks):
    channels, baselines = valid.shape
    per = DIRECTIONS * channels
    chunk = min(SWEEP_CHUNK, baselines)
    count = owned * blocks
    whole = lambda shape: pl.BlockSpec(shape, lambda i: (0,) * len(shape))
    return pl.pallas_call(
        partial(sweep_kernel, first, blocks, owned),
        grid=(baselines // chunk,),
        in_specs=[whole(g.shape) for g in gains] + [
            pl.BlockSpec((2, chunk), lambda i: (0, i)),
            pl.BlockSpec((2, TIME_SLOTS, per, chunk), lambda i: (0, 0, 0, i)),
            pl.BlockSpec((per, chunk), lambda i: (0, i)),
            pl.BlockSpec((channels, chunk), lambda i: (0, i)),
            pl.BlockSpec((2, TIME_SLOTS, channels, chunk), lambda i: (0, 0, 0, i)),
            whole(normal.shape),
            whole(right.shape),
        ],
        out_specs=[whole((12 * HALF, count)), whole((12 * HALF, count)), whole((2 * per, count))],
        out_shape=[
            jax.ShapeDtypeStruct((12 * HALF, count), F32),
            jax.ShapeDtypeStruct((12 * HALF, count), F32),
            jax.ShapeDtypeStruct((2 * per, count), F32),
        ],
        scratch_shapes=[
            pltpu.VMEM((2 * per, count), BF16),
            pltpu.VMEM((3 * per, count), F32),
            pltpu.VMEM((2 * per, chunk), F32),
            pltpu.VMEM((2 * per, chunk), F32),
            pltpu.VMEM((3 * per, chunk), F32),
            pltpu.VMEM((3 * per, chunk), F32),
        ],
        compiler_params=pltpu.CompilerParams(vmem_limit_bytes=40 << 20),
        name="sweep",
    )(*gains, stations, model, power, valid, visible, normal, right)


def final_kernel(channels, before_ref, fit_ref, own_ref, other_ref, out_ref):
    per = DIRECTIONS * channels
    result = 0.5 * (before_ref[...] + fitted_values(fit_ref, (own_ref[...], other_ref[...])))
    for x in range(2):
        for d in range(DIRECTIONS):
            row = x * per + d * channels
            out_ref[x, d] = result[row:row + channels, :]


def finish(before, fit, own, other, channels):
    owned = own.shape[1]
    return pl.pallas_call(
        partial(final_kernel, channels),
        grid=(1,),
        in_specs=[
            pl.BlockSpec((before.shape[0], owned), lambda i: (0, 0)),
            pl.BlockSpec(fit.shape, lambda i: (0, 0, 0)),
            pl.BlockSpec(own.shape, lambda i: (0, 0)),
            pl.BlockSpec(other.shape, lambda i: (0, 0)),
        ],
        out_specs=pl.BlockSpec((2, DIRECTIONS, channels, owned), lambda i: (0, 0, 0, 0)),
        out_shape=jax.ShapeDtypeStruct((2, DIRECTIONS, channels, owned), F32),
        name="finish",
    )(before, fit, own, other)


def solve(moments):
    m = [moments[k * HALF:(k + 1) * HALF] for k in range(12)]
    low_aa = jnp.sqrt(m[0])
    low_ba = m[1] / low_aa
    low_ca = m[2] / low_aa
    low_bb = jnp.sqrt(m[3] - low_ba * low_ba)
    low_cb = (m[4] - low_ca * low_ba) / low_bb
    low_cc = jnp.sqrt(m[5] - low_ca * low_ca - low_cb * low_cb)
    out = []
    for x in range(2):
        r = m[6 + 3 * x:9 + 3 * x]
        first_y = r[0] / low_aa
        second_y = (r[1] - low_ba * first_y) / low_bb
        third_y = (r[2] - low_ca * first_y - low_cb * second_y) / low_cc
        third_x = third_y / low_cc
        second_x = (second_y - low_cb * third_x) / low_bb
        first_x = (first_y - low_ba * second_x - low_ca * third_x) / low_aa
        out += [first_x, second_x, third_x]
    return jnp.concatenate(out, axis=0)


def other_core(value):
    count = lax.axis_size("chan")
    return lax.ppermute(value, "chan", [(j, j ^ 1) for j in range(count)])


def from_later(value, k):
    count = lax.axis_size("bl")
    return lax.ppermute(value, "bl", [((j + k) % count, j) for j in range(count)])


def over_chips(value):
    count = lax.axis_size("chan")
    chips = count // 2
    swap = lambda v, k: lax.ppermute(v, "chan", [(j, j ^ (2 * k)) for j in range(count)])
    if chips <= 4:
        parts = [swap(value, k) for k in range(1, chips)]
        for part in parts:
            value = value + part
        return value
    k = 1
    while k < chips:
        value = value + swap(value, k)
        k *= 2
    return value


def body(patches, visibilities, valid, baseline_stations, cluster, gains):
    channels = visibilities.shape[2]
    owned = gains.shape[3]
    blocks = lax.axis_size("bl")
    total = channels * lax.axis_size("chan")
    all_gains = [gains] + [from_later(gains, k) for k in range(1, blocks)]
    model, power, normal, right, fit = prepare(cluster[:, 0], patches, valid, total)
    common = (baseline_stations, model, power, valid, visibilities, normal, right, owned, blocks)
    inputs = all_gains
    for number in range(ITERS):
        own, other, current = sweep(number == 0, inputs, *common)
        mine = own + other_core(other)
        part = lambda k: mine[:, k * owned:(k + 1) * owned]
        kept = part(0)
        for k in range(1, blocks):
            kept = kept + from_later(part(blocks - k), k)
        coefs = solve(over_chips(kept))
        if number < ITERS - 1:
            coefs = jnp.concatenate([coefs] + [from_later(coefs, k) for k in range(1, blocks)], axis=1)
        inputs = [current, fit, coefs, other_core(coefs)]
    return finish(*inputs, channels)


def solution(mesh):
    in_specs = (
        P(None, None, None, ("grp", "chan"), "bl"),
        P(None, None, ("grp", "chan"), "bl"),
        P(("grp", "chan"), "bl"),
        P(None, "bl"),
        P(),
        P(None, None, ("grp", "chan"), "bl"),
    )
    out_specs = P(None, None, ("grp", "chan"), "bl")
    return jax.shard_map(body, mesh=mesh, in_specs=in_specs, out_specs=out_specs, check_vma=False)
```

profile of v0, /device:TPU:0, one launch (start us, length us, event | category | flops | bytes accessed | tf_op | source)
XLA Modules:
  0.0 73.3 jit_solution(4796708648916761754)
XLA Ops:
  0.0 2.9 %collective-permute-start = (f32[2,16,4,256]{3,2,1,0:T(4,128)}, f32[2,16,4,256]{3,2,1,0:T(4,128)S(1)}, u32[]{:S(2)}, u32[]{:S(2)}) collective-permute-start(f32[2,16,4,256]{3,2,1,0:T(4,128)} %refs_0_.1), channel_id=1, source_target_pairs={{1,0},{0,1},{3,2},{2,3},{5,4},{4,5},{7,6},{6,7},{9,8},{8,9},{11,10... | collective-permute-start | bytes 393224 | tf_op jit(solution)/shard_map/ppermute | solution.py:349
  2.9 2.2 %copy-done = bf16[32,2,2,4,4096]{4,3,2,1,0:T(4,128)(2,1)S(1)} copy-done((bf16[32,2,2,4,4096]{4,3,2,1,0:T(4,128)(2,1)S(1)}, bf16[32,2,2,4,4096]{4,3,2,1,0:T(4,128)(2,1)}, u32[]{:S(2)}) %copy-start) | copy-done | bytes 4194328
  5.1 0.8 %copy-done.2 = s32[4,4096]{1,0:T(4,128)S(1)} copy-done((s32[4,4096]{1,0:T(4,128)S(1)}, s32[4,4096]{1,0:T(4,128)}, u32[]{:S(2)}) %copy-start.2) | copy-done | bytes 65560
  6.0 0.7 copy-done.8
  6.6 4.4 %prepare.1 = (f32[2,2,64,4096]{3,2,1,0:T(8,128)S(1)}, f32[64,4096]{1,0:T(8,128)S(1)}, f32[96,64]{1,0:T(8,128)S(1)}, f32[48,64]{1,0:T(8,128)S(1)}, f32[2,128,48]{2,1,0:T(8,128)S(1)}) custom-call(s32[32]{0:T(128)S(1)} %bitcast.1, bf16[32,2,2,4,4096]{4,3,2,1,0:T(4,128)(2,1)S(1)} %copy-done, s32[4,4096]{1,0:T(4,128)S(1)} %copy-done.2), custom_call_target="tpu_custom_call" | custom-call | tf_op jit(solution)/shard_map/prepare/pallas_call | solution.py:122
  11.1 7.9 %sweep.2 = (f32[96,512]{1,0:T(8,128)S(1)}, f32[96,512]{1,0:T(8,128)S(1)}, f32[128,512]{1,0:T(8,128)S(1)}) custom-call(f32[2,16,4,256]{3,2,1,0:T(4,128)S(1)} %copy-done.7, f32[2,16,4,256]{3,2,1,0:T(4,128)S(1)} %collective-permute-done.refs_1_, s32[2,4096]{1,0:T(2,128)S(1)} %copy-done.6, f32[2,2,64,4096]{3,2,1,0:T(8,128)S(1)} %get-tuple-element.16.refs_3_.refs_5_, ...), custom_call_target="tpu_custom_call" | custom-call | tf_op jit(solution)/shard_map/sweep/pallas_call | solution.py:264
  19.1 0.1 collective-permute-start.1
  19.1 1.4 %collective-permute-done.1 = f32[96,512]{1,0:T(8,128)S(1)} collective-permute-done((f32[96,512]{1,0:T(8,128)S(1)}, f32[96,512]{1,0:T(8,128)S(1)}, u32[]{:S(2)}, u32[]{:S(2)}) %collective-permute-start.1) | collective-permute-done | bytes 196640 | tf_op jit(solution)/shard_map/ppermute | solution.py:344
  20.6 0.1 collective-permute-start.2
  20.7 4.8 %collective-permute-done.2 = f32[96,256]{1,0:T(8,128)S(1)} collective-permute-done((f32[96,256]{1,0:T(8,128)S(1)}, f32[96,256]{1,0:T(8,128)S(1)}, u32[]{:S(2)}, u32[]{:S(2)}) %collective-permute-start.2) | collective-permute-done | bytes 98336 | tf_op jit(solution)/shard_map/ppermute | solution.py:349
  25.5 3.7 %collective-permute-start.5 = (f32[96,256]{1,0:T(8,128)S(1)}, f32[96,256]{1,0:T(8,128)S(1)}, u32[]{:S(2)}, u32[]{:S(2)}) collective-permute-start(f32[96,256]{1,0:T(8,128)S(1)} %slice_add_fusion.1), channel_id=1, source_target_pairs={{0,12},{2,14},{4,8},{6,10},{8,4},{10,6},{12,0},{14,2},{1,13},{3,15... | collective-permute-start | bytes 294920 | tf_op jit(solution)/shard_map/ppermute | solution.py:355
  29.2 0.8 %collective-permute-start.3 = (f32[96,256]{1,0:T(8,128)S(1)}, f32[96,256]{1,0:T(8,128)S(1)}, u32[]{:S(2)}, u32[]{:S(2)}) collective-permute-start(f32[96,256]{1,0:T(8,128)S(1)} %slice_add_fusion.1), channel_id=1, source_target_pairs={{0,4},{2,6},{4,0},{6,2},{8,12},{10,14},{12,8},{14,10},{1,5},{3,7},... | collective-permute-start | bytes 294920 | tf_op jit(solution)/shard_map/ppermute | solution.py:355
  30.0 3.0 %collective-permute-done.5 = f32[96,256]{1,0:T(8,128)S(1)} collective-permute-done((f32[96,256]{1,0:T(8,128)S(1)}, f32[96,256]{1,0:T(8,128)S(1)}, u32[]{:S(2)}, u32[]{:S(2)}) %collective-permute-start.5) | collective-permute-done | bytes 98336 | tf_op jit(solution)/shard_map/ppermute | solution.py:355
  33.0 4.0 %collective-permute-done.4 = f32[96,256]{1,0:T(8,128)S(1)} collective-permute-done((f32[96,256]{1,0:T(8,128)S(1)}, f32[96,256]{1,0:T(8,128)S(1)}, u32[]{:S(2)}, u32[]{:S(2)}) %collective-permute-start.4) | collective-permute-done | bytes 98336 | tf_op jit(solution)/shard_map/ppermute | solution.py:355
  37.1 0.6 collective-permute-start.6
  37.7 3.6 %collective-permute-done.6 = f32[48,256]{1,0:T(8,128)S(1)} collective-permute-done((f32[48,256]{1,0:T(8,128)S(1)}, f32[48,256]{1,0:T(8,128)S(1)}, u32[]{:S(2)}, u32[]{:S(2)}) %collective-permute-start.6) | collective-permute-done | bytes 49184 | tf_op jit(solution)/shard_map/ppermute | solution.py:349
  41.3 0.1 collective-permute-start.7
  41.4 1.3 %collective-permute-done.7.refs_3_ = f32[48,512]{1,0:T(8,128)S(1)} collective-permute-done((f32[48,512]{1,0:T(8,128)S(1)}, f32[48,512]{1,0:T(8,128)S(1)}, u32[]{:S(2)}, u32[]{:S(2)}) %collective-permute-start.7) | collective-permute-done | bytes 98336 | tf_op jit(solution)/shard_map/ppermute | solution.py:344
  42.7 8.4 %sweep.3 = (f32[96,512]{1,0:T(8,128)S(1)}, f32[96,512]{1,0:T(8,128)S(1)}, f32[128,512]{1,0:T(8,128)S(1)}) custom-call(f32[128,512]{1,0:T(8,128)S(1)} %get-tuple-element.20.refs_0_, f32[2,128,48]{2,1,0:T(8,128)S(1)} %get-tuple-element.21.refs_1_.fit_ref, f32[48,512]{1,0:T(8,128)S(1)} %pad_maximum_fusion.refs_2_, ...), custom_call_target="tpu_custom_call" | custom-call | tf_op jit(solution)/shard_map/sweep/pallas_call | solution.py:264
  51.1 0.7 copy-done.5
  51.8 0.2 collective-permute-start.8
  51.9 1.3 %collective-permute-done.8 = f32[96,512]{1,0:T(8,128)S(1)} collective-permute-done((f32[96,512]{1,0:T(8,128)S(1)}, f32[96,512]{1,0:T(8,128)S(1)}, u32[]{:S(2)}, u32[]{:S(2)}) %collective-permute-start.8) | collective-permute-done | bytes 196640 | tf_op jit(solution)/shard_map/ppermute | solution.py:344
  53.3 0.6 collective-permute-start.9
  53.9 4.3 %collective-permute-done.9 = f32[96,256]{1,0:T(8,128)S(1)} collective-permute-done((f32[96,256]{1,0:T(8,128)S(1)}, f32[96,256]{1,0:T(8,128)S(1)}, u32[]{:S(2)}, u32[]{:S(2)}) %collective-permute-start.9) | collective-permute-done | bytes 98336 | tf_op jit(solution)/shard_map/ppermute | solution.py:349
  58.2 2.6 %collective-permute-start.12 = (f32[96,256]{1,0:T(8,128)S(1)}, f32[96,256]{1,0:T(8,128)S(1)}, u32[]{:S(2)}, u32[]{:S(2)}) collective-permute-start(f32[96,256]{1,0:T(8,128)S(1)} %slice_add_fusion), channel_id=1, source_target_pairs={{0,12},{2,14},{4,8},{6,10},{8,4},{10,6},{12,0},{14,2},{1,13},{3,15... | collective-permute-start | bytes 294920 | tf_op jit(solution)/shard_map/ppermute | solution.py:355
  60.8 1.9 %collective-permute-start.10 = (f32[96,256]{1,0:T(8,128)S(1)}, f32[96,256]{1,0:T(8,128)S(1)}, u32[]{:S(2)}, u32[]{:S(2)}) collective-permute-start(f32[96,256]{1,0:T(8,128)S(1)} %slice_add_fusion), channel_id=1, source_target_pairs={{0,4},{2,6},{4,0},{6,2},{8,12},{10,14},{12,8},{14,10},{1,5},{3,7},... | collective-permute-start | bytes 294920 | tf_op jit(solution)/shard_map/ppermute | solution.py:355
  62.7 3.1 %collective-permute-done.12 = f32[96,256]{1,0:T(8,128)S(1)} collective-permute-done((f32[96,256]{1,0:T(8,128)S(1)}, f32[96,256]{1,0:T(8,128)S(1)}, u32[]{:S(2)}, u32[]{:S(2)}) %collective-permute-start.12) | collective-permute-done | bytes 98336 | tf_op jit(solution)/shard_map/ppermute | solution.py:355
  65.8 3.4 %collective-permute-done.11 = f32[96,256]{1,0:T(8,128)S(1)} collective-permute-done((f32[96,256]{1,0:T(8,128)S(1)}, f32[96,256]{1,0:T(8,128)S(1)}, u32[]{:S(2)}, u32[]{:S(2)}) %collective-permute-start.11) | collective-permute-done | bytes 98336 | tf_op jit(solution)/shard_map/ppermute | solution.py:355
  69.4 0.1 collective-permute-start.13
  69.5 1.2 %collective-permute-done.13.other_ref = f32[48,256]{1,0:T(8,128)S(1)} collective-permute-done((f32[48,256]{1,0:T(8,128)S(1)}, f32[48,256]{1,0:T(8,128)S(1)}, u32[]{:S(2)}, u32[]{:S(2)}) %collective-permute-start.13) | collective-permute-done | bytes 49184 | tf_op jit(solution)/shard_map/ppermute | solution.py:344
  70.7 0.6 copy-done.10
  71.3 2.0 %finish.1 = f32[2,16,4,256]{3,2,1,0:T(4,128)} custom-call(f32[128,512]{1,0:T(8,128)} %copy-done.5, f32[2,128,48]{2,1,0:T(8,128)} %copy-done.4, f32[48,256]{1,0:T(8,128)} %copy-done.9, f32[48,256]{1,0:T(8,128)} %copy-done.10), custom_call_target="tpu_custom_call" | custom-call | tf_op jit(solution)/shard_map/finish/pallas_call | solution.py:306
  (43 shorter events, 0.4 us)
Async XLA Ops:
  0.0 11.1 %collective-permute-start = (f32[2,16,4,256]{3,2,1,0:T(4,128)}, f32[2,16,4,256]{3,2,1,0:T(4,128)S(1)}, u32[]{:S(2)}, u32[]{:S(2)}) collective-permute-start(f32[2,16,4,256]{3,2,1,0:T(4,128)} %refs_0_.1), channel_id=1, source_target_pairs={{1,0},{0,1},{3,2},{2,3},{5,4},{4,5},{7,6},{6,7},{9,8},{8,9},{11,10... | collective-permute-start | bytes 393224 | tf_op jit(solution)/shard_map/ppermute | solution.py:349
  2.9 2.2 %copy-start = (bf16[32,2,2,4,4096]{4,3,2,1,0:T(4,128)(2,1)S(1)}, bf16[32,2,2,4,4096]{4,3,2,1,0:T(4,128)(2,1)}, u32[]{:S(2)}) copy-start(bf16[32,2,2,4,4096]{4,3,2,1,0:T(4,128)(2,1)} %patches_ref.1) | copy-start | bytes 12582916
  5.1 0.8 %copy-start.2 = (s32[4,4096]{1,0:T(4,128)S(1)}, s32[4,4096]{1,0:T(4,128)}, u32[]{:S(2)}) copy-start(s32[4,4096]{1,0:T(4,128)} %refs_7_.1) | copy-start | bytes 196612
  6.0 0.7 copy-start.8
  6.6 4.5 %copy-start.1 = (f32[2,2,4,4096]{3,2,1,0:T(4,128)S(1)}, f32[2,2,4,4096]{3,2,1,0:T(4,128)}, u32[]{:S(2)}) copy-start(f32[2,2,4,4096]{3,2,1,0:T(4,128)} %refs_8_.1) | copy-start | bytes 786436
  6.6 4.5 %copy-start.3 = (s32[4,4096]{1,0:T(4,128)S(1)}, s32[4,4096]{1,0:T(4,128)}, u32[]{:S(2)}) copy-start(s32[4,4096]{1,0:T(4,128)} %refs_7_.1) | copy-start | bytes 196612
  6.6 4.5 %copy-start.6 = (s32[2,4096]{1,0:T(2,128)S(1)}, s32[2,4096]{1,0:T(2,128)}, u32[]{:S(2)}) copy-start(s32[2,4096]{1,0:T(2,128)} %refs_4_.1) | copy-start | bytes 98308
  6.6 4.5 %copy-start.7 = (f32[2,16,4,256]{3,2,1,0:T(4,128)S(1)}, f32[2,16,4,256]{3,2,1,0:T(4,128)}, u32[]{:S(2)}) copy-start(f32[2,16,4,256]{3,2,1,0:T(4,128)} %refs_0_.1) | copy-start | bytes 393220
  11.1 40.0 %copy-start.4 = (f32[2,128,48]{2,1,0:T(8,128)}, f32[2,128,48]{2,1,0:T(8,128)S(1)}, u32[]{:S(2)}) copy-start(f32[2,128,48]{2,1,0:T(8,128)S(1)} %get-tuple-element.21.refs_1_.fit_ref) | copy-start | bytes 147460
  19.1 1.5 %collective-permute-start.1 = (f32[96,512]{1,0:T(8,128)S(1)}, f32[96,512]{1,0:T(8,128)S(1)}, u32[]{:S(2)}, u32[]{:S(2)}) collective-permute-start(f32[96,512]{1,0:T(8,128)S(1)} %get-tuple-element.23), channel_id=1, source_target_pairs={{0,2},{2,0},{4,6},{6,4},{8,10},{10,8},{12,14},{14,12},{1,3},{3,1},... | collective-permute-start | bytes 589832 | tf_op jit(solution)/shard_map/ppermute | solution.py:344
  20.6 4.9 %collective-permute-start.2 = (f32[96,256]{1,0:T(8,128)S(1)}, f32[96,256]{1,0:T(8,128)S(1)}, u32[]{:S(2)}, u32[]{:S(2)}) collective-permute-start(f32[96,256]{1,0:T(8,128)S(1)} %slice.113), channel_id=1, source_target_pairs={{1,0},{0,1},{3,2},{2,3},{5,4},{4,5},{7,6},{6,7},{9,8},{8,9},{11,10... | collective-permute-start | bytes 294920 | tf_op jit(solution)/shard_map/ppermute | solution.py:349
  25.5 7.4 %collective-permute-start.5 = (f32[96,256]{1,0:T(8,128)S(1)}, f32[96,256]{1,0:T(8,128)S(1)}, u32[]{:S(2)}, u32[]{:S(2)}) collective-permute-start(f32[96,256]{1,0:T(8,128)S(1)} %slice_add_fusion.1), channel_id=1, source_target_pairs={{0,12},{2,14},{4,8},{6,10},{8,4},{10,6},{12,0},{14,2},{1,13},{3,15... | collective-permute-start | bytes 294920 | tf_op jit(solution)/shard_map/ppermute | solution.py:355
  29.2 7.7 %collective-permute-start.4 = (f32[96,256]{1,0:T(8,128)S(1)}, f32[96,256]{1,0:T(8,128)S(1)}, u32[]{:S(2)}, u32[]{:S(2)}) collective-permute-start(f32[96,256]{1,0:T(8,128)S(1)} %slice_add_fusion.1), channel_id=1, source_target_pairs={{0,8},{2,10},{4,12},{6,14},{8,0},{10,2},{12,4},{14,6},{1,9},{3,11}... | collective-permute-start | bytes 294920 | tf_op jit(solution)/shard_map/ppermute | solution.py:355
  29.2 7.7 %collective-permute-start.3 = (f32[96,256]{1,0:T(8,128)S(1)}, f32[96,256]{1,0:T(8,128)S(1)}, u32[]{:S(2)}, u32[]{:S(2)}) collective-permute-start(f32[96,256]{1,0:T(8,128)S(1)} %slice_add_fusion.1), channel_id=1, source_target_pairs={{0,4},{2,6},{4,0},{6,2},{8,12},{10,14},{12,8},{14,10},{1,5},{3,7},... | collective-permute-start | bytes 294920 | tf_op jit(solution)/shard_map/ppermute | solution.py:355
  37.1 4.2 %collective-permute-start.6 = (f32[48,256]{1,0:T(8,128)S(1)}, f32[48,256]{1,0:T(8,128)S(1)}, u32[]{:S(2)}, u32[]{:S(2)}) collective-permute-start(f32[48,256]{1,0:T(8,128)S(1)} %constant_dynamic-update-slice_fusion), channel_id=1, source_target_pairs={{1,0},{0,1},{3,2},{2,3},{5,4},{4,5},{7,6},{6,7},{9,8},{8,9},{11,10... | collective-permute-start | bytes 147464 | tf_op jit(solution)/shard_map/ppermute | solution.py:349
  41.3 1.4 %collective-permute-start.7 = (f32[48,512]{1,0:T(8,128)S(1)}, f32[48,512]{1,0:T(8,128)S(1)}, u32[]{:S(2)}, u32[]{:S(2)}) collective-permute-start(f32[48,512]{1,0:T(8,128)S(1)} %pad_maximum_fusion.refs_2_), channel_id=1, source_target_pairs={{0,2},{2,0},{4,6},{6,4},{8,10},{10,8},{12,14},{14,12},{1,3},{3,1},... | collective-permute-start | bytes 294920 | tf_op jit(solution)/shard_map/ppermute | solution.py:344
  51.1 0.7 copy-start.5
  51.8 1.4 %collective-permute-start.8 = (f32[96,512]{1,0:T(8,128)S(1)}, f32[96,512]{1,0:T(8,128)S(1)}, u32[]{:S(2)}, u32[]{:S(2)}) collective-permute-start(f32[96,512]{1,0:T(8,128)S(1)} %get-tuple-element.26), channel_id=1, source_target_pairs={{0,2},{2,0},{4,6},{6,4},{8,10},{10,8},{12,14},{14,12},{1,3},{3,1},... | collective-permute-start | bytes 589832 | tf_op jit(solution)/shard_map/ppermute | solution.py:344
  53.3 4.9 %collective-permute-start.9 = (f32[96,256]{1,0:T(8,128)S(1)}, f32[96,256]{1,0:T(8,128)S(1)}, u32[]{:S(2)}, u32[]{:S(2)}) collective-permute-start(f32[96,256]{1,0:T(8,128)S(1)} %slice.127), channel_id=1, source_target_pairs={{1,0},{0,1},{3,2},{2,3},{5,4},{4,5},{7,6},{6,7},{9,8},{8,9},{11,10... | collective-permute-start | bytes 294920 | tf_op jit(solution)/shard_map/ppermute | solution.py:349
  58.2 7.6 %collective-permute-start.12 = (f32[96,256]{1,0:T(8,128)S(1)}, f32[96,256]{1,0:T(8,128)S(1)}, u32[]{:S(2)}, u32[]{:S(2)}) collective-permute-start(f32[96,256]{1,0:T(8,128)S(1)} %slice_add_fusion), channel_id=1, source_target_pairs={{0,12},{2,14},{4,8},{6,10},{8,4},{10,6},{12,0},{14,2},{1,13},{3,15... | collective-permute-start | bytes 294920 | tf_op jit(solution)/shard_map/ppermute | solution.py:355
  60.8 8.4 %collective-permute-start.11 = (f32[96,256]{1,0:T(8,128)S(1)}, f32[96,256]{1,0:T(8,128)S(1)}, u32[]{:S(2)}, u32[]{:S(2)}) collective-permute-start(f32[96,256]{1,0:T(8,128)S(1)} %slice_add_fusion), channel_id=1, source_target_pairs={{0,8},{2,10},{4,12},{6,14},{8,0},{10,2},{12,4},{14,6},{1,9},{3,11}... | collective-permute-start | bytes 294920 | tf_op jit(solution)/shard_map/ppermute | solution.py:355
  60.8 8.4 %collective-permute-start.10 = (f32[96,256]{1,0:T(8,128)S(1)}, f32[96,256]{1,0:T(8,128)S(1)}, u32[]{:S(2)}, u32[]{:S(2)}) collective-permute-start(f32[96,256]{1,0:T(8,128)S(1)} %slice_add_fusion), channel_id=1, source_target_pairs={{0,4},{2,6},{4,0},{6,2},{8,12},{10,14},{12,8},{14,10},{1,5},{3,7},... | collective-permute-start | bytes 294920 | tf_op jit(solution)/shard_map/ppermute | solution.py:355
  69.4 1.3 %copy-start.9 = (f32[48,256]{1,0:T(8,128)}, f32[48,256]{1,0:T(8,128)S(1)}, u32[]{:S(2)}) copy-start(f32[48,256]{1,0:T(8,128)S(1)} %constant_dynamic-update-slice_fusion.6.own_ref) | copy-start | bytes 147460
  69.4 1.3 %collective-permute-start.13 = (f32[48,256]{1,0:T(8,128)S(1)}, f32[48,256]{1,0:T(8,128)S(1)}, u32[]{:S(2)}, u32[]{:S(2)}) collective-permute-start(f32[48,256]{1,0:T(8,128)S(1)} %constant_dynamic-update-slice_fusion.6.own_ref), channel_id=1, source_target_pairs={{0,2},{2,0},{4,6},{6,4},{8,10},{10,8},{12,14},{14,12},{1,3},{3,1},... | collective-permute-start | bytes 147464 | tf_op jit(solution)/shard_map/ppermute | solution.py:344
  70.7 0.6 copy-start.10
where the time goes:
time: 73.5 us; the launch traced here: 73.3 us
  waiting for transfers between devices  31.4 us (43%)
  Pallas kernels  22.8 us (31%)
  starting transfers between devices  13.5 us (18%)
  local copies, waits for them, and re-layouts  5.07 us (7%)
    pallas_call x2, Pallas kernels, sweep(): pl.pallas_call(partial(sweep_kernel, first, blocks, owned), grid=(baselin...  16.3 us
    ppermute x6, waiting for transfers between devices, over_chips(): lax.ppermute(v, 'chan', [(j, j ^ 2 * k) for j in range(count)])  13.5 us
    ppermute x4, waiting for transfers between devices, from_later(): lax.ppermute(value, 'bl', [((j + k) % count, j) for j in range(count)])  12.7 us
    ppermute x6, starting transfers between devices, over_chips(): lax.ppermute(v, 'chan', [(j, j ^ 2 * k) for j in range(count)])  8.91 us
    ppermute x4, waiting for transfers between devices, other_core(): return lax.ppermute(value, 'chan', [(j, j ^ 1) for j in range(count)])  5.22 us
    unnamed x28, local copies, waits for them, and re-layouts  5.05 us
    pallas_call x1, Pallas kernels, prepare(): pl.pallas_call(partial(prep_kernel, total, channels), grid=(baselines //...  4.42 us
    ppermute x4, starting transfers between devices, from_later(): lax.ppermute(value, 'bl', [((j + k) % count, j) for j in range(count)])  4.22 us
  transfers between devices with their start and end apart: 14, of which 11 were waited for; matrix products, arithmetic and copies ran while one was open for 0% of the time, Pallas kernels for 6%

commit v1 on v0

v1 whole, which is shorter than its diff:
```python
from functools import partial

import jax
import jax.numpy as jnp
from jax import lax
from jax.experimental import pallas as pl
from jax.experimental.pallas import tpu as pltpu
from jax.sharding import PartitionSpec as P

DIRECTIONS = 16
SKY_PATCHES = 32
TIME_SLOTS = 2
ITERS = 2
LANES = 128
PREP_CHUNK = 1024
SWEEP_TILE = 256
HALF = DIRECTIONS // 2
HIGHEST = lax.Precision.HIGHEST
F32, BF16 = jnp.float32, jnp.bfloat16


def basis_at(channel, total):
    ratio = 1.0 + channel.astype(F32) / total
    inverse = 4.0 / ratio - 3.0
    return jnp.ones_like(inverse), inverse, 2.0 * inverse * inverse - 1.0


def iotas(shape):
    return lax.broadcasted_iota(jnp.int32, shape, 0), lax.broadcasted_iota(jnp.int32, shape, 1)


def pick(index, values):
    out = values[-1]
    for k in range(len(values) - 2, -1, -1):
        out = jnp.where(index == k, values[k], out)
    return out


def moment_matrix(terms, channels, total, chan):
    row, col = iotas((2 * terms * HALF, DIRECTIONS * channels))
    block = row // HALF
    half = (block >= terms).astype(jnp.int32)
    term = block - half * terms
    direction = jnp.bitwise_xor(half, lax.rem(chan, 2)) * HALF + row % HALF
    one, first, second = basis_at(chan * channels + col % channels, total)
    if terms == 5:
        values = (one, first, second, first * second, second * second)
    else:
        values = (one, first, second)
    return jnp.where(direction == col // channels, pick(term, values), 0.0)


def fit_matrix(half, channels, total, chan):
    per = DIRECTIONS * channels
    row, col = iotas((2 * per, 6 * HALF))
    place = row % per
    block = col // HALF
    direction = jnp.bitwise_xor(half, lax.rem(chan, 2)) * HALF + col % HALF
    basis = basis_at(chan * channels + place % channels, total)
    same = (direction == place // channels) & (row // per == block // 3)
    return jnp.where(same, pick(block % 3, basis), 0.0)


def prep_kernel(total, channels, chunk, cluster_hbm, patches_hbm, valid_hbm, model_ref, power_ref,
                normal_ref, right_ref, fit_ref, patches_ref, valid_ref, cluster_ref, sems, order_ref, start_ref):
    chan = lax.axis_index("chan")
    baselines = valid_ref.shape[1]
    cluster_copy = pltpu.make_async_copy(cluster_hbm, cluster_ref, sems.at[baselines // chunk])
    cluster_copy.start()
    valid_copy = pltpu.make_async_copy(valid_hbm, valid_ref, sems.at[baselines // chunk + 1])
    valid_copy.start()
    copies = []
    for part in range(baselines // chunk):
        here = pl.ds(part * chunk, chunk)
        copies.append(pltpu.make_async_copy(patches_hbm.at[..., here], patches_ref.at[..., here], sems.at[part]))
        copies[-1].start()
    normal_ref[...] = moment_matrix(5, channels, total, chan)
    right_ref[...] = moment_matrix(3, channels, total, chan)
    fit_ref[0] = fit_matrix(0, channels, total, chan)
    fit_ref[1] = fit_matrix(1, channels, total, chan)
    for d in range(DIRECTIONS + 1):
        start_ref[d] = 0
    cluster_copy.wait()

    @pl.loop(0, SKY_PATCHES)
    def _(q):
        d = cluster_ref[q]
        start_ref[d + 1] = start_ref[d + 1] + 1

    for d in range(DIRECTIONS):
        start_ref[d + 1] = start_ref[d + 1] + start_ref[d]
    for d in range(DIRECTIONS):
        start_ref[DIRECTIONS + 1 + d] = start_ref[d]

    @pl.loop(0, SKY_PATCHES)
    def _(q):
        d = cluster_ref[q]
        place = start_ref[DIRECTIONS + 1 + d]
        order_ref[place] = q
        start_ref[DIRECTIONS + 1 + d] = place + 1

    valid_copy.wait()
    fold = 8 // channels
    parts = [(x, t) for x in range(2) for t in range(TIME_SLOTS)]
    for part in range(baselines // chunk):
        copies[part].wait()
        here = slice(part * chunk, (part + 1) * chunk)
        validity = valid_ref[:, here].astype(F32)

        @pl.loop(0, DIRECTIONS // fold)
        def _(group):
            found = []
            for k in range(fold):
                d = group * fold + k

                def add(i, sums):
                    q = order_ref[i]
                    return tuple(
                        s + patches_ref[q, x, t, :, here].astype(F32) for s, (x, t) in zip(sums, parts)
                    )

                zero = jnp.zeros((channels, chunk), F32)
                found.append(lax.fori_loop(start_ref[d], start_ref[d + 1], add, (zero,) * len(parts)))
            rows = pl.ds(pl.multiple_of(group * 8, 8), 8)
            power = None
            for j, (x, t) in enumerate(parts):
                s = jnp.concatenate([f[j] for f in found], axis=0)
                model_ref[x, t, rows, here] = s
                power = s * s if power is None else power + s * s
            power_ref[rows, here] = power * jnp.concatenate([validity] * fold, axis=0)


def prepare(cluster, patches, valid, total):
    channels, baselines = valid.shape
    chunk = min(PREP_CHUNK, baselines)
    per = DIRECTIONS * channels
    vmem = pl.BlockSpec(memory_space=pltpu.VMEM)
    return pl.pallas_call(
        partial(prep_kernel, total, channels, chunk),
        in_specs=[
            pl.BlockSpec(memory_space=pltpu.HBM),
            pl.BlockSpec(memory_space=pltpu.HBM),
            pl.BlockSpec(memory_space=pltpu.HBM),
        ],
        out_specs=[vmem] * 5,
        out_shape=[
            jax.ShapeDtypeStruct((2, TIME_SLOTS, per, baselines), F32),
            jax.ShapeDtypeStruct((per, baselines), F32),
            jax.ShapeDtypeStruct((10 * HALF, per), F32),
            jax.ShapeDtypeStruct((6 * HALF, per), F32),
            jax.ShapeDtypeStruct((2, 2 * per, 6 * HALF), F32),
        ],
        scratch_shapes=[
            pltpu.VMEM(patches.shape, BF16),
            pltpu.VMEM(valid.shape, valid.dtype),
            pltpu.SMEM((SKY_PATCHES,), jnp.int32),
            pltpu.SemaphoreType.DMA((baselines // chunk + 2,)),
            pltpu.SMEM((SKY_PATCHES,), jnp.int32),
            pltpu.SMEM((2 * DIRECTIONS + 1,), jnp.int32),
        ],
        compiler_params=pltpu.CompilerParams(vmem_limit_bytes=32 << 20),
        name="prepare",
    )(*(pltpu.with_memory_space_constraint(v, pltpu.HBM) for v in (cluster, patches, valid)))


def fitted_values(fit_ref, coefs):
    out = jnp.dot(fit_ref[0], coefs[0], precision=HIGHEST, preferred_element_type=F32)
    return out + jnp.dot(fit_ref[1], coefs[1], precision=HIGHEST, preferred_element_type=F32)


def sweep_kernel(first, blocks, owned, tile, *refs):
    if first:
        gain_refs, refs = refs[:blocks], refs[blocks:]
        (stations_ref, model_ref, power_ref, valid_ref, visible_ref, normal_ref, right_ref,
         own_ref, other_ref, current_ref, picks_ref, *refs) = refs
    else:
        (before_ref, fit_ref, own_coef_ref, other_coef_ref, picks_ref), refs = refs[:5], refs[5:]
        (model_ref, power_ref, valid_ref, visible_ref, normal_ref, right_ref,
         own_ref, other_ref, current_ref, *refs) = refs
    rounded_ref, sums_ref, chosen_even, chosen_odd, terms_even, terms_odd = refs
    chosen_refs, terms_refs = (chosen_even, chosen_odd), (terms_even, terms_odd)
    channels, baselines = valid_ref.shape
    per = DIRECTIONS * channels
    stations = blocks * owned
    fold = 8 // channels
    if first:
        for k in range(blocks):
            for x in range(2):
                for d in range(0, DIRECTIONS, fold):
                    row = x * per + d * channels
                    pair = jnp.concatenate([gain_refs[k][x, d + j] for j in range(fold)], axis=0)
                    current_ref[row:row + 8, k * owned:(k + 1) * owned] = pair
    else:
        fitted = fitted_values(fit_ref, (own_coef_ref[...], other_coef_ref[...]))
        current_ref[...] = 0.5 * (before_ref[...] + fitted)
    rounded_ref[...] = current_ref[...].astype(BF16)

    def span(i, width):
        if isinstance(i, int):
            return slice(i * width, (i + 1) * width)
        return pl.ds(pl.multiple_of(i * width, width), width)

    def choose(i, slot):
        here = span(i, 2 * tile)
        if first:
            shift = lax.axis_index("bl") * owned
            place = stations_ref[:, span(i, tile)] - shift
            place = jnp.where(place < 0, place + stations, place)
            place = jnp.concatenate([place[0:1, :], place[1:2, :]], axis=1)
            ids = lax.broadcasted_iota(jnp.int32, (stations, 2 * tile), 0)
            picks_ref[:, here] = (ids == place).astype(BF16)
        chosen_refs[slot][...] = jnp.dot(rounded_ref[...], picks_ref[:, here], preferred_element_type=F32)

    def terms(i, slot):
        chosen_ref, terms_ref = chosen_refs[slot], terms_refs[slot]
        for part in range(tile // LANES):
            near, far = (slice(k * tile + part * LANES, k * tile + (part + 1) * LANES) for k in range(2))
            if isinstance(i, int):
                along = slice(i * tile + part * LANES, i * tile + (part + 1) * LANES)
            else:
                along = pl.ds(pl.multiple_of(i * tile + part * LANES, LANES), LANES)
            pred = [jnp.zeros((8, LANES), F32) for _ in range(2 * TIME_SLOTS)]
            for row in range(0, per, 8):
                re, im = slice(row, row + 8), slice(per + row, per + row + 8)
                pr, pi, qr, qi = chosen_ref[re, near], chosen_ref[im, near], chosen_ref[re, far], chosen_ref[im, far]
                gr = pr * qr + pi * qi
                gi = pi * qr - pr * qi
                for t in range(TIME_SLOTS):
                    mr, mi = model_ref[0, t, re, along], model_ref[1, t, re, along]
                    pred[2 * t] = pred[2 * t] + (gr * mr - gi * mi)
                    pred[2 * t + 1] = pred[2 * t + 1] + (gr * mi + gi * mr)
            validity = valid_ref[:, along].astype(F32)
            resid = []
            for t in range(TIME_SLOTS):
                for x in range(2):
                    p = pred[2 * t + x]
                    total = p[0:channels]
                    for k in range(1, fold):
                        total = total + p[k * channels:(k + 1) * channels]
                    r = (visible_ref[x, t, :, along] - total) * validity
                    resid.append(jnp.concatenate([r] * fold, axis=0))
            rows = [[None] * (per // 8) for _ in range(6)]
            for row in range(0, per, 8):
                re, im = slice(row, row + 8), slice(per + row, per + row + 8)
                pr, pi, qr, qi = chosen_ref[re, near], chosen_ref[im, near], chosen_ref[re, far], chosen_ref[im, far]
                ar = ai = None
                for t in range(TIME_SLOTS):
                    mr, mi = model_ref[0, t, re, along], model_ref[1, t, re, along]
                    rr, ri = resid[2 * t], resid[2 * t + 1]
                    br = mr * rr + mi * ri
                    bi = mr * ri - mi * rr
                    ar, ai = (br, bi) if ar is None else (ar + br, ai + bi)
                power = power_ref[re, along]
                values = (qr * ar - qi * ai, qr * ai + qi * ar, power * (qr * qr + qi * qi),
                          pr * ar + pi * ai, pi * ar - pr * ai, power * (pr * pr + pi * pi))
                for k in range(6):
                    rows[k][row // 8] = values[k]
                if row % 16 == 8:
                    for k in range(6):
                        two = jnp.concatenate(rows[k][row // 8 - 1:row // 8 + 1], axis=0).astype(BF16)
                        terms_ref[(k % 3) * per + row - 8:(k % 3) * per + row + 8, (near, far)[k // 3]] = two

    def add_up(i, slot):
        more = lax.dot_general(
            picks_ref[:, span(i, 2 * tile)], terms_refs[slot][...], (((1,), (1,)), ((), ())),
            preferred_element_type=F32,
        )
        if isinstance(i, int) and i == 0:
            sums_ref[...] = more
        else:
            sums_ref[...] += more

    count = baselines // tile
    choose(0, 0)
    choose(1, 1)
    terms(0, 0)
    add_up(0, 0)
    choose(2, 0)
    terms(1, 1)

    @pl.loop(0, (count - 4) // 2)
    def _(j):
        i = 2 * j + 3
        for k in range(2):
            add_up(i + k - 2, 1 - k)
            choose(i + k, 1 - k)
            terms(i + k - 1, k)

    for i in range(count - 1, count):
        add_up(i - 2, i % 2)
        choose(i, i % 2)
        terms(i - 1, 1 - i % 2)
    add_up(count - 2, count % 2)
    terms(count - 1, 1 - count % 2)
    add_up(count - 1, 1 - count % 2)

    sums = sums_ref[...].T
    weight = sums[2 * per:3 * per, :] + 1.0 / blocks
    product = partial(jnp.dot, precision=HIGHEST, preferred_element_type=F32)
    normal = product(normal_ref[...], weight)
    right = [
        product(right_ref[...], weight * current_ref[x * per:(x + 1) * per, :] + sums[x * per:(x + 1) * per, :])
        for x in range(2)
    ]
    for half, out in enumerate((own_ref, other_ref)):
        out[0:5 * HALF, :] = normal[half * 5 * HALF:(half + 1) * 5 * HALF, :]
        for x in range(2):
            out[(5 + 3 * x) * HALF:(8 + 3 * x) * HALF, :] = right[x][half * 3 * HALF:(half + 1) * 3 * HALF, :]


def sweep(first, inputs, model, power, valid, visible, normal, right, owned, blocks):
    channels, baselines = valid.shape
    per = DIRECTIONS * channels
    count = owned * blocks
    vmem = pl.BlockSpec(memory_space=pltpu.VMEM)
    outs = [
        jax.ShapeDtypeStruct((11 * HALF, count), F32),
        jax.ShapeDtypeStruct((11 * HALF, count), F32),
        jax.ShapeDtypeStruct((2 * per, count), F32),
    ]
    if first:
        outs.append(jax.ShapeDtypeStruct((count, 2 * baselines), BF16))
    return pl.pallas_call(
        partial(sweep_kernel, first, blocks, owned, SWEEP_TILE),
        in_specs=[vmem] * (len(inputs) + 6),
        out_specs=[vmem] * len(outs),
        out_shape=outs,
        scratch_shapes=[
            pltpu.VMEM((2 * per, count), BF16),
            pltpu.VMEM((count, 3 * per), F32),
            pltpu.VMEM((2 * per, 2 * SWEEP_TILE), F32),
            pltpu.VMEM((2 * per, 2 * SWEEP_TILE), F32),
            pltpu.VMEM((3 * per, 2 * SWEEP_TILE), BF16),
            pltpu.VMEM((3 * per, 2 * SWEEP_TILE), BF16),
        ],
        compiler_params=pltpu.CompilerParams(vmem_limit_bytes=24 << 20),
        name="sweep",
    )(*inputs, model, power, valid, visible, normal, right)


def final_kernel(channels, before_ref, fit_ref, own_ref, other_ref, out_ref):
    per = DIRECTIONS * channels
    result = 0.5 * (before_ref[:, 0:out_ref.shape[3]] + fitted_values(fit_ref, (own_ref[...], other_ref[...])))
    for x in range(2):
        for d in range(DIRECTIONS):
            row = x * per + d * channels
            out_ref[x, d] = result[row:row + channels, :]


def finish(before, fit, own, other, channels):
    owned = own.shape[1]
    return pl.pallas_call(
        partial(final_kernel, channels),
        in_specs=[pl.BlockSpec(memory_space=pltpu.VMEM)] * 4,
        out_specs=pl.BlockSpec(memory_space=pltpu.VMEM),
        out_shape=jax.ShapeDtypeStruct((2, DIRECTIONS, channels, owned), F32),
        compiler_params=pltpu.CompilerParams(vmem_limit_bytes=8 << 20),
        name="finish",
    )(before, fit, own, other)


def solve(moments):
    m = [moments[k * HALF:(k + 1) * HALF] for k in range(11)]
    m.insert(3, 0.5 * (m[0] + m[2]))
    low_aa = jnp.sqrt(m[0])
    low_ba = m[1] / low_aa
    low_ca = m[2] / low_aa
    low_bb = jnp.sqrt(m[3] - low_ba * low_ba)
    low_cb = (m[4] - low_ca * low_ba) / low_bb
    low_cc = jnp.sqrt(m[5] - low_ca * low_ca - low_cb * low_cb)
    out = []
    for x in range(2):
        r = m[6 + 3 * x:9 + 3 * x]
        first_y = r[0] / low_aa
        second_y = (r[1] - low_ba * first_y) / low_bb
        third_y = (r[2] - low_ca * first_y - low_cb * second_y) / low_cc
        third_x = third_y / low_cc
        second_x = (second_y - low_cb * third_x) / low_bb
        first_x = (first_y - low_ba * second_x - low_ca * third_x) / low_aa
        out += [first_x, second_x, third_x]
    return jnp.concatenate(out, axis=0)


def other_core(value):
    count = lax.axis_size("chan")
    return lax.ppermute(value, "chan", [(j, j ^ 1) for j in range(count)])


def from_later(value, k):
    count = lax.axis_size("bl")
    return lax.ppermute(value, "bl", [((j + k) % count, j) for j in range(count)])


def over_chips(value):
    count = lax.axis_size("chan")
    chips = count // 2
    swap = lambda v, k: lax.ppermute(v, "chan", [(j, j ^ (2 * k)) for j in range(count)])
    if chips <= 4:
        parts = [swap(value, k) for k in range(1, chips)]
        for part in parts:
            value = value + part
        return value
    k = 1
    while k < chips:
        value = value + swap(value, k)
        k *= 2
    return value


def body(patches, visibilities, valid, baseline_stations, cluster, gains):
    channels = visibilities.shape[2]
    owned = gains.shape[3]
    blocks = lax.axis_size("bl")
    total = channels * lax.axis_size("chan")
    all_gains = [gains] + [from_later(gains, k) for k in range(1, blocks)]
    model, power, normal, right, fit = prepare(cluster[:, 0], patches, valid, total)
    common = (model, power, valid, visibilities, normal, right, owned, blocks)
    inputs = all_gains + [baseline_stations]
    picks = None
    for number in range(ITERS):
        own, other, current, *made = sweep(number == 0, inputs, *common)
        picks = made[0] if made else picks
        mine = own + other_core(other)
        part = lambda k: mine[:, k * owned:(k + 1) * owned]
        kept = part(0)
        for k in range(1, blocks):
            kept = kept + from_later(part(blocks - k), k)
        coefs = solve(over_chips(kept))
        if number < ITERS - 1:
            coefs = jnp.concatenate([coefs] + [from_later(coefs, k) for k in range(1, blocks)], axis=1)
        inputs = [current, fit, coefs, other_core(coefs), picks]
    return finish(*inputs[:4], channels)


def solution(mesh):
    in_specs = (
        P(None, None, None, ("grp", "chan"), "bl"),
        P(None, None, ("grp", "chan"), "bl"),
        P(("grp", "chan"), "bl"),
        P(None, "bl"),
        P(),
        P(None, None, ("grp", "chan"), "bl"),
    )
    out_specs = P(None, None, ("grp", "chan"), "bl")
    return jax.shard_map(body, mesh=mesh, in_specs=in_specs, out_specs=out_specs, check_vma=False)
```

time: 73.5 us -> 65.2 us (0.89)
  local copies, waits for them, and re-layouts: 5.07 us -> 0.05 us
  waiting for transfers between devices: 31.4 us -> 27 us
  starting transfers between devices: 13.5 us -> 16.5 us
  Pallas kernels: 22.8 us -> 21 us
    unnamed x28 -> x12, local copies, waits for them, and re-layouts: 5.05 us -> 0.03 us
    ppermute x4, waiting for transfers between devices: 12.7 us -> 9.47 us  [from_later(): lax.ppermute(value, 'bl', [((j + k) % count, j) for j in range(count)])]
    ppermute x4, starting transfers between devices: 4.22 us -> 7.17 us  [from_later(): lax.ppermute(value, 'bl', [((j + k) % count, j) for j in range(count)])]
    pallas_call x4, Pallas kernels: 22.8 us -> 21 us  [the longest x2 15.9 us: sweep(): pl.pallas_call(partial(sweep_kernel, first, blocks, owned, SWEEP_TILE), i...]
    ppermute x6, waiting for transfers between devices: 13.5 us -> 12.3 us  [over_chips(): lax.ppermute(v, 'chan', [(j, j ^ 2 * k) for j in range(count)])]
where the time goes in v1:
time: 65.2 us; the launch traced here: 65.1 us
  waiting for transfers between devices  27 us (41%)
  Pallas kernels  21 us (32%)
  starting transfers between devices  16.5 us (25%)
    pallas_call x2, Pallas kernels, sweep(): pl.pallas_call(partial(sweep_kernel, first, blocks, owned, SWEEP_TILE), i...  15.9 us
    ppermute x6, waiting for transfers between devices, over_chips(): lax.ppermute(v, 'chan', [(j, j ^ 2 * k) for j in range(count)])  12.3 us
    ppermute x4, waiting for transfers between devices, from_later(): lax.ppermute(value, 'bl', [((j + k) % count, j) for j in range(count)])  9.47 us
    ppermute x6, starting transfers between devices, over_chips(): lax.ppermute(v, 'chan', [(j, j ^ 2 * k) for j in range(count)])  8.91 us
    ppermute x4, starting transfers between devices, from_later(): lax.ppermute(value, 'bl', [((j + k) % count, j) for j in range(count)])  7.17 us
    ppermute x4, waiting for transfers between devices, other_core(): return lax.ppermute(value, 'chan', [(j, j ^ 1) for j in range(count)])  5.17 us
    pallas_call x1, Pallas kernels, prepare(): pl.pallas_call(partial(prep_kernel, total, channels, chunk), in_specs=[pl...  4.09 us
  transfers between devices with their start and end apart: 14, of which 11 were waited for; matrix products, arithmetic and copies ran while one was open for 0% of the time, Pallas kernels for 6%

profile of v1, /device:TPU:0, one launch (start us, length us, event | category | flops | bytes accessed | tf_op | source)
XLA Modules:
  0.0 65.1 jit_solution(6913566307520155362)
XLA Ops:
  0.0 3.0 %collective-permute-start = (f32[2,16,4,256]{3,2,1,0:T(4,128)}, f32[2,16,4,256]{3,2,1,0:T(4,128)S(1)}, u32[]{:S(2)}, u32[]{:S(2)}) collective-permute-start(f32[2,16,4,256]{3,2,1,0:T(4,128)} %refs_0_.1), channel_id=1, source_target_pairs={{1,0},{0,1},{3,2},{2,3},{5,4},{4,5},{7,6},{6,7},{9,8},{8,9},{11,10... | collective-permute-start | bytes 393224 | tf_op jit(solution)/shard_map/ppermute | solution.py:391
  3.0 4.1 %prepare.1 = (f32[2,2,64,4096]{3,2,1,0:T(8,128)S(1)}, f32[64,4096]{1,0:T(8,128)S(1)}, f32[80,64]{1,0:T(8,128)S(1)}, f32[48,64]{1,0:T(8,128)S(1)}, f32[2,128,48]{2,1,0:T(8,128)S(1)}) custom-call(s32[32]{0:T(128)} %bitcast.1, bf16[32,2,2,4,4096]{4,3,2,1,0:T(4,128)(2,1)} %patches_hbm.1, s32[4,4096]{1,0:T(4,128)} %refs_7_.1), custom_call_target="tpu_custom_call" | custom-call | tf_op jit(solution)/shard_map/prepare/pallas_call | solution.py:138
  7.2 8.4 %sweep.2 = (f32[88,512]{1,0:T(8,128)S(1)}, f32[88,512]{1,0:T(8,128)S(1)}, f32[128,512]{1,0:T(8,128)S(1)}, bf16[512,8192]{1,0:T(8,128)(2,1)S(1)}) custom-call(f32[2,16,4,256]{3,2,1,0:T(4,128)S(1)} %copy-done.2, f32[2,16,4,256]{3,2,1,0:T(4,128)S(1)} %collective-permute-done.refs_1_, s32[2,4096]{1,0:T(2,128)S(1)} %copy-done.3, ...), custom_call_target="tpu_custom_call" | custom-call | tf_op jit(solution)/shard_map/sweep/pallas_call | solution.py:323
  15.5 0.1 collective-permute-start.1
  15.6 1.4 %collective-permute-done.1 = f32[88,512]{1,0:T(8,128)S(1)} collective-permute-done((f32[88,512]{1,0:T(8,128)S(1)}, f32[88,512]{1,0:T(8,128)S(1)}, u32[]{:S(2)}, u32[]{:S(2)}) %collective-permute-start.1) | collective-permute-done | bytes 180256 | tf_op jit(solution)/shard_map/ppermute | solution.py:386
  17.1 1.4 %collective-permute-start.2 = (f32[88,256]{1,0:T(8,128)S(1)}, f32[88,256]{1,0:T(8,128)S(1)}, u32[]{:S(2)}, u32[]{:S(2)}) collective-permute-start(f32[88,256]{1,0:T(8,128)S(1)} %slice.105), channel_id=1, source_target_pairs={{1,0},{0,1},{3,2},{2,3},{5,4},{4,5},{7,6},{6,7},{9,8},{8,9},{11,10... | collective-permute-start | bytes 270344 | tf_op jit(solution)/shard_map/ppermute | solution.py:391
  18.5 3.3 %collective-permute-done.2 = f32[88,256]{1,0:T(8,128)S(1)} collective-permute-done((f32[88,256]{1,0:T(8,128)S(1)}, f32[88,256]{1,0:T(8,128)S(1)}, u32[]{:S(2)}, u32[]{:S(2)}) %collective-permute-start.2) | collective-permute-done | bytes 90144 | tf_op jit(solution)/shard_map/ppermute | solution.py:391
  21.8 3.7 %collective-permute-start.5 = (f32[88,256]{1,0:T(8,128)S(1)}, f32[88,256]{1,0:T(8,128)S(1)}, u32[]{:S(2)}, u32[]{:S(2)}) collective-permute-start(f32[88,256]{1,0:T(8,128)S(1)} %slice_add_fusion.1), channel_id=1, source_target_pairs={{0,12},{2,14},{4,8},{6,10},{8,4},{10,6},{12,0},{14,2},{1,13},{3,15... | collective-permute-start | bytes 270344 | tf_op jit(solution)/shard_map/ppermute | solution.py:397
  25.5 0.0 collective-permute-start.4
  25.5 0.8 %collective-permute-start.3 = (f32[88,256]{1,0:T(8,128)S(1)}, f32[88,256]{1,0:T(8,128)S(1)}, u32[]{:S(2)}, u32[]{:S(2)}) collective-permute-start(f32[88,256]{1,0:T(8,128)S(1)} %slice_add_fusion.1), channel_id=1, source_target_pairs={{0,4},{2,6},{4,0},{6,2},{8,12},{10,14},{12,8},{14,10},{1,5},{3,7},... | collective-permute-start | bytes 270344 | tf_op jit(solution)/shard_map/ppermute | solution.py:397
  26.3 2.8 %collective-permute-done.5 = f32[88,256]{1,0:T(8,128)S(1)} collective-permute-done((f32[88,256]{1,0:T(8,128)S(1)}, f32[88,256]{1,0:T(8,128)S(1)}, u32[]{:S(2)}, u32[]{:S(2)}) %collective-permute-start.5) | collective-permute-done | bytes 90144 | tf_op jit(solution)/shard_map/ppermute | solution.py:397
  29.0 3.5 %collective-permute-done.4 = f32[88,256]{1,0:T(8,128)S(1)} collective-permute-done((f32[88,256]{1,0:T(8,128)S(1)}, f32[88,256]{1,0:T(8,128)S(1)}, u32[]{:S(2)}, u32[]{:S(2)}) %collective-permute-start.4) | collective-permute-done | bytes 90144 | tf_op jit(solution)/shard_map/ppermute | solution.py:397
  32.5 0.0 collective-permute-done.3
  32.6 0.1 constant_dynamic-update-slice_fusion.5
  32.7 1.4 %collective-permute-start.6 = (f32[48,256]{1,0:T(8,128)S(1)}, f32[48,256]{1,0:T(8,128)S(1)}, u32[]{:S(2)}, u32[]{:S(2)}) collective-permute-start(f32[48,256]{1,0:T(8,128)S(1)} %constant_dynamic-update-slice_fusion), channel_id=1, source_target_pairs={{1,0},{0,1},{3,2},{2,3},{5,4},{4,5},{7,6},{6,7},{9,8},{8,9},{11,10... | collective-permute-start | bytes 147464 | tf_op jit(solution)/shard_map/ppermute | solution.py:391
  34.1 2.8 %collective-permute-done.6 = f32[48,256]{1,0:T(8,128)S(1)} collective-permute-done((f32[48,256]{1,0:T(8,128)S(1)}, f32[48,256]{1,0:T(8,128)S(1)}, u32[]{:S(2)}, u32[]{:S(2)}) %collective-permute-start.6) | collective-permute-done | bytes 49184 | tf_op jit(solution)/shard_map/ppermute | solution.py:391
  36.9 0.1 collective-permute-start.7
  37.0 1.3 %collective-permute-done.7.refs_3_ = f32[48,512]{1,0:T(8,128)S(1)} collective-permute-done((f32[48,512]{1,0:T(8,128)S(1)}, f32[48,512]{1,0:T(8,128)S(1)}, u32[]{:S(2)}, u32[]{:S(2)}) %collective-permute-start.7) | collective-permute-done | bytes 98336 | tf_op jit(solution)/shard_map/ppermute | solution.py:386
  38.2 7.5 %sweep.3 = (f32[88,512]{1,0:T(8,128)S(1)}, f32[88,512]{1,0:T(8,128)S(1)}, f32[128,512]{1,0:T(8,128)S(1)}) custom-call(f32[128,512]{1,0:T(8,128)S(1)} %get-tuple-element.21.refs_0_, f32[2,128,48]{2,1,0:T(8,128)S(1)} %get-tuple-element.22.refs_1_.fit_ref, f32[48,512]{1,0:T(8,128)S(1)} %pad_maximum_fusion.refs_2_, ...), custom_call_target="tpu_custom_call" | custom-call | tf_op jit(solution)/shard_map/sweep/pallas_call | solution.py:323
  45.8 0.2 collective-permute-start.8
  46.0 1.3 %collective-permute-done.8 = f32[88,512]{1,0:T(8,128)S(1)} collective-permute-done((f32[88,512]{1,0:T(8,128)S(1)}, f32[88,512]{1,0:T(8,128)S(1)}, u32[]{:S(2)}, u32[]{:S(2)}) %collective-permute-start.8) | collective-permute-done | bytes 180256 | tf_op jit(solution)/shard_map/ppermute | solution.py:386
  47.3 1.4 %collective-permute-start.9 = (f32[88,256]{1,0:T(8,128)S(1)}, f32[88,256]{1,0:T(8,128)S(1)}, u32[]{:S(2)}, u32[]{:S(2)}) collective-permute-start(f32[88,256]{1,0:T(8,128)S(1)} %slice.118), channel_id=1, source_target_pairs={{1,0},{0,1},{3,2},{2,3},{5,4},{4,5},{7,6},{6,7},{9,8},{8,9},{11,10... | collective-permute-start | bytes 270344 | tf_op jit(solution)/shard_map/ppermute | solution.py:391
  48.7 3.4 %collective-permute-done.9 = f32[88,256]{1,0:T(8,128)S(1)} collective-permute-done((f32[88,256]{1,0:T(8,128)S(1)}, f32[88,256]{1,0:T(8,128)S(1)}, u32[]{:S(2)}, u32[]{:S(2)}) %collective-permute-start.9) | collective-permute-done | bytes 90144 | tf_op jit(solution)/shard_map/ppermute | solution.py:391
  52.0 2.7 %collective-permute-start.12 = (f32[88,256]{1,0:T(8,128)S(1)}, f32[88,256]{1,0:T(8,128)S(1)}, u32[]{:S(2)}, u32[]{:S(2)}) collective-permute-start(f32[88,256]{1,0:T(8,128)S(1)} %slice_add_fusion), channel_id=1, source_target_pairs={{0,12},{2,14},{4,8},{6,10},{8,4},{10,6},{12,0},{14,2},{1,13},{3,15... | collective-permute-start | bytes 270344 | tf_op jit(solution)/shard_map/ppermute | solution.py:397
  54.7 0.0 collective-permute-start.11
  54.7 1.8 %collective-permute-start.10 = (f32[88,256]{1,0:T(8,128)S(1)}, f32[88,256]{1,0:T(8,128)S(1)}, u32[]{:S(2)}, u32[]{:S(2)}) collective-permute-start(f32[88,256]{1,0:T(8,128)S(1)} %slice_add_fusion), channel_id=1, source_target_pairs={{0,4},{2,6},{4,0},{6,2},{8,12},{10,14},{12,8},{14,10},{1,5},{3,7},... | collective-permute-start | bytes 270344 | tf_op jit(solution)/shard_map/ppermute | solution.py:397
  56.5 2.6 %collective-permute-done.12 = f32[88,256]{1,0:T(8,128)S(1)} collective-permute-done((f32[88,256]{1,0:T(8,128)S(1)}, f32[88,256]{1,0:T(8,128)S(1)}, u32[]{:S(2)}, u32[]{:S(2)}) %collective-permute-start.12) | collective-permute-done | bytes 90144 | tf_op jit(solution)/shard_map/ppermute | solution.py:397
  59.1 3.5 %collective-permute-done.11 = f32[88,256]{1,0:T(8,128)S(1)} collective-permute-done((f32[88,256]{1,0:T(8,128)S(1)}, f32[88,256]{1,0:T(8,128)S(1)}, u32[]{:S(2)}, u32[]{:S(2)}) %collective-permute-start.11) | collective-permute-done | bytes 90144 | tf_op jit(solution)/shard_map/ppermute | solution.py:397
  62.6 0.1 constant_dynamic-update-slice_fusion.11
  62.8 0.1 collective-permute-start.13
  62.8 1.2 %collective-permute-done.13.other_ref = f32[48,256]{1,0:T(8,128)S(1)} collective-permute-done((f32[48,256]{1,0:T(8,128)S(1)}, f32[48,256]{1,0:T(8,128)S(1)}, u32[]{:S(2)}, u32[]{:S(2)}) %collective-permute-start.13) | collective-permute-done | bytes 49184 | tf_op jit(solution)/shard_map/ppermute | solution.py:386
  64.1 1.0 %finish.1 = f32[2,16,4,256]{3,2,1,0:T(4,128)} custom-call(f32[128,512]{1,0:T(8,128)S(1)} %get-tuple-element.26.before_ref, f32[2,128,48]{2,1,0:T(8,128)S(1)} %get-tuple-element.22.refs_1_.fit_ref, f32[48,256]{1,0:T(8,128)S(1)} %constant_dynamic-update-slice_fusion.6.own_ref, f32[48,256]{1,0:T(8,128)S(1)} %collective-permute-done.13.other_ref), custom_call_target="tpu_custom_call" | custom-call | tf_op jit(solution)/shard_map/finish/pallas_call | solution.py:352
  (29 shorter events, 0.3 us)
Async XLA Ops:
  0.0 7.1 %copy-start.2 = (f32[2,16,4,256]{3,2,1,0:T(4,128)S(1)}, f32[2,16,4,256]{3,2,1,0:T(4,128)}, u32[]{:S(2)}) copy-start(f32[2,16,4,256]{3,2,1,0:T(4,128)} %refs_0_.1) | copy-start | bytes 393220
  0.0 7.1 %copy-start.1 = (s32[4,4096]{1,0:T(4,128)S(1)}, s32[4,4096]{1,0:T(4,128)}, u32[]{:S(2)}) copy-start(s32[4,4096]{1,0:T(4,128)} %refs_7_.1) | copy-start | bytes 196612
  0.0 7.2 %copy-start = (f32[2,2,4,4096]{3,2,1,0:T(4,128)S(1)}, f32[2,2,4,4096]{3,2,1,0:T(4,128)}, u32[]{:S(2)}) copy-start(f32[2,2,4,4096]{3,2,1,0:T(4,128)} %refs_8_.1) | copy-start | bytes 786436
  0.0 7.2 %copy-start.3 = (s32[2,4096]{1,0:T(2,128)S(1)}, s32[2,4096]{1,0:T(2,128)}, u32[]{:S(2)}) copy-start(s32[2,4096]{1,0:T(2,128)} %refs_2_.1) | copy-start | bytes 98308
  0.0 7.1 %collective-permute-start = (f32[2,16,4,256]{3,2,1,0:T(4,128)}, f32[2,16,4,256]{3,2,1,0:T(4,128)S(1)}, u32[]{:S(2)}, u32[]{:S(2)}) collective-permute-start(f32[2,16,4,256]{3,2,1,0:T(4,128)} %refs_0_.1), channel_id=1, source_target_pairs={{1,0},{0,1},{3,2},{2,3},{5,4},{4,5},{7,6},{6,7},{9,8},{8,9},{11,10... | collective-permute-start | bytes 393224 | tf_op jit(solution)/shard_map/ppermute | solution.py:391
  15.5 1.5 %collective-permute-start.1 = (f32[88,512]{1,0:T(8,128)S(1)}, f32[88,512]{1,0:T(8,128)S(1)}, u32[]{:S(2)}, u32[]{:S(2)}) collective-permute-start(f32[88,512]{1,0:T(8,128)S(1)} %get-tuple-element.24), channel_id=1, source_target_pairs={{0,2},{2,0},{4,6},{6,4},{8,10},{10,8},{12,14},{14,12},{1,3},{3,1},... | collective-permute-start | bytes 540680 | tf_op jit(solution)/shard_map/ppermute | solution.py:386
  17.1 4.7 %collective-permute-start.2 = (f32[88,256]{1,0:T(8,128)S(1)}, f32[88,256]{1,0:T(8,128)S(1)}, u32[]{:S(2)}, u32[]{:S(2)}) collective-permute-start(f32[88,256]{1,0:T(8,128)S(1)} %slice.105), channel_id=1, source_target_pairs={{1,0},{0,1},{3,2},{2,3},{5,4},{4,5},{7,6},{6,7},{9,8},{8,9},{11,10... | collective-permute-start | bytes 270344 | tf_op jit(solution)/shard_map/ppermute | solution.py:391
  21.8 7.2 %collective-permute-start.5 = (f32[88,256]{1,0:T(8,128)S(1)}, f32[88,256]{1,0:T(8,128)S(1)}, u32[]{:S(2)}, u32[]{:S(2)}) collective-permute-start(f32[88,256]{1,0:T(8,128)S(1)} %slice_add_fusion.1), channel_id=1, source_target_pairs={{0,12},{2,14},{4,8},{6,10},{8,4},{10,6},{12,0},{14,2},{1,13},{3,15... | collective-permute-start | bytes 270344 | tf_op jit(solution)/shard_map/ppermute | solution.py:397
  25.5 7.0 %collective-permute-start.4 = (f32[88,256]{1,0:T(8,128)S(1)}, f32[88,256]{1,0:T(8,128)S(1)}, u32[]{:S(2)}, u32[]{:S(2)}) collective-permute-start(f32[88,256]{1,0:T(8,128)S(1)} %slice_add_fusion.1), channel_id=1, source_target_pairs={{0,8},{2,10},{4,12},{6,14},{8,0},{10,2},{12,4},{14,6},{1,9},{3,11}... | collective-permute-start | bytes 270344 | tf_op jit(solution)/shard_map/ppermute | solution.py:397
  25.5 7.0 %collective-permute-start.3 = (f32[88,256]{1,0:T(8,128)S(1)}, f32[88,256]{1,0:T(8,128)S(1)}, u32[]{:S(2)}, u32[]{:S(2)}) collective-permute-start(f32[88,256]{1,0:T(8,128)S(1)} %slice_add_fusion.1), channel_id=1, source_target_pairs={{0,4},{2,6},{4,0},{6,2},{8,12},{10,14},{12,8},{14,10},{1,5},{3,7},... | collective-permute-start | bytes 270344 | tf_op jit(solution)/shard_map/ppermute | solution.py:397
  32.7 4.2 %collective-permute-start.6 = (f32[48,256]{1,0:T(8,128)S(1)}, f32[48,256]{1,0:T(8,128)S(1)}, u32[]{:S(2)}, u32[]{:S(2)}) collective-permute-start(f32[48,256]{1,0:T(8,128)S(1)} %constant_dynamic-update-slice_fusion), channel_id=1, source_target_pairs={{1,0},{0,1},{3,2},{2,3},{5,4},{4,5},{7,6},{6,7},{9,8},{8,9},{11,10... | collective-permute-start | bytes 147464 | tf_op jit(solution)/shard_map/ppermute | solution.py:391
  36.9 1.4 %collective-permute-start.7 = (f32[48,512]{1,0:T(8,128)S(1)}, f32[48,512]{1,0:T(8,128)S(1)}, u32[]{:S(2)}, u32[]{:S(2)}) collective-permute-start(f32[48,512]{1,0:T(8,128)S(1)} %pad_maximum_fusion.refs_2_), channel_id=1, source_target_pairs={{0,2},{2,0},{4,6},{6,4},{8,10},{10,8},{12,14},{14,12},{1,3},{3,1},... | collective-permute-start | bytes 294920 | tf_op jit(solution)/shard_map/ppermute | solution.py:386
  45.8 1.5 %collective-permute-start.8 = (f32[88,512]{1,0:T(8,128)S(1)}, f32[88,512]{1,0:T(8,128)S(1)}, u32[]{:S(2)}, u32[]{:S(2)}) collective-permute-start(f32[88,512]{1,0:T(8,128)S(1)} %get-tuple-element.28), channel_id=1, source_target_pairs={{0,2},{2,0},{4,6},{6,4},{8,10},{10,8},{12,14},{14,12},{1,3},{3,1},... | collective-permute-start | bytes 540680 | tf_op jit(solution)/shard_map/ppermute | solution.py:386
  47.3 4.7 %collective-permute-start.9 = (f32[88,256]{1,0:T(8,128)S(1)}, f32[88,256]{1,0:T(8,128)S(1)}, u32[]{:S(2)}, u32[]{:S(2)}) collective-permute-start(f32[88,256]{1,0:T(8,128)S(1)} %slice.118), channel_id=1, source_target_pairs={{1,0},{0,1},{3,2},{2,3},{5,4},{4,5},{7,6},{6,7},{9,8},{8,9},{11,10... | collective-permute-start | bytes 270344 | tf_op jit(solution)/shard_map/ppermute | solution.py:391
  52.0 7.1 %collective-permute-start.12 = (f32[88,256]{1,0:T(8,128)S(1)}, f32[88,256]{1,0:T(8,128)S(1)}, u32[]{:S(2)}, u32[]{:S(2)}) collective-permute-start(f32[88,256]{1,0:T(8,128)S(1)} %slice_add_fusion), channel_id=1, source_target_pairs={{0,12},{2,14},{4,8},{6,10},{8,4},{10,6},{12,0},{14,2},{1,13},{3,15... | collective-permute-start | bytes 270344 | tf_op jit(solution)/shard_map/ppermute | solution.py:397
  54.7 7.9 %collective-permute-start.11 = (f32[88,256]{1,0:T(8,128)S(1)}, f32[88,256]{1,0:T(8,128)S(1)}, u32[]{:S(2)}, u32[]{:S(2)}) collective-permute-start(f32[88,256]{1,0:T(8,128)S(1)} %slice_add_fusion), channel_id=1, source_target_pairs={{0,8},{2,10},{4,12},{6,14},{8,0},{10,2},{12,4},{14,6},{1,9},{3,11}... | collective-permute-start | bytes 270344 | tf_op jit(solution)/shard_map/ppermute | solution.py:397
  54.7 7.9 %collective-permute-start.10 = (f32[88,256]{1,0:T(8,128)S(1)}, f32[88,256]{1,0:T(8,128)S(1)}, u32[]{:S(2)}, u32[]{:S(2)}) collective-permute-start(f32[88,256]{1,0:T(8,128)S(1)} %slice_add_fusion), channel_id=1, source_target_pairs={{0,4},{2,6},{4,0},{6,2},{8,12},{10,14},{12,8},{14,10},{1,5},{3,7},... | collective-permute-start | bytes 270344 | tf_op jit(solution)/shard_map/ppermute | solution.py:397
  62.8 1.3 %collective-permute-start.13 = (f32[48,256]{1,0:T(8,128)S(1)}, f32[48,256]{1,0:T(8,128)S(1)}, u32[]{:S(2)}, u32[]{:S(2)}) collective-permute-start(f32[48,256]{1,0:T(8,128)S(1)} %constant_dynamic-update-slice_fusion.6.own_ref), channel_id=1, source_target_pairs={{0,2},{2,0},{4,6},{6,4},{8,10},{10,8},{12,14},{14,12},{1,3},{3,1},... | collective-permute-start | bytes 147464 | tf_op jit(solution)/shard_map/ppermute | solution.py:386

commit v2 on v1

--- a/solution.py
+++ b/solution.py
@@ -12,8 +12,9 @@
 TIME_SLOTS = 2
 ITERS = 2
 LANES = 128
+EXACT = 256
 PREP_CHUNK = 1024
-SWEEP_TILE = 256
+SWEEP_TILE = 1024
 HALF = DIRECTIONS // 2
 HIGHEST = lax.Precision.HIGHEST
 F32, BF16 = jnp.float32, jnp.bfloat16
@@ -50,11 +51,13 @@
     return jnp.where(direction == col // channels, pick(term, values), 0.0)
 
 
-def fit_matrix(half, channels, total, chan):
+def fit_matrix(channels, total, chan):
     per = DIRECTIONS * channels
-    row, col = iotas((2 * per, 6 * HALF))
+    row, col = iotas((2 * per, 12 * HALF))
     place = row % per
     block = col // HALF
+    half = (block >= 6).astype(jnp.int32)
+    block = block - 6 * half
     direction = jnp.bitwise_xor(half, lax.rem(chan, 2)) * HALF + col % HALF
     basis = basis_at(chan * channels + place % channels, total)
     same = (direction == place // channels) & (row // per == block // 3)
@@ -70,14 +73,14 @@
     valid_copy = pltpu.make_async_copy(valid_hbm, valid_ref, sems.at[baselines // chunk + 1])
     valid_copy.start()
     copies = []
+    rows = channels * chunk // LANES
     for part in range(baselines // chunk):
-        here = pl.ds(part * chunk, chunk)
-        copies.append(pltpu.make_async_copy(patches_hbm.at[..., here], patches_ref.at[..., here], sems.at[part]))
+        here = pl.ds(part * rows, rows)
+        copies.append(pltpu.make_async_copy(patches_hbm.at[:, :, :, here], patches_ref.at[:, :, :, here], sems.at[part]))
         copies[-1].start()
     normal_ref[...] = moment_matrix(5, channels, total, chan)
     right_ref[...] = moment_matrix(3, channels, total, chan)
-    fit_ref[0] = fit_matrix(0, channels, total, chan)
-    fit_ref[1] = fit_matrix(1, channels, total, chan)
+    fit_ref[...] = fit_matrix(channels, total, chan)
     for d in range(DIRECTIONS + 1):
         start_ref[d] = 0
     cluster_copy.wait()
@@ -104,8 +107,7 @@
     parts = [(x, t) for x in range(2) for t in range(TIME_SLOTS)]
     for part in range(baselines // chunk):
         copies[part].wait()
-        here = slice(part * chunk, (part + 1) * chunk)
-        validity = valid_ref[:, here].astype(F32)
+        own_rows = slice(part * rows, (part + 1) * rows)
 
         @pl.loop(0, DIRECTIONS // fold)
         def _(group):
@@ -113,25 +115,32 @@
             for k in range(fold):
                 d = group * fold + k
 
+                def patch(i):
+                    q = order_ref[i]
+                    return tuple(patches_ref[q, x, t, own_rows, :].astype(F32) for x, t in parts)
+
                 def add(i, sums):
-                    q = order_ref[i]
-                    return tuple(
-                        s + patches_ref[q, x, t, :, here].astype(F32) for s, (x, t) in zip(sums, parts)
-                    )
-
-                zero = jnp.zeros((channels, chunk), F32)
-                found.append(lax.fori_loop(start_ref[d], start_ref[d + 1], add, (zero,) * len(parts)))
-            rows = pl.ds(pl.multiple_of(group * 8, 8), 8)
-            power = None
-            for j, (x, t) in enumerate(parts):
-                s = jnp.concatenate([f[j] for f in found], axis=0)
-                model_ref[x, t, rows, here] = s
-                power = s * s if power is None else power + s * s
-            power_ref[rows, here] = power * jnp.concatenate([validity] * fold, axis=0)
+                    return tuple(s + p for s, p in zip(sums, patch(i)))
+
+                found.append(lax.fori_loop(start_ref[d] + 1, start_ref[d + 1], add, patch(start_ref[d])))
+            place = pl.ds(pl.multiple_of(group * 8, 8), 8)
+            for tile in range(chunk // LANES):
+                here = slice(part * chunk + tile * LANES, part * chunk + (tile + 1) * LANES)
+                mine = slice(tile * channels, (tile + 1) * channels)
+                power = None
+                for j, (x, t) in enumerate(parts):
+                    s = jnp.concatenate([f[j][mine] for f in found], axis=0)
+                    model_ref[x, t, place, here] = s
+                    power = s * s if power is None else power + s * s
+                validity = valid_ref[:, here].astype(F32)
+                power_ref[place, here] = power * jnp.concatenate([validity] * fold, axis=0)
 
 
 def prepare(cluster, patches, valid, total):
     channels, baselines = valid.shape
+    lead = patches.shape[:3]
+    tiled = patches.reshape(*lead, channels, baselines // LANES, LANES)
+    tiled = jnp.swapaxes(tiled, 3, 4).reshape(*lead, channels * baselines // LANES, LANES)
     chunk = min(PREP_CHUNK, baselines)
     per = DIRECTIONS * channels
     vmem = pl.BlockSpec(memory_space=pltpu.VMEM)
@@ -148,10 +157,10 @@
             jax.ShapeDtypeStruct((per, baselines), F32),
             jax.ShapeDtypeStruct((10 * HALF, per), F32),
             jax.ShapeDtypeStruct((6 * HALF, per), F32),
-            jax.ShapeDtypeStruct((2, 2 * per, 6 * HALF), F32),
+            jax.ShapeDtypeStruct((2 * per, 12 * HALF), F32),
         ],
         scratch_shapes=[
-            pltpu.VMEM(patches.shape, BF16),
+            pltpu.VMEM(tiled.shape, BF16),
             pltpu.VMEM(valid.shape, valid.dtype),
             pltpu.SMEM((SKY_PATCHES,), jnp.int32),
             pltpu.SemaphoreType.DMA((baselines // chunk + 2,)),
@@ -160,12 +169,12 @@
         ],
         compiler_params=pltpu.CompilerParams(vmem_limit_bytes=32 << 20),
         name="prepare",
-    )(*(pltpu.with_memory_space_constraint(v, pltpu.HBM) for v in (cluster, patches, valid)))
-
-
-def fitted_values(fit_ref, coefs):
-    out = jnp.dot(fit_ref[0], coefs[0], precision=HIGHEST, preferred_element_type=F32)
-    return out + jnp.dot(fit_ref[1], coefs[1], precision=HIGHEST, preferred_element_type=F32)
+    )(*(pltpu.with_memory_space_constraint(v, pltpu.HBM) for v in (cluster, tiled, valid)))
+
+
+def fitted_values(fit_ref, own_ref, other_ref):
+    coefs = jnp.concatenate([own_ref[...], other_ref[...]], axis=0)
+    return jnp.dot(fit_ref[...], coefs, precision=HIGHEST, preferred_element_type=F32)
 
 
 def sweep_kernel(first, blocks, owned, tile, *refs):
@@ -177,8 +186,9 @@
         (before_ref, fit_ref, own_coef_ref, other_coef_ref, picks_ref), refs = refs[:5], refs[5:]
         (model_ref, power_ref, valid_ref, visible_ref, normal_ref, right_ref,
          own_ref, other_ref, current_ref, *refs) = refs
-    rounded_ref, sums_ref, chosen_even, chosen_odd, terms_even, terms_odd = refs
-    chosen_refs, terms_refs = (chosen_even, chosen_odd), (terms_even, terms_odd)
+    rounded_ref, sums_ref, chosen_ref, terms_ref, ids_ref = refs
+    if first:
+        ids_ref[...] = iotas(ids_ref.shape)[0].astype(F32).astype(BF16)
     channels, baselines = valid_ref.shape
     per = DIRECTIONS * channels
     stations = blocks * owned
@@ -191,7 +201,7 @@
                     pair = jnp.concatenate([gain_refs[k][x, d + j] for j in range(fold)], axis=0)
                     current_ref[row:row + 8, k * owned:(k + 1) * owned] = pair
     else:
-        fitted = fitted_values(fit_ref, (own_coef_ref[...], other_coef_ref[...]))
+        fitted = fitted_values(fit_ref, own_coef_ref, other_coef_ref)
         current_ref[...] = 0.5 * (before_ref[...] + fitted)
     rounded_ref[...] = current_ref[...].astype(BF16)
 
@@ -200,21 +210,26 @@
             return slice(i * width, (i + 1) * width)
         return pl.ds(pl.multiple_of(i * width, width), width)
 
-    def choose(i, slot):
+    def choose(i):
         here = span(i, 2 * tile)
         if first:
             shift = lax.axis_index("bl") * owned
             place = stations_ref[:, span(i, tile)] - shift
             place = jnp.where(place < 0, place + stations, place)
-            place = jnp.concatenate([place[0:1, :], place[1:2, :]], axis=1)
-            ids = lax.broadcasted_iota(jnp.int32, (stations, 2 * tile), 0)
-            picks_ref[:, here] = (ids == place).astype(BF16)
-        chosen_refs[slot][...] = jnp.dot(rounded_ref[...], picks_ref[:, here], preferred_element_type=F32)
-
-    def terms(i, slot):
-        chosen_ref, terms_ref = chosen_refs[slot], terms_refs[slot]
+            columns = []
+            for part in range(tile // LANES):
+                columns += [place[k:k + 1, part * LANES:(part + 1) * LANES] for k in range(2)]
+            place = jnp.concatenate(columns, axis=1)
+            ids = ids_ref[...]
+            for start in range(0, stations, EXACT):
+                local = jnp.where((place >= start) & (place < start + EXACT), place - start, -1)
+                local = local.astype(F32).astype(BF16)
+                picks_ref[start:start + EXACT, here] = jnp.where(ids == local, jnp.ones((), BF16), jnp.zeros((), BF16))
+        chosen_ref[...] = jnp.dot(rounded_ref[...], picks_ref[:, here], preferred_element_type=F32)
+
+    def terms(i):
         for part in range(tile // LANES):
-            near, far = (slice(k * tile + part * LANES, k * tile + (part + 1) * LANES) for k in range(2))
+            near, far = (slice((2 * part + k) * LANES, (2 * part + k + 1) * LANES) for k in range(2))
             if isinstance(i, int):
                 along = slice(i * tile + part * LANES, i * tile + (part + 1) * LANES)
             else:
@@ -260,9 +275,9 @@
                         two = jnp.concatenate(rows[k][row // 8 - 1:row // 8 + 1], axis=0).astype(BF16)
                         terms_ref[(k % 3) * per + row - 8:(k % 3) * per + row + 8, (near, far)[k // 3]] = two
 
-    def add_up(i, slot):
+    def add_up(i):
         more = lax.dot_general(
-            picks_ref[:, span(i, 2 * tile)], terms_refs[slot][...], (((1,), (1,)), ((), ())),
+            picks_ref[:, span(i, 2 * tile)], terms_ref[...], (((1,), (1,)), ((), ())),
             preferred_element_type=F32,
         )
         if isinstance(i, int) and i == 0:
@@ -271,28 +286,22 @@
             sums_ref[...] += more
 
     count = baselines // tile
-    choose(0, 0)
-    choose(1, 1)
-    terms(0, 0)
-    add_up(0, 0)
-    choose(2, 0)
-    terms(1, 1)
-
-    @pl.loop(0, (count - 4) // 2)
-    def _(j):
-        i = 2 * j + 3
-        for k in range(2):
-            add_up(i + k - 2, 1 - k)
-            choose(i + k, 1 - k)
-            terms(i + k - 1, k)
-
-    for i in range(count - 1, count):
-        add_up(i - 2, i % 2)
-        choose(i, i % 2)
-        terms(i - 1, 1 - i % 2)
-    add_up(count - 2, count % 2)
-    terms(count - 1, 1 - count % 2)
-    add_up(count - 1, 1 - count % 2)
+    choose(0)
+    terms(0)
+    choose(1)
+    add_up(0)
+    terms(1)
+    choose(2)
+
+    @pl.loop(3, count)
+    def _(i):
+        add_up(i - 2)
+        terms(i - 1)
+        choose(i)
+
+    add_up(count - 2)
+    terms(count - 1)
+    add_up(count - 1)
 
     sums = sums_ref[...].T
     weight = sums[2 * per:3 * per, :] + 1.0 / blocks
@@ -329,9 +338,8 @@
             pltpu.VMEM((2 * per, count), BF16),
             pltpu.VMEM((count, 3 * per), F32),
             pltpu.VMEM((2 * per, 2 * SWEEP_TILE), F32),
-            pltpu.VMEM((2 * per, 2 * SWEEP_TILE), F32),
             pltpu.VMEM((3 * per, 2 * SWEEP_TILE), BF16),
-            pltpu.VMEM((3 * per, 2 * SWEEP_TILE), BF16),
+            pltpu.VMEM((EXACT, 2 * SWEEP_TILE), BF16),
         ],
         compiler_params=pltpu.CompilerParams(vmem_limit_bytes=24 << 20),
         name="sweep",
@@ -340,7 +348,7 @@
 
 def final_kernel(channels, before_ref, fit_ref, own_ref, other_ref, out_ref):
     per = DIRECTIONS * channels
-    result = 0.5 * (before_ref[:, 0:out_ref.shape[3]] + fitted_values(fit_ref, (own_ref[...], other_ref[...])))
+    result = 0.5 * (before_ref[:, 0:out_ref.shape[3]] + fitted_values(fit_ref, own_ref, other_ref))
     for x in range(2):
         for d in range(DIRECTIONS):
             row = x * per + d * channels

time: 65.2 us -> 60.4 us (0.926)
  Pallas kernels: 21 us -> 15.9 us
  starting transfers between devices: 16.5 us -> 17.4 us
    pallas_call x2, Pallas kernels: 15.9 us -> 11.4 us  [sweep(): pl.pallas_call(partial(sweep_kernel, first, blocks, owned, SWEEP_TILE), i...]
    ppermute x4, starting transfers between devices: 7.17 us -> 7.95 us  [from_later(): lax.ppermute(value, 'bl', [((j + k) % count, j) for j in range(count)])]
    ppermute x4, waiting for transfers between devices: 9.47 us -> 8.75 us  [from_later(): lax.ppermute(value, 'bl', [((j + k) % count, j) for j in range(count)])]
  transfers between devices with their start and end apart: 14 -> 14, of which waited for: 11 -> 12; matrix products, arithmetic and copies ran while one was open for 0% -> 0% of each run, Pallas kernels for 6% -> 6%
where the time goes in v2:
time: 60.4 us; the launch traced here: 60.3 us
  waiting for transfers between devices  26.4 us (44%)
  starting transfers between devices  17.4 us (29%)
  Pallas kernels  15.9 us (26%)
    ppermute x6, waiting for transfers between devices, over_chips(): lax.ppermute(v, 'chan', [(j, j ^ 2 * k) for j in range(count)])  12.5 us
    pallas_call x2, Pallas kernels, sweep(): pl.pallas_call(partial(sweep_kernel, first, blocks, owned, SWEEP_TILE), i...  11.4 us
    ppermute x6, starting transfers between devices, over_chips(): lax.ppermute(v, 'chan', [(j, j ^ 2 * k) for j in range(count)])  9.01 us
    ppermute x4, waiting for transfers between devices, from_later(): lax.ppermute(value, 'bl', [((j + k) % count, j) for j in range(count)])  8.75 us
    ppermute x4, starting transfers between devices, from_later(): lax.ppermute(value, 'bl', [((j + k) % count, j) for j in range(count)])  7.95 us
    ppermute x4, waiting for transfers between devices, other_core(): return lax.ppermute(value, 'chan', [(j, j ^ 1) for j in range(count)])  5.18 us
    pallas_call x1, Pallas kernels, prepare(): pl.pallas_call(partial(prep_kernel, total, channels, chunk), in_specs=[pl...  3.64 us
  transfers between devices with their start and end apart: 14, of which 12 were waited for; matrix products, arithmetic and copies ran while one was open for 0% of the time, Pallas kernels for 6%

profile of v2, /device:TPU:0, one launch (start us, length us, event | category | flops | bytes accessed | tf_op | source)
XLA Modules:
  0.0 60.3 jit_solution(17691868070618714630)
XLA Ops:
  0.0 3.0 %collective-permute-start = (f32[2,16,4,256]{3,2,1,0:T(4,128)}, f32[2,16,4,256]{3,2,1,0:T(4,128)S(1)}, u32[]{:S(2)}, u32[]{:S(2)}) collective-permute-start(f32[2,16,4,256]{3,2,1,0:T(4,128)} %refs_0_.1), channel_id=1, source_target_pairs={{1,0},{0,1},{3,2},{2,3},{5,4},{4,5},{7,6},{6,7},{9,8},{8,9},{11,10... | collective-permute-start | bytes 393224 | tf_op jit(solution)/shard_map/ppermute | solution.py:399
  3.0 3.6 %prepare.1 = (f32[2,2,64,4096]{3,2,1,0:T(8,128)S(1)}, f32[64,4096]{1,0:T(8,128)S(1)}, f32[80,64]{1,0:T(8,128)S(1)}, f32[48,64]{1,0:T(8,128)S(1)}, f32[128,96]{1,0:T(8,128)S(1)}) custom-call(s32[32]{0:T(128)} %bitcast.7, bf16[32,2,2,128,128]{4,3,2,1,0:T(8,128)(2,1)} %bitcast.6, s32[4,4096]{1,0:T(4,128)} %refs_7_.1), custom_call_target="tpu_custom_call" | custom-call | tf_op jit(solution)/shard_map/prepare/pallas_call | solution.py:147
  6.7 0.1 collective-permute-done.refs_1_
  6.8 5.9 %sweep.2 = (f32[88,512]{1,0:T(8,128)S(1)}, f32[88,512]{1,0:T(8,128)S(1)}, f32[128,512]{1,0:T(8,128)S(1)}, bf16[512,8192]{1,0:T(8,128)(2,1)S(1)}) custom-call(f32[2,16,4,256]{3,2,1,0:T(4,128)S(1)} %copy-done.2, f32[2,16,4,256]{3,2,1,0:T(4,128)S(1)} %collective-permute-done.refs_1_, s32[2,4096]{1,0:T(2,128)S(1)} %copy-done.3, ...), custom_call_target="tpu_custom_call" | custom-call | tf_op jit(solution)/shard_map/sweep/pallas_call | solution.py:332
  12.7 0.1 collective-permute-start.1
  12.8 1.4 %collective-permute-done.1 = f32[88,512]{1,0:T(8,128)S(1)} collective-permute-done((f32[88,512]{1,0:T(8,128)S(1)}, f32[88,512]{1,0:T(8,128)S(1)}, u32[]{:S(2)}, u32[]{:S(2)}) %collective-permute-start.1) | collective-permute-done | bytes 180256 | tf_op jit(solution)/shard_map/ppermute | solution.py:394
  14.2 1.8 %collective-permute-start.2 = (f32[88,256]{1,0:T(8,128)S(1)}, f32[88,256]{1,0:T(8,128)S(1)}, u32[]{:S(2)}, u32[]{:S(2)}) collective-permute-start(f32[88,256]{1,0:T(8,128)S(1)} %slice.105), channel_id=1, source_target_pairs={{1,0},{0,1},{3,2},{2,3},{5,4},{4,5},{7,6},{6,7},{9,8},{8,9},{11,10... | collective-permute-start | bytes 270344 | tf_op jit(solution)/shard_map/ppermute | solution.py:399
  16.0 2.9 %collective-permute-done.2 = f32[88,256]{1,0:T(8,128)S(1)} collective-permute-done((f32[88,256]{1,0:T(8,128)S(1)}, f32[88,256]{1,0:T(8,128)S(1)}, u32[]{:S(2)}, u32[]{:S(2)}) %collective-permute-start.2) | collective-permute-done | bytes 90144 | tf_op jit(solution)/shard_map/ppermute | solution.py:399
  19.0 3.9 %collective-permute-start.5 = (f32[88,256]{1,0:T(8,128)S(1)}, f32[88,256]{1,0:T(8,128)S(1)}, u32[]{:S(2)}, u32[]{:S(2)}) collective-permute-start(f32[88,256]{1,0:T(8,128)S(1)} %slice_add_fusion.1), channel_id=1, source_target_pairs={{0,12},{2,14},{4,8},{6,10},{8,4},{10,6},{12,0},{14,2},{1,13},{3,15... | collective-permute-start | bytes 270344 | tf_op jit(solution)/shard_map/ppermute | solution.py:405
  22.9 0.6 %collective-permute-start.3 = (f32[88,256]{1,0:T(8,128)S(1)}, f32[88,256]{1,0:T(8,128)S(1)}, u32[]{:S(2)}, u32[]{:S(2)}) collective-permute-start(f32[88,256]{1,0:T(8,128)S(1)} %slice_add_fusion.1), channel_id=1, source_target_pairs={{0,4},{2,6},{4,0},{6,2},{8,12},{10,14},{12,8},{14,10},{1,5},{3,7},... | collective-permute-start | bytes 270344 | tf_op jit(solution)/shard_map/ppermute | solution.py:405
  23.5 2.9 %collective-permute-done.5 = f32[88,256]{1,0:T(8,128)S(1)} collective-permute-done((f32[88,256]{1,0:T(8,128)S(1)}, f32[88,256]{1,0:T(8,128)S(1)}, u32[]{:S(2)}, u32[]{:S(2)}) %collective-permute-start.5) | collective-permute-done | bytes 90144 | tf_op jit(solution)/shard_map/ppermute | solution.py:405
  26.4 3.5 %collective-permute-done.4 = f32[88,256]{1,0:T(8,128)S(1)} collective-permute-done((f32[88,256]{1,0:T(8,128)S(1)}, f32[88,256]{1,0:T(8,128)S(1)}, u32[]{:S(2)}, u32[]{:S(2)}) %collective-permute-start.4) | collective-permute-done | bytes 90144 | tf_op jit(solution)/shard_map/ppermute | solution.py:405
  29.9 0.1 constant_dynamic-update-slice_fusion.5
  30.1 1.6 %collective-permute-start.6 = (f32[48,256]{1,0:T(8,128)S(1)}, f32[48,256]{1,0:T(8,128)S(1)}, u32[]{:S(2)}, u32[]{:S(2)}) collective-permute-start(f32[48,256]{1,0:T(8,128)S(1)} %constant_dynamic-update-slice_fusion), channel_id=1, source_target_pairs={{1,0},{0,1},{3,2},{2,3},{5,4},{4,5},{7,6},{6,7},{9,8},{8,9},{11,10... | collective-permute-start | bytes 147464 | tf_op jit(solution)/shard_map/ppermute | solution.py:399
  31.7 2.6 %collective-permute-done.6 = f32[48,256]{1,0:T(8,128)S(1)} collective-permute-done((f32[48,256]{1,0:T(8,128)S(1)}, f32[48,256]{1,0:T(8,128)S(1)}, u32[]{:S(2)}, u32[]{:S(2)}) %collective-permute-start.6) | collective-permute-done | bytes 49184 | tf_op jit(solution)/shard_map/ppermute | solution.py:399
  34.3 0.1 collective-permute-start.7
  34.4 1.3 %collective-permute-done.7.refs_3_ = f32[48,512]{1,0:T(8,128)S(1)} collective-permute-done((f32[48,512]{1,0:T(8,128)S(1)}, f32[48,512]{1,0:T(8,128)S(1)}, u32[]{:S(2)}, u32[]{:S(2)}) %collective-permute-start.7) | collective-permute-done | bytes 98336 | tf_op jit(solution)/shard_map/ppermute | solution.py:394
  35.6 5.4 %sweep.3 = (f32[88,512]{1,0:T(8,128)S(1)}, f32[88,512]{1,0:T(8,128)S(1)}, f32[128,512]{1,0:T(8,128)S(1)}) custom-call(f32[128,512]{1,0:T(8,128)S(1)} %get-tuple-element.21.refs_0_, f32[128,96]{1,0:T(8,128)S(1)} %get-tuple-element.22.refs_1_.fit_ref, f32[48,512]{1,0:T(8,128)S(1)} %pad_maximum_fusion.refs_2_, f32[48,512]{1,0:T(8,128)S(1)} %collective-permute-done.7.refs_3_, ...), custom_call_target="tpu_custom_call" | custom-call | tf_op jit(solution)/shard_map/sweep/pallas_call | solution.py:332
  41.1 0.2 collective-permute-start.8
  41.3 1.3 %collective-permute-done.8 = f32[88,512]{1,0:T(8,128)S(1)} collective-permute-done((f32[88,512]{1,0:T(8,128)S(1)}, f32[88,512]{1,0:T(8,128)S(1)}, u32[]{:S(2)}, u32[]{:S(2)}) %collective-permute-start.8) | collective-permute-done | bytes 180256 | tf_op jit(solution)/shard_map/ppermute | solution.py:394
  42.6 1.6 %collective-permute-start.9 = (f32[88,256]{1,0:T(8,128)S(1)}, f32[88,256]{1,0:T(8,128)S(1)}, u32[]{:S(2)}, u32[]{:S(2)}) collective-permute-start(f32[88,256]{1,0:T(8,128)S(1)} %slice.118), channel_id=1, source_target_pairs={{1,0},{0,1},{3,2},{2,3},{5,4},{4,5},{7,6},{6,7},{9,8},{8,9},{11,10... | collective-permute-start | bytes 270344 | tf_op jit(solution)/shard_map/ppermute | solution.py:399
  44.2 3.2 %collective-permute-done.9 = f32[88,256]{1,0:T(8,128)S(1)} collective-permute-done((f32[88,256]{1,0:T(8,128)S(1)}, f32[88,256]{1,0:T(8,128)S(1)}, u32[]{:S(2)}, u32[]{:S(2)}) %collective-permute-start.9) | collective-permute-done | bytes 90144 | tf_op jit(solution)/shard_map/ppermute | solution.py:399
  47.4 2.7 %collective-permute-start.12 = (f32[88,256]{1,0:T(8,128)S(1)}, f32[88,256]{1,0:T(8,128)S(1)}, u32[]{:S(2)}, u32[]{:S(2)}) collective-permute-start(f32[88,256]{1,0:T(8,128)S(1)} %slice_add_fusion), channel_id=1, source_target_pairs={{0,12},{2,14},{4,8},{6,10},{8,4},{10,6},{12,0},{14,2},{1,13},{3,15... | collective-permute-start | bytes 270344 | tf_op jit(solution)/shard_map/ppermute | solution.py:405
  50.0 0.0 collective-permute-start.11
  50.0 1.8 %collective-permute-start.10 = (f32[88,256]{1,0:T(8,128)S(1)}, f32[88,256]{1,0:T(8,128)S(1)}, u32[]{:S(2)}, u32[]{:S(2)}) collective-permute-start(f32[88,256]{1,0:T(8,128)S(1)} %slice_add_fusion), channel_id=1, source_target_pairs={{0,4},{2,6},{4,0},{6,2},{8,12},{10,14},{12,8},{14,10},{1,5},{3,7},... | collective-permute-start | bytes 270344 | tf_op jit(solution)/shard_map/ppermute | solution.py:405
  51.8 2.6 %collective-permute-done.12 = f32[88,256]{1,0:T(8,128)S(1)} collective-permute-done((f32[88,256]{1,0:T(8,128)S(1)}, f32[88,256]{1,0:T(8,128)S(1)}, u32[]{:S(2)}, u32[]{:S(2)}) %collective-permute-start.12) | collective-permute-done | bytes 90144 | tf_op jit(solution)/shard_map/ppermute | solution.py:405
  54.4 3.5 %collective-permute-done.11 = f32[88,256]{1,0:T(8,128)S(1)} collective-permute-done((f32[88,256]{1,0:T(8,128)S(1)}, f32[88,256]{1,0:T(8,128)S(1)}, u32[]{:S(2)}, u32[]{:S(2)}) %collective-permute-start.11) | collective-permute-done | bytes 90144 | tf_op jit(solution)/shard_map/ppermute | solution.py:405
  57.9 0.0 collective-permute-done.10
  57.9 0.1 constant_dynamic-update-slice_fusion.11
  58.1 0.1 collective-permute-start.13
  58.1 1.2 %collective-permute-done.13.other_ref = f32[48,256]{1,0:T(8,128)S(1)} collective-permute-done((f32[48,256]{1,0:T(8,128)S(1)}, f32[48,256]{1,0:T(8,128)S(1)}, u32[]{:S(2)}, u32[]{:S(2)}) %collective-permute-start.13) | collective-permute-done | bytes 49184 | tf_op jit(solution)/shard_map/ppermute | solution.py:394
  59.4 0.9 %finish.1 = f32[2,16,4,256]{3,2,1,0:T(4,128)} custom-call(f32[128,512]{1,0:T(8,128)S(1)} %get-tuple-element.26.before_ref, f32[128,96]{1,0:T(8,128)S(1)} %get-tuple-element.22.refs_1_.fit_ref, f32[48,256]{1,0:T(8,128)S(1)} %constant_dynamic-update-slice_fusion.6.own_ref, f32[48,256]{1,0:T(8,128)S(1)} %collective-permute-done.13.other_ref), custom_call_target="tpu_custom_call" | custom-call | tf_op jit(solution)/shard_map/finish/pallas_call | solution.py:360
  (29 shorter events, 0.3 us)
Async XLA Ops:
  0.0 6.7 %copy-start.2 = (f32[2,16,4,256]{3,2,1,0:T(4,128)S(1)}, f32[2,16,4,256]{3,2,1,0:T(4,128)}, u32[]{:S(2)}) copy-start(f32[2,16,4,256]{3,2,1,0:T(4,128)} %refs_0_.1) | copy-start | bytes 393220
  0.0 6.7 %copy-start.1 = (s32[4,4096]{1,0:T(4,128)S(1)}, s32[4,4096]{1,0:T(4,128)}, u32[]{:S(2)}) copy-start(s32[4,4096]{1,0:T(4,128)} %refs_7_.1) | copy-start | bytes 196612
  0.0 6.7 %copy-start = (f32[2,2,4,4096]{3,2,1,0:T(4,128)S(1)}, f32[2,2,4,4096]{3,2,1,0:T(4,128)}, u32[]{:S(2)}) copy-start(f32[2,2,4,4096]{3,2,1,0:T(4,128)} %refs_8_.1) | copy-start | bytes 786436
  0.0 6.7 %copy-start.3 = (s32[2,4096]{1,0:T(2,128)S(1)}, s32[2,4096]{1,0:T(2,128)}, u32[]{:S(2)}) copy-start(s32[2,4096]{1,0:T(2,128)} %refs_2_.1) | copy-start | bytes 98308
  0.0 6.7 %collective-permute-start = (f32[2,16,4,256]{3,2,1,0:T(4,128)}, f32[2,16,4,256]{3,2,1,0:T(4,128)S(1)}, u32[]{:S(2)}, u32[]{:S(2)}) collective-permute-start(f32[2,16,4,256]{3,2,1,0:T(4,128)} %refs_0_.1), channel_id=1, source_target_pairs={{1,0},{0,1},{3,2},{2,3},{5,4},{4,5},{7,6},{6,7},{9,8},{8,9},{11,10... | collective-permute-start | bytes 393224 | tf_op jit(solution)/shard_map/ppermute | solution.py:399
  12.7 1.5 %collective-permute-start.1 = (f32[88,512]{1,0:T(8,128)S(1)}, f32[88,512]{1,0:T(8,128)S(1)}, u32[]{:S(2)}, u32[]{:S(2)}) collective-permute-start(f32[88,512]{1,0:T(8,128)S(1)} %get-tuple-element.24), channel_id=1, source_target_pairs={{0,2},{2,0},{4,6},{6,4},{8,10},{10,8},{12,14},{14,12},{1,3},{3,1},... | collective-permute-start | bytes 540680 | tf_op jit(solution)/shard_map/ppermute | solution.py:394
  14.2 4.7 %collective-permute-start.2 = (f32[88,256]{1,0:T(8,128)S(1)}, f32[88,256]{1,0:T(8,128)S(1)}, u32[]{:S(2)}, u32[]{:S(2)}) collective-permute-start(f32[88,256]{1,0:T(8,128)S(1)} %slice.105), channel_id=1, source_target_pairs={{1,0},{0,1},{3,2},{2,3},{5,4},{4,5},{7,6},{6,7},{9,8},{8,9},{11,10... | collective-permute-start | bytes 270344 | tf_op jit(solution)/shard_map/ppermute | solution.py:399
  19.0 7.4 %collective-permute-start.5 = (f32[88,256]{1,0:T(8,128)S(1)}, f32[88,256]{1,0:T(8,128)S(1)}, u32[]{:S(2)}, u32[]{:S(2)}) collective-permute-start(f32[88,256]{1,0:T(8,128)S(1)} %slice_add_fusion.1), channel_id=1, source_target_pairs={{0,12},{2,14},{4,8},{6,10},{8,4},{10,6},{12,0},{14,2},{1,13},{3,15... | collective-permute-start | bytes 270344 | tf_op jit(solution)/shard_map/ppermute | solution.py:405
  22.9 7.0 %collective-permute-start.4 = (f32[88,256]{1,0:T(8,128)S(1)}, f32[88,256]{1,0:T(8,128)S(1)}, u32[]{:S(2)}, u32[]{:S(2)}) collective-permute-start(f32[88,256]{1,0:T(8,128)S(1)} %slice_add_fusion.1), channel_id=1, source_target_pairs={{0,8},{2,10},{4,12},{6,14},{8,0},{10,2},{12,4},{14,6},{1,9},{3,11}... | collective-permute-start | bytes 270344 | tf_op jit(solution)/shard_map/ppermute | solution.py:405
  22.9 7.0 %collective-permute-start.3 = (f32[88,256]{1,0:T(8,128)S(1)}, f32[88,256]{1,0:T(8,128)S(1)}, u32[]{:S(2)}, u32[]{:S(2)}) collective-permute-start(f32[88,256]{1,0:T(8,128)S(1)} %slice_add_fusion.1), channel_id=1, source_target_pairs={{0,4},{2,6},{4,0},{6,2},{8,12},{10,14},{12,8},{14,10},{1,5},{3,7},... | collective-permute-start | bytes 270344 | tf_op jit(solution)/shard_map/ppermute | solution.py:405
  30.1 4.2 %collective-permute-start.6 = (f32[48,256]{1,0:T(8,128)S(1)}, f32[48,256]{1,0:T(8,128)S(1)}, u32[]{:S(2)}, u32[]{:S(2)}) collective-permute-start(f32[48,256]{1,0:T(8,128)S(1)} %constant_dynamic-update-slice_fusion), channel_id=1, source_target_pairs={{1,0},{0,1},{3,2},{2,3},{5,4},{4,5},{7,6},{6,7},{9,8},{8,9},{11,10... | collective-permute-start | bytes 147464 | tf_op jit(solution)/shard_map/ppermute | solution.py:399
  34.3 1.4 %collective-permute-start.7 = (f32[48,512]{1,0:T(8,128)S(1)}, f32[48,512]{1,0:T(8,128)S(1)}, u32[]{:S(2)}, u32[]{:S(2)}) collective-permute-start(f32[48,512]{1,0:T(8,128)S(1)} %pad_maximum_fusion.refs_2_), channel_id=1, source_target_pairs={{0,2},{2,0},{4,6},{6,4},{8,10},{10,8},{12,14},{14,12},{1,3},{3,1},... | collective-permute-start | bytes 294920 | tf_op jit(solution)/shard_map/ppermute | solution.py:394
  41.1 1.5 %collective-permute-start.8 = (f32[88,512]{1,0:T(8,128)S(1)}, f32[88,512]{1,0:T(8,128)S(1)}, u32[]{:S(2)}, u32[]{:S(2)}) collective-permute-start(f32[88,512]{1,0:T(8,128)S(1)} %get-tuple-element.28), channel_id=1, source_target_pairs={{0,2},{2,0},{4,6},{6,4},{8,10},{10,8},{12,14},{14,12},{1,3},{3,1},... | collective-permute-start | bytes 540680 | tf_op jit(solution)/shard_map/ppermute | solution.py:394
  42.6 4.7 %collective-permute-start.9 = (f32[88,256]{1,0:T(8,128)S(1)}, f32[88,256]{1,0:T(8,128)S(1)}, u32[]{:S(2)}, u32[]{:S(2)}) collective-permute-start(f32[88,256]{1,0:T(8,128)S(1)} %slice.118), channel_id=1, source_target_pairs={{1,0},{0,1},{3,2},{2,3},{5,4},{4,5},{7,6},{6,7},{9,8},{8,9},{11,10... | collective-permute-start | bytes 270344 | tf_op jit(solution)/shard_map/ppermute | solution.py:399
  47.4 7.0 %collective-permute-start.12 = (f32[88,256]{1,0:T(8,128)S(1)}, f32[88,256]{1,0:T(8,128)S(1)}, u32[]{:S(2)}, u32[]{:S(2)}) collective-permute-start(f32[88,256]{1,0:T(8,128)S(1)} %slice_add_fusion), channel_id=1, source_target_pairs={{0,12},{2,14},{4,8},{6,10},{8,4},{10,6},{12,0},{14,2},{1,13},{3,15... | collective-permute-start | bytes 270344 | tf_op jit(solution)/shard_map/ppermute | solution.py:405
  50.0 7.9 %collective-permute-start.11 = (f32[88,256]{1,0:T(8,128)S(1)}, f32[88,256]{1,0:T(8,128)S(1)}, u32[]{:S(2)}, u32[]{:S(2)}) collective-permute-start(f32[88,256]{1,0:T(8,128)S(1)} %slice_add_fusion), channel_id=1, source_target_pairs={{0,8},{2,10},{4,12},{6,14},{8,0},{10,2},{12,4},{14,6},{1,9},{3,11}... | collective-permute-start | bytes 270344 | tf_op jit(solution)/shard_map/ppermute | solution.py:405
  50.0 7.9 %collective-permute-start.10 = (f32[88,256]{1,0:T(8,128)S(1)}, f32[88,256]{1,0:T(8,128)S(1)}, u32[]{:S(2)}, u32[]{:S(2)}) collective-permute-start(f32[88,256]{1,0:T(8,128)S(1)} %slice_add_fusion), channel_id=1, source_target_pairs={{0,4},{2,6},{4,0},{6,2},{8,12},{10,14},{12,8},{14,10},{1,5},{3,7},... | collective-permute-start | bytes 270344 | tf_op jit(solution)/shard_map/ppermute | solution.py:405
  58.1 1.3 %collective-permute-start.13 = (f32[48,256]{1,0:T(8,128)S(1)}, f32[48,256]{1,0:T(8,128)S(1)}, u32[]{:S(2)}, u32[]{:S(2)}) collective-permute-start(f32[48,256]{1,0:T(8,128)S(1)} %constant_dynamic-update-slice_fusion.6.own_ref), channel_id=1, source_target_pairs={{0,2},{2,0},{4,6},{6,4},{8,10},{10,8},{12,14},{14,12},{1,3},{3,1},... | collective-permute-start | bytes 147464 | tf_op jit(solution)/shard_map/ppermute | solution.py:394

commit v3 on v2

--- a/solution.py
+++ b/solution.py
@@ -15,6 +15,7 @@
 EXACT = 256
 PREP_CHUNK = 1024
 SWEEP_TILE = 1024
+OWN_CHUNK = 2048
 HALF = DIRECTIONS // 2
 HIGHEST = lax.Precision.HIGHEST
 F32, BF16 = jnp.float32, jnp.bfloat16
@@ -177,16 +178,38 @@
     return jnp.dot(fit_ref[...], coefs, precision=HIGHEST, preferred_element_type=F32)
 
 
+def station_sums(picks_ref, terms_ref, rows, columns):
+    return lax.dot_general(
+        picks_ref[rows, columns], terms_ref[:, columns], (((1,), (1,)), ((), ())), preferred_element_type=F32
+    )
+
+
+def moments(sums, current, normal_ref, right_ref, blocks, own_ref, other_ref):
+    per = current.shape[0] // 2
+    sums = sums.T
+    weight = sums[2 * per:3 * per, :] + 1.0 / blocks
+    product = partial(jnp.dot, precision=HIGHEST, preferred_element_type=F32)
+    normal = product(normal_ref[...], weight)
+    right = [
+        product(right_ref[...], weight * current[x * per:(x + 1) * per, :] + sums[x * per:(x + 1) * per, :])
+        for x in range(2)
+    ]
+    for half, out in enumerate((own_ref, other_ref)):
+        out[0:5 * HALF, :] = normal[half * 5 * HALF:(half + 1) * 5 * HALF, :]
+        for x in range(2):
+            out[(5 + 3 * x) * HALF:(8 + 3 * x) * HALF, :] = right[x][half * 3 * HALF:(half + 1) * 3 * HALF, :]
+
+
 def sweep_kernel(first, blocks, owned, tile, *refs):
     if first:
         gain_refs, refs = refs[:blocks], refs[blocks:]
         (stations_ref, model_ref, power_ref, valid_ref, visible_ref, normal_ref, right_ref,
-         own_ref, other_ref, current_ref, picks_ref, *refs) = refs
+         own_ref, other_ref, current_ref, terms_ref, picks_ref, *refs) = refs
     else:
         (before_ref, fit_ref, own_coef_ref, other_coef_ref, picks_ref), refs = refs[:5], refs[5:]
         (model_ref, power_ref, valid_ref, visible_ref, normal_ref, right_ref,
-         own_ref, other_ref, current_ref, *refs) = refs
-    rounded_ref, sums_ref, chosen_ref, terms_ref, ids_ref = refs
+         own_ref, other_ref, current_ref, terms_ref, *refs) = refs
+    rounded_ref, sums_ref, chosen_ref, ids_ref = refs
     if first:
         ids_ref[...] = iotas(ids_ref.shape)[0].astype(F32).astype(BF16)
     channels, baselines = valid_ref.shape
@@ -273,13 +296,14 @@
                 if row % 16 == 8:
                     for k in range(6):
                         two = jnp.concatenate(rows[k][row // 8 - 1:row // 8 + 1], axis=0).astype(BF16)
-                        terms_ref[(k % 3) * per + row - 8:(k % 3) * per + row + 8, (near, far)[k // 3]] = two
+                        place = (k % 3) * per + row - 8
+                        column = (2 * (i * (tile // LANES) + part) + k // 3) * LANES
+                        if not isinstance(i, int):
+                            column = pl.multiple_of(column, LANES)
+                        terms_ref[place:place + 16, pl.ds(column, LANES)] = two
 
     def add_up(i):
-        more = lax.dot_general(
-            picks_ref[:, span(i, 2 * tile)], terms_ref[...], (((1,), (1,)), ((), ())),
-            preferred_element_type=F32,
-        )
+        more = station_sums(picks_ref, terms_ref, slice(owned, stations), span(i, 2 * tile))
         if isinstance(i, int) and i == 0:
             sums_ref[...] = more
         else:
@@ -303,18 +327,32 @@
     terms(count - 1)
     add_up(count - 1)
 
-    sums = sums_ref[...].T
-    weight = sums[2 * per:3 * per, :] + 1.0 / blocks
-    product = partial(jnp.dot, precision=HIGHEST, preferred_element_type=F32)
-    normal = product(normal_ref[...], weight)
-    right = [
-        product(right_ref[...], weight * current_ref[x * per:(x + 1) * per, :] + sums[x * per:(x + 1) * per, :])
-        for x in range(2)
-    ]
-    for half, out in enumerate((own_ref, other_ref)):
-        out[0:5 * HALF, :] = normal[half * 5 * HALF:(half + 1) * 5 * HALF, :]
-        for x in range(2):
-            out[(5 + 3 * x) * HALF:(8 + 3 * x) * HALF, :] = right[x][half * 3 * HALF:(half + 1) * 3 * HALF, :]
+    moments(sums_ref[...], current_ref[:, owned:stations], normal_ref, right_ref, blocks, own_ref, other_ref)
+
+
+def own_kernel(blocks, chunk, picks_ref, terms_ref, current_ref, normal_ref, right_ref, own_ref, other_ref):
+    owned = own_ref.shape[1]
+    sums = None
+    for start in range(0, picks_ref.shape[1], chunk):
+        more = station_sums(picks_ref, terms_ref, slice(0, owned), slice(start, start + chunk))
+        sums = more if sums is None else sums + more
+    moments(sums, current_ref[:, 0:owned], normal_ref, right_ref, blocks, own_ref, other_ref)
+
+
+def own_moments(picks, terms, current, normal, right, owned, blocks):
+    vmem = pl.BlockSpec(memory_space=pltpu.VMEM)
+    return pl.pallas_call(
+        partial(own_kernel, blocks, OWN_CHUNK),
+        in_specs=[vmem] * 5,
+        out_specs=[vmem] * 2,
+        out_shape=[jax.ShapeDtypeStruct((11 * HALF, owned), F32)] * 2,
+        compiler_params=pltpu.CompilerParams(vmem_limit_bytes=16 << 20),
+        cost_estimate=pl.CostEstimate(
+            flops=2 * owned * picks.shape[1] * terms.shape[0], transcendentals=0,
+            bytes_accessed=2 * picks.shape[1] * (owned + terms.shape[0]),
+        ),
+        name="own_moments",
+    )(picks, terms, current, normal, right)
 
 
 def sweep(first, inputs, model, power, valid, visible, normal, right, owned, blocks):
@@ -323,9 +361,10 @@
     count = owned * blocks
     vmem = pl.BlockSpec(memory_space=pltpu.VMEM)
     outs = [
-        jax.ShapeDtypeStruct((11 * HALF, count), F32),
-        jax.ShapeDtypeStruct((11 * HALF, count), F32),
+        jax.ShapeDtypeStruct((11 * HALF, count - owned), F32),
+        jax.ShapeDtypeStruct((11 * HALF, count - owned), F32),
         jax.ShapeDtypeStruct((2 * per, count), F32),
+        jax.ShapeDtypeStruct((3 * per, 2 * baselines), BF16),
     ]
     if first:
         outs.append(jax.ShapeDtypeStruct((count, 2 * baselines), BF16))
@@ -336,9 +375,8 @@
         out_shape=outs,
         scratch_shapes=[
             pltpu.VMEM((2 * per, count), BF16),
-            pltpu.VMEM((count, 3 * per), F32),
+            pltpu.VMEM((count - owned, 3 * per), F32),
             pltpu.VMEM((2 * per, 2 * SWEEP_TILE), F32),
-            pltpu.VMEM((3 * per, 2 * SWEEP_TILE), BF16),
             pltpu.VMEM((EXACT, 2 * SWEEP_TILE), BF16),
         ],
         compiler_params=pltpu.CompilerParams(vmem_limit_bytes=24 << 20),
@@ -426,13 +464,18 @@
     inputs = all_gains + [baseline_stations]
     picks = None
     for number in range(ITERS):
-        own, other, current, *made = sweep(number == 0, inputs, *common)
+        own, other, current, terms, *made = sweep(number == 0, inputs, *common)
         picks = made[0] if made else picks
-        mine = own + other_core(other)
-        part = lambda k: mine[:, k * owned:(k + 1) * owned]
-        kept = part(0)
-        for k in range(1, blocks):
-            kept = kept + from_later(part(blocks - k), k)
+        others = own + other_core(other)
+        others, terms = lax.optimization_barrier((others, terms))
+        received = [
+            from_later(others[:, (blocks - k - 1) * owned:(blocks - k) * owned], k) for k in range(1, blocks)
+        ]
+        own, other = own_moments(picks, terms, current, normal, right, owned, blocks)
+        kept = own
+        for part in received:
+            kept = kept + part
+        kept = lax.optimization_barrier(kept) + other_core(other)
         coefs = solve(over_chips(kept))
         if number < ITERS - 1:
             coefs = jnp.concatenate([coefs] + [from_later(coefs, k) for k in range(1, blocks)], axis=1)

time: 60.4 us -> 59.7 us (0.988)
  Pallas kernels: 15.9 us -> 18.4 us
  starting transfers between devices: 17.4 us -> 15.7 us
  waiting for transfers between devices: 26.4 us -> 24.9 us
    pallas_call x0 -> x2, Pallas kernels: none -> 3.74 us  [own_moments(): pl.pallas_call(partial(own_kernel, blocks, OWN_CHUNK), in_specs=[vmem] *...]
    ppermute x4, waiting for transfers between devices: 8.75 us -> 6.55 us  [from_later(): lax.ppermute(value, 'bl', [((j + k) % count, j) for j in range(count)])]
    ppermute x4, starting transfers between devices: 7.95 us -> 6.25 us  [from_later(): lax.ppermute(value, 'bl', [((j + k) % count, j) for j in range(count)])]
    pallas_call x2, Pallas kernels: 11.4 us -> 10.1 us  [sweep(): pl.pallas_call(partial(sweep_kernel, first, blocks, owned, SWEEP_TILE), i...]
    ppermute x6, waiting for transfers between devices: 12.5 us -> 13.2 us  [over_chips(): lax.ppermute(v, 'chan', [(j, j ^ 2 * k) for j in range(count)])]
    ppermute x4 -> x6, waiting for transfers between devices: 5.18 us -> 5.2 us  [other_core(): return lax.ppermute(value, 'chan', [(j, j ^ 1) for j in range(count)])]
  transfers between devices with their start and end apart: 14 -> 16, of which waited for: 12 -> 13; matrix products, arithmetic and copies ran while one was open for 0% -> 0% of each run, Pallas kernels for 6% -> 12%
where the time goes in v3:
time: 59.7 us; the launch traced here: 59.6 us
  waiting for transfers between devices  24.9 us (42%)
  Pallas kernels  18.4 us (31%)
  starting transfers between devices  15.7 us (26%)
    ppermute x6, waiting for transfers between devices, over_chips(): lax.ppermute(v, 'chan', [(j, j ^ 2 * k) for j in range(count)])  13.2 us
    pallas_call x2, Pallas kernels, sweep(): pl.pallas_call(partial(sweep_kernel, first, blocks, owned, SWEEP_TILE), i...  10.1 us
    ppermute x6, starting transfers between devices, over_chips(): lax.ppermute(v, 'chan', [(j, j ^ 2 * k) for j in range(count)])  8.91 us
    ppermute x4, waiting for transfers between devices, from_later(): lax.ppermute(value, 'bl', [((j + k) % count, j) for j in range(count)])  6.55 us
    ppermute x4, starting transfers between devices, from_later(): lax.ppermute(value, 'bl', [((j + k) % count, j) for j in range(count)])  6.25 us
    ppermute x6, waiting for transfers between devices, other_core(): return lax.ppermute(value, 'chan', [(j, j ^ 1) for j in range(count)])  5.2 us
    pallas_call x2, Pallas kernels, own_moments(): pl.pallas_call(partial(own_kernel, blocks, OWN_CHUNK), in_specs=[vmem] *...  3.74 us
    pallas_call x1, Pallas kernels, prepare(): pl.pallas_call(partial(prep_kernel, total, channels, chunk), in_specs=[pl...  3.64 us
  transfers between devices with their start and end apart: 16, of which 13 were waited for; matrix products, arithmetic and copies ran while one was open for 0% of the time, Pallas kernels for 12%

profile of v3, /device:TPU:0, one launch (start us, length us, event | category | flops | bytes accessed | tf_op | source)
XLA Modules:
  0.0 59.6 jit_solution(12651798290891221088)
XLA Ops:
  0.0 3.0 %collective-permute-start = (f32[2,16,4,256]{3,2,1,0:T(4,128)}, f32[2,16,4,256]{3,2,1,0:T(4,128)S(1)}, u32[]{:S(2)}, u32[]{:S(2)}) collective-permute-start(f32[2,16,4,256]{3,2,1,0:T(4,128)} %refs_0_.1), channel_id=1, source_target_pairs={{1,0},{0,1},{3,2},{2,3},{5,4},{4,5},{7,6},{6,7},{9,8},{8,9},{11,10... | collective-permute-start | bytes 393224 | tf_op jit(solution)/shard_map/ppermute | solution.py:437
  3.0 3.6 %prepare.1 = (f32[2,2,64,4096]{3,2,1,0:T(8,128)S(1)}, f32[64,4096]{1,0:T(8,128)S(1)}, f32[80,64]{1,0:T(8,128)S(1)}, f32[48,64]{1,0:T(8,128)S(1)}, f32[128,96]{1,0:T(8,128)S(1)}) custom-call(s32[32]{0:T(128)} %bitcast.7, bf16[32,2,2,128,128]{4,3,2,1,0:T(8,128)(2,1)} %bitcast.6, s32[4,4096]{1,0:T(4,128)} %refs_7_.1), custom_call_target="tpu_custom_call" | custom-call | tf_op jit(solution)/shard_map/prepare/pallas_call | solution.py:148
  6.8 5.2 %sweep.2 = (f32[88,256]{1,0:T(8,128)S(1)}, f32[88,256]{1,0:T(8,128)S(1)}, f32[128,512]{1,0:T(8,128)S(1)}, bf16[192,8192]{1,0:T(8,128)(2,1)S(1)}, bf16[512,8192]{1,0:T(8,128)(2,1)S(1)}) custom-call(f32[2,16,4,256]{3,2,1,0:T(4,128)S(1)} %copy-done.2, f32[2,16,4,256]{3,2,1,0:T(4,128)S(1)} %collective-permute-done.refs_1_, s32[2,4096]{1,0:T(2,128)S(1)} %copy-done.3, ...), custom_call_target="tpu_custom_call" | custom-call | tf_op jit(solution)/shard_map/sweep/pallas_call | solution.py:371
  12.0 0.1 collective-permute-start.1
  12.1 1.3 %collective-permute-done.1 = f32[88,256]{1,0:T(8,128)S(1)} collective-permute-done((f32[88,256]{1,0:T(8,128)S(1)}, f32[88,256]{1,0:T(8,128)S(1)}, u32[]{:S(2)}, u32[]{:S(2)}) %collective-permute-start.1) | collective-permute-done | bytes 90144 | tf_op jit(solution)/shard_map/ppermute | solution.py:432
  13.3 1.8 %collective-permute-start.2 = (f32[88,256]{1,0:T(8,128)S(1)}, f32[88,256]{1,0:T(8,128)S(1)}, u32[]{:S(2)}, u32[]{:S(2)}) collective-permute-start(f32[88,256]{1,0:T(8,128)S(1)} %add.42), channel_id=1, source_target_pairs={{1,0},{0,1},{3,2},{2,3},{5,4},{4,5},{7,6},{6,7},{9,8},{8,9},{11,10... | collective-permute-start | bytes 270344 | tf_op jit(solution)/shard_map/ppermute | solution.py:437
  15.2 1.9 %own_moments.2 = (f32[88,256]{1,0:T(8,128)S(1)}, f32[88,256]{1,0:T(8,128)S(1)}) custom-call(bf16[512,8192]{1,0:T(8,128)(2,1)S(1)} %get-tuple-element.33.picks_ref.refs_4_, bf16[192,8192]{1,0:T(8,128)(2,1)S(1)} %get-tuple-element.37.terms_ref, f32[128,512]{1,0:T(8,128)S(1)} %get-tuple-element.31.current_ref.refs_0_, ...), custom_call_target="tpu_custom_call" | custom-call | flops 805306368 | bytes 7340032 | tf_op jit(solution)/shard_map/own_moments/pallas_call | solution.py:344
  17.0 0.1 collective-permute-start.3
  17.1 1.0 %collective-permute-done.2 = f32[88,256]{1,0:T(8,128)S(1)} collective-permute-done((f32[88,256]{1,0:T(8,128)S(1)}, f32[88,256]{1,0:T(8,128)S(1)}, u32[]{:S(2)}, u32[]{:S(2)}) %collective-permute-start.2) | collective-permute-done | bytes 90144 | tf_op jit(solution)/shard_map/ppermute | solution.py:437
  18.1 0.3 collective-permute-done.3
  18.4 3.7 %collective-permute-start.6 = (f32[88,256]{1,0:T(8,128)S(1)}, f32[88,256]{1,0:T(8,128)S(1)}, u32[]{:S(2)}, u32[]{:S(2)}) collective-permute-start(f32[88,256]{1,0:T(8,128)S(1)} %add.44), channel_id=1, source_target_pairs={{0,12},{2,14},{4,8},{6,10},{8,4},{10,6},{12,0},{14,2},{1,13},{3,15... | collective-permute-start | bytes 270344 | tf_op jit(solution)/shard_map/ppermute | solution.py:443
  22.1 0.8 %collective-permute-start.4 = (f32[88,256]{1,0:T(8,128)S(1)}, f32[88,256]{1,0:T(8,128)S(1)}, u32[]{:S(2)}, u32[]{:S(2)}) collective-permute-start(f32[88,256]{1,0:T(8,128)S(1)} %add.44), channel_id=1, source_target_pairs={{0,4},{2,6},{4,0},{6,2},{8,12},{10,14},{12,8},{14,10},{1,5},{3,7},... | collective-permute-start | bytes 270344 | tf_op jit(solution)/shard_map/ppermute | solution.py:443
  22.9 2.9 %collective-permute-done.6 = f32[88,256]{1,0:T(8,128)S(1)} collective-permute-done((f32[88,256]{1,0:T(8,128)S(1)}, f32[88,256]{1,0:T(8,128)S(1)}, u32[]{:S(2)}, u32[]{:S(2)}) %collective-permute-start.6) | collective-permute-done | bytes 90144 | tf_op jit(solution)/shard_map/ppermute | solution.py:443
  25.7 4.2 %collective-permute-done.5 = f32[88,256]{1,0:T(8,128)S(1)} collective-permute-done((f32[88,256]{1,0:T(8,128)S(1)}, f32[88,256]{1,0:T(8,128)S(1)}, u32[]{:S(2)}, u32[]{:S(2)}) %collective-permute-start.5) | collective-permute-done | bytes 90144 | tf_op jit(solution)/shard_map/ppermute | solution.py:443
  30.1 0.7 %collective-permute-start.7 = (f32[48,256]{1,0:T(8,128)S(1)}, f32[48,256]{1,0:T(8,128)S(1)}, u32[]{:S(2)}, u32[]{:S(2)}) collective-permute-start(f32[48,256]{1,0:T(8,128)S(1)} %constant_dynamic-update-slice_fusion), channel_id=1, source_target_pairs={{1,0},{0,1},{3,2},{2,3},{5,4},{4,5},{7,6},{6,7},{9,8},{8,9},{11,10... | collective-permute-start | bytes 147464 | tf_op jit(solution)/shard_map/ppermute | solution.py:437
  30.9 3.4 %collective-permute-done.7 = f32[48,256]{1,0:T(8,128)S(1)} collective-permute-done((f32[48,256]{1,0:T(8,128)S(1)}, f32[48,256]{1,0:T(8,128)S(1)}, u32[]{:S(2)}, u32[]{:S(2)}) %collective-permute-start.7) | collective-permute-done | bytes 49184 | tf_op jit(solution)/shard_map/ppermute | solution.py:437
  34.3 0.1 collective-permute-start.8
  34.4 1.3 %collective-permute-done.8.refs_3_ = f32[48,512]{1,0:T(8,128)S(1)} collective-permute-done((f32[48,512]{1,0:T(8,128)S(1)}, f32[48,512]{1,0:T(8,128)S(1)}, u32[]{:S(2)}, u32[]{:S(2)}) %collective-permute-start.8) | collective-permute-done | bytes 98336 | tf_op jit(solution)/shard_map/ppermute | solution.py:432
  35.7 4.8 %sweep.3 = (f32[88,256]{1,0:T(8,128)S(1)}, f32[88,256]{1,0:T(8,128)S(1)}, f32[128,512]{1,0:T(8,128)S(1)}, bf16[192,8192]{1,0:T(8,128)(2,1)S(1)}) custom-call(f32[128,512]{1,0:T(8,128)S(1)} %get-tuple-element.31.current_ref.refs_0_, f32[128,96]{1,0:T(8,128)S(1)} %get-tuple-element.32.refs_1_.fit_ref, f32[48,512]{1,0:T(8,128)S(1)} %pad_maximum_fusion.refs_2_, ...), custom_call_target="tpu_custom_call" | custom-call | tf_op jit(solution)/shard_map/sweep/pallas_call | solution.py:371
  40.5 0.2 collective-permute-start.9
  40.7 1.1 %collective-permute-done.9 = f32[88,256]{1,0:T(8,128)S(1)} collective-permute-done((f32[88,256]{1,0:T(8,128)S(1)}, f32[88,256]{1,0:T(8,128)S(1)}, u32[]{:S(2)}, u32[]{:S(2)}) %collective-permute-start.9) | collective-permute-done | bytes 90144 | tf_op jit(solution)/shard_map/ppermute | solution.py:432
  41.9 0.7 %collective-permute-start.10 = (f32[88,256]{1,0:T(8,128)S(1)}, f32[88,256]{1,0:T(8,128)S(1)}, u32[]{:S(2)}, u32[]{:S(2)}) collective-permute-start(f32[88,256]{1,0:T(8,128)S(1)} %add.49), channel_id=1, source_target_pairs={{1,0},{0,1},{3,2},{2,3},{5,4},{4,5},{7,6},{6,7},{9,8},{8,9},{11,10... | collective-permute-start | bytes 270344 | tf_op jit(solution)/shard_map/ppermute | solution.py:437
  42.6 1.9 %own_moments.3 = (f32[88,256]{1,0:T(8,128)S(1)}, f32[88,256]{1,0:T(8,128)S(1)}) custom-call(bf16[512,8192]{1,0:T(8,128)(2,1)S(1)} %get-tuple-element.33.picks_ref.refs_4_, bf16[192,8192]{1,0:T(8,128)(2,1)S(1)} %get-tuple-element.45.terms_ref, f32[128,512]{1,0:T(8,128)S(1)} %get-tuple-element.41.current_ref.before_ref, ...), custom_call_target="tpu_custom_call" | custom-call | flops 805306368 | bytes 7340032 | tf_op jit(solution)/shard_map/own_moments/pallas_call | solution.py:344
  44.5 0.1 collective-permute-start.11
  44.5 2.1 %collective-permute-done.10 = f32[88,256]{1,0:T(8,128)S(1)} collective-permute-done((f32[88,256]{1,0:T(8,128)S(1)}, f32[88,256]{1,0:T(8,128)S(1)}, u32[]{:S(2)}, u32[]{:S(2)}) %collective-permute-start.10) | collective-permute-done | bytes 90144 | tf_op jit(solution)/shard_map/ppermute | solution.py:437
  46.7 2.5 %collective-permute-start.14 = (f32[88,256]{1,0:T(8,128)S(1)}, f32[88,256]{1,0:T(8,128)S(1)}, u32[]{:S(2)}, u32[]{:S(2)}) collective-permute-start(f32[88,256]{1,0:T(8,128)S(1)} %add.51), channel_id=1, source_target_pairs={{0,12},{2,14},{4,8},{6,10},{8,4},{10,6},{12,0},{14,2},{1,13},{3,15... | collective-permute-start | bytes 270344 | tf_op jit(solution)/shard_map/ppermute | solution.py:443
  49.2 1.9 %collective-permute-start.12 = (f32[88,256]{1,0:T(8,128)S(1)}, f32[88,256]{1,0:T(8,128)S(1)}, u32[]{:S(2)}, u32[]{:S(2)}) collective-permute-start(f32[88,256]{1,0:T(8,128)S(1)} %add.51), channel_id=1, source_target_pairs={{0,4},{2,6},{4,0},{6,2},{8,12},{10,14},{12,8},{14,10},{1,5},{3,7},... | collective-permute-start | bytes 270344 | tf_op jit(solution)/shard_map/ppermute | solution.py:443
  51.1 2.6 %collective-permute-done.14 = f32[88,256]{1,0:T(8,128)S(1)} collective-permute-done((f32[88,256]{1,0:T(8,128)S(1)}, f32[88,256]{1,0:T(8,128)S(1)}, u32[]{:S(2)}, u32[]{:S(2)}) %collective-permute-start.14) | collective-permute-done | bytes 90144 | tf_op jit(solution)/shard_map/ppermute | solution.py:443
  53.8 3.4 %collective-permute-done.13 = f32[88,256]{1,0:T(8,128)S(1)} collective-permute-done((f32[88,256]{1,0:T(8,128)S(1)}, f32[88,256]{1,0:T(8,128)S(1)}, u32[]{:S(2)}, u32[]{:S(2)}) %collective-permute-start.13) | collective-permute-done | bytes 90144 | tf_op jit(solution)/shard_map/ppermute | solution.py:443
  57.4 0.1 collective-permute-start.15
  57.5 1.2 %collective-permute-done.15.other_ref = f32[48,256]{1,0:T(8,128)S(1)} collective-permute-done((f32[48,256]{1,0:T(8,128)S(1)}, f32[48,256]{1,0:T(8,128)S(1)}, u32[]{:S(2)}, u32[]{:S(2)}) %collective-permute-start.15) | collective-permute-done | bytes 49184 | tf_op jit(solution)/shard_map/ppermute | solution.py:432
  58.7 0.9 %finish.1 = f32[2,16,4,256]{3,2,1,0:T(4,128)} custom-call(f32[128,512]{1,0:T(8,128)S(1)} %get-tuple-element.41.current_ref.before_ref, f32[128,96]{1,0:T(8,128)S(1)} %get-tuple-element.32.refs_1_.fit_ref, f32[48,256]{1,0:T(8,128)S(1)} %constant_dynamic-update-slice_fusion.6.own_ref, f32[48,256]{1,0:T(8,128)S(1)} %collective-permute-done.15.other_ref), custom_call_target="tpu_custom_call" | custom-call | tf_op jit(solution)/shard_map/finish/pallas_call | solution.py:398
  (35 shorter events, 0.5 us)
Async XLA Ops:
  0.0 6.7 %copy-start.2 = (f32[2,16,4,256]{3,2,1,0:T(4,128)S(1)}, f32[2,16,4,256]{3,2,1,0:T(4,128)}, u32[]{:S(2)}) copy-start(f32[2,16,4,256]{3,2,1,0:T(4,128)} %refs_0_.1) | copy-start | bytes 393220
  0.0 6.7 %copy-start.1 = (s32[4,4096]{1,0:T(4,128)S(1)}, s32[4,4096]{1,0:T(4,128)}, u32[]{:S(2)}) copy-start(s32[4,4096]{1,0:T(4,128)} %refs_7_.1) | copy-start | bytes 196612
  0.0 6.7 %copy-start = (f32[2,2,4,4096]{3,2,1,0:T(4,128)S(1)}, f32[2,2,4,4096]{3,2,1,0:T(4,128)}, u32[]{:S(2)}) copy-start(f32[2,2,4,4096]{3,2,1,0:T(4,128)} %refs_8_.1) | copy-start | bytes 786436
  0.0 6.7 %copy-start.3 = (s32[2,4096]{1,0:T(2,128)S(1)}, s32[2,4096]{1,0:T(2,128)}, u32[]{:S(2)}) copy-start(s32[2,4096]{1,0:T(2,128)} %refs_2_.1) | copy-start | bytes 98308
  0.0 6.7 %collective-permute-start = (f32[2,16,4,256]{3,2,1,0:T(4,128)}, f32[2,16,4,256]{3,2,1,0:T(4,128)S(1)}, u32[]{:S(2)}, u32[]{:S(2)}) collective-permute-start(f32[2,16,4,256]{3,2,1,0:T(4,128)} %refs_0_.1), channel_id=1, source_target_pairs={{1,0},{0,1},{3,2},{2,3},{5,4},{4,5},{7,6},{6,7},{9,8},{8,9},{11,10... | collective-permute-start | bytes 393224 | tf_op jit(solution)/shard_map/ppermute | solution.py:437
  12.0 1.4 %collective-permute-start.1 = (f32[88,256]{1,0:T(8,128)S(1)}, f32[88,256]{1,0:T(8,128)S(1)}, u32[]{:S(2)}, u32[]{:S(2)}) collective-permute-start(f32[88,256]{1,0:T(8,128)S(1)} %get-tuple-element.35), channel_id=1, source_target_pairs={{0,2},{2,0},{4,6},{6,4},{8,10},{10,8},{12,14},{14,12},{1,3},{3,1},... | collective-permute-start | bytes 270344 | tf_op jit(solution)/shard_map/ppermute | solution.py:432
  13.3 4.7 %collective-permute-start.2 = (f32[88,256]{1,0:T(8,128)S(1)}, f32[88,256]{1,0:T(8,128)S(1)}, u32[]{:S(2)}, u32[]{:S(2)}) collective-permute-start(f32[88,256]{1,0:T(8,128)S(1)} %add.42), channel_id=1, source_target_pairs={{1,0},{0,1},{3,2},{2,3},{5,4},{4,5},{7,6},{6,7},{9,8},{8,9},{11,10... | collective-permute-start | bytes 270344 | tf_op jit(solution)/shard_map/ppermute | solution.py:437
  17.0 1.4 %collective-permute-start.3 = (f32[88,256]{1,0:T(8,128)S(1)}, f32[88,256]{1,0:T(8,128)S(1)}, u32[]{:S(2)}, u32[]{:S(2)}) collective-permute-start(f32[88,256]{1,0:T(8,128)S(1)} %get-tuple-element.40), channel_id=1, source_target_pairs={{0,2},{2,0},{4,6},{6,4},{8,10},{10,8},{12,14},{14,12},{1,3},{3,1},... | collective-permute-start | bytes 270344 | tf_op jit(solution)/shard_map/ppermute | solution.py:432
  18.4 7.3 %collective-permute-start.6 = (f32[88,256]{1,0:T(8,128)S(1)}, f32[88,256]{1,0:T(8,128)S(1)}, u32[]{:S(2)}, u32[]{:S(2)}) collective-permute-start(f32[88,256]{1,0:T(8,128)S(1)} %add.44), channel_id=1, source_target_pairs={{0,12},{2,14},{4,8},{6,10},{8,4},{10,6},{12,0},{14,2},{1,13},{3,15... | collective-permute-start | bytes 270344 | tf_op jit(solution)/shard_map/ppermute | solution.py:443
  22.1 7.9 %collective-permute-start.5 = (f32[88,256]{1,0:T(8,128)S(1)}, f32[88,256]{1,0:T(8,128)S(1)}, u32[]{:S(2)}, u32[]{:S(2)}) collective-permute-start(f32[88,256]{1,0:T(8,128)S(1)} %add.44), channel_id=1, source_target_pairs={{0,8},{2,10},{4,12},{6,14},{8,0},{10,2},{12,4},{14,6},{1,9},{3,11}... | collective-permute-start | bytes 270344 | tf_op jit(solution)/shard_map/ppermute | solution.py:443
  22.1 7.9 %collective-permute-start.4 = (f32[88,256]{1,0:T(8,128)S(1)}, f32[88,256]{1,0:T(8,128)S(1)}, u32[]{:S(2)}, u32[]{:S(2)}) collective-permute-start(f32[88,256]{1,0:T(8,128)S(1)} %add.44), channel_id=1, source_target_pairs={{0,4},{2,6},{4,0},{6,2},{8,12},{10,14},{12,8},{14,10},{1,5},{3,7},... | collective-permute-start | bytes 270344 | tf_op jit(solution)/shard_map/ppermute | solution.py:443
  30.1 4.2 %collective-permute-start.7 = (f32[48,256]{1,0:T(8,128)S(1)}, f32[48,256]{1,0:T(8,128)S(1)}, u32[]{:S(2)}, u32[]{:S(2)}) collective-permute-start(f32[48,256]{1,0:T(8,128)S(1)} %constant_dynamic-update-slice_fusion), channel_id=1, source_target_pairs={{1,0},{0,1},{3,2},{2,3},{5,4},{4,5},{7,6},{6,7},{9,8},{8,9},{11,10... | collective-permute-start | bytes 147464 | tf_op jit(solution)/shard_map/ppermute | solution.py:437
  34.3 1.4 %collective-permute-start.8 = (f32[48,512]{1,0:T(8,128)S(1)}, f32[48,512]{1,0:T(8,128)S(1)}, u32[]{:S(2)}, u32[]{:S(2)}) collective-permute-start(f32[48,512]{1,0:T(8,128)S(1)} %pad_maximum_fusion.refs_2_), channel_id=1, source_target_pairs={{0,2},{2,0},{4,6},{6,4},{8,10},{10,8},{12,14},{14,12},{1,3},{3,1},... | collective-permute-start | bytes 294920 | tf_op jit(solution)/shard_map/ppermute | solution.py:432
  40.5 1.4 %collective-permute-start.9 = (f32[88,256]{1,0:T(8,128)S(1)}, f32[88,256]{1,0:T(8,128)S(1)}, u32[]{:S(2)}, u32[]{:S(2)}) collective-permute-start(f32[88,256]{1,0:T(8,128)S(1)} %get-tuple-element.43), channel_id=1, source_target_pairs={{0,2},{2,0},{4,6},{6,4},{8,10},{10,8},{12,14},{14,12},{1,3},{3,1},... | collective-permute-start | bytes 270344 | tf_op jit(solution)/shard_map/ppermute | solution.py:432
  41.9 4.7 %collective-permute-start.10 = (f32[88,256]{1,0:T(8,128)S(1)}, f32[88,256]{1,0:T(8,128)S(1)}, u32[]{:S(2)}, u32[]{:S(2)}) collective-permute-start(f32[88,256]{1,0:T(8,128)S(1)} %add.49), channel_id=1, source_target_pairs={{1,0},{0,1},{3,2},{2,3},{5,4},{4,5},{7,6},{6,7},{9,8},{8,9},{11,10... | collective-permute-start | bytes 270344 | tf_op jit(solution)/shard_map/ppermute | solution.py:437
  44.5 2.2 %collective-permute-start.11 = (f32[88,256]{1,0:T(8,128)S(1)}, f32[88,256]{1,0:T(8,128)S(1)}, u32[]{:S(2)}, u32[]{:S(2)}) collective-permute-start(f32[88,256]{1,0:T(8,128)S(1)} %get-tuple-element.48), channel_id=1, source_target_pairs={{0,2},{2,0},{4,6},{6,4},{8,10},{10,8},{12,14},{14,12},{1,3},{3,1},... | collective-permute-start | bytes 270344 | tf_op jit(solution)/shard_map/ppermute | solution.py:432
  46.7 7.1 %collective-permute-start.14 = (f32[88,256]{1,0:T(8,128)S(1)}, f32[88,256]{1,0:T(8,128)S(1)}, u32[]{:S(2)}, u32[]{:S(2)}) collective-permute-start(f32[88,256]{1,0:T(8,128)S(1)} %add.51), channel_id=1, source_target_pairs={{0,12},{2,14},{4,8},{6,10},{8,4},{10,6},{12,0},{14,2},{1,13},{3,15... | collective-permute-start | bytes 270344 | tf_op jit(solution)/shard_map/ppermute | solution.py:443
  49.2 8.0 %collective-permute-start.13 = (f32[88,256]{1,0:T(8,128)S(1)}, f32[88,256]{1,0:T(8,128)S(1)}, u32[]{:S(2)}, u32[]{:S(2)}) collective-permute-start(f32[88,256]{1,0:T(8,128)S(1)} %add.51), channel_id=1, source_target_pairs={{0,8},{2,10},{4,12},{6,14},{8,0},{10,2},{12,4},{14,6},{1,9},{3,11}... | collective-permute-start | bytes 270344 | tf_op jit(solution)/shard_map/ppermute | solution.py:443
  49.2 8.0 %collective-permute-start.12 = (f32[88,256]{1,0:T(8,128)S(1)}, f32[88,256]{1,0:T(8,128)S(1)}, u32[]{:S(2)}, u32[]{:S(2)}) collective-permute-start(f32[88,256]{1,0:T(8,128)S(1)} %add.51), channel_id=1, source_target_pairs={{0,4},{2,6},{4,0},{6,2},{8,12},{10,14},{12,8},{14,10},{1,5},{3,7},... | collective-permute-start | bytes 270344 | tf_op jit(solution)/shard_map/ppermute | solution.py:443
  57.4 1.3 %collective-permute-start.15 = (f32[48,256]{1,0:T(8,128)S(1)}, f32[48,256]{1,0:T(8,128)S(1)}, u32[]{:S(2)}, u32[]{:S(2)}) collective-permute-start(f32[48,256]{1,0:T(8,128)S(1)} %constant_dynamic-update-slice_fusion.6.own_ref), channel_id=1, source_target_pairs={{0,2},{2,0},{4,6},{6,4},{8,10},{10,8},{12,14},{14,12},{1,3},{3,1},... | collective-permute-start | bytes 147464 | tf_op jit(solution)/shard_map/ppermute | solution.py:432

commit v4 on v3

--- a/solution.py
+++ b/solution.py
@@ -432,9 +432,14 @@
     return lax.ppermute(value, "chan", [(j, j ^ 1) for j in range(count)])
 
 
-def from_later(value, k):
+def from_later(value, k, cross=False):
     count = lax.axis_size("bl")
-    return lax.ppermute(value, "bl", [((j + k) % count, j) for j in range(count)])
+    if not cross:
+        return lax.ppermute(value, "bl", [((j + k) % count, j) for j in range(count)])
+    pairs = [
+        ((c ^ 1) * count + (j + k) % count, c * count + j) for c in range(lax.axis_size("chan")) for j in range(count)
+    ]
+    return lax.ppermute(value, ("chan", "bl"), pairs)
 
 
 def over_chips(value):
@@ -442,7 +447,8 @@
     chips = count // 2
     swap = lambda v, k: lax.ppermute(v, "chan", [(j, j ^ (2 * k)) for j in range(count)])
     if chips <= 4:
-        parts = [swap(value, k) for k in range(1, chips)]
+        order = (1, 3, 2) if chips == 4 else range(1, chips)
+        parts = [swap(value, k) for k in order]
         for part in parts:
             value = value + part
         return value
@@ -478,8 +484,12 @@
         kept = lax.optimization_barrier(kept) + other_core(other)
         coefs = solve(over_chips(kept))
         if number < ITERS - 1:
-            coefs = jnp.concatenate([coefs] + [from_later(coefs, k) for k in range(1, blocks)], axis=1)
-        inputs = [current, fit, coefs, other_core(coefs), picks]
+            across = [from_later(coefs, k, True) for k in range(1, blocks)]
+            along = [from_later(coefs, k) for k in range(1, blocks)]
+            beside = other_core(coefs)
+            inputs = [current, fit, jnp.concatenate([coefs] + along, axis=1), jnp.concatenate([beside] + across, axis=1), picks]
+        else:
+            inputs = [current, fit, coefs, other_core(coefs), picks]
     return finish(*inputs[:4], channels)
 
 

time: 59.7 us -> 59 us (0.988)
  waiting for transfers between devices: 24.9 us -> 22.8 us
  starting transfers between devices: 15.7 us -> 17.1 us
    ppermute x6, starting transfers between devices: 0.57 us -> 2.18 us  [other_core(): return lax.ppermute(value, 'chan', [(j, j ^ 1) for j in range(count)])]
    ppermute x6, waiting for transfers between devices: 5.2 us -> 3.75 us  [other_core(): return lax.ppermute(value, 'chan', [(j, j ^ 1) for j in range(count)])]
    ppermute x4, waiting for transfers between devices: 6.55 us -> 5.22 us  [from_later(): lax.ppermute(value, 'bl', [((j + k) % count, j) for j in range(count)])]
    ppermute x6, waiting for transfers between devices: 13.2 us -> 13.8 us  [over_chips(): lax.ppermute(v, 'chan', [(j, j ^ 2 * k) for j in range(count)])]
    ppermute x6, starting transfers between devices: 8.91 us -> 8.24 us  [over_chips(): lax.ppermute(v, 'chan', [(j, j ^ 2 * k) for j in range(count)])]
  transfers between devices with their start and end apart: 16 -> 17, of which waited for: 13 -> 13; matrix products, arithmetic and copies ran while one was open for 0% -> 0% of each run, Pallas kernels for 12% -> 13%
where the time goes in v4:
time: 59 us; the launch traced here: 58.8 us
  waiting for transfers between devices  22.8 us (39%)
  Pallas kernels  18.3 us (31%)
  starting transfers between devices  17.1 us (29%)
    ppermute x6, waiting for transfers between devices, over_chips(): lax.ppermute(v, 'chan', [(j, j ^ 2 * k) for j in range(count)])  13.8 us
    pallas_call x2, Pallas kernels, sweep(): pl.pallas_call(partial(sweep_kernel, first, blocks, owned, SWEEP_TILE), i...  10.1 us
    ppermute x6, starting transfers between devices, over_chips(): lax.ppermute(v, 'chan', [(j, j ^ 2 * k) for j in range(count)])  8.24 us
    ppermute x4, starting transfers between devices, from_later(): lax.ppermute(value, 'bl', [((j + k) % count, j) for j in range(count)])  6.49 us
    ppermute x4, waiting for transfers between devices, from_later(): lax.ppermute(value, 'bl', [((j + k) % count, j) for j in range(count)])  5.22 us
    ppermute x6, waiting for transfers between devices, other_core(): return lax.ppermute(value, 'chan', [(j, j ^ 1) for j in range(count)])  3.75 us
    pallas_call x2, Pallas kernels, own_moments(): pl.pallas_call(partial(own_kernel, blocks, OWN_CHUNK), in_specs=[vmem] *...  3.74 us
    pallas_call x1, Pallas kernels, prepare(): pl.pallas_call(partial(prep_kernel, total, channels, chunk), in_specs=[pl...  3.64 us
  transfers between devices with their start and end apart: 17, of which 13 were waited for; matrix products, arithmetic and copies ran while one was open for 0% of the time, Pallas kernels for 13%

profile of v4, /device:TPU:0, one launch (start us, length us, event | category | flops | bytes accessed | tf_op | source)
XLA Modules:
  0.0 58.8 jit_solution(2958220527365747448)
XLA Ops:
  0.0 3.0 %collective-permute-start = (f32[2,16,4,256]{3,2,1,0:T(4,128)}, f32[2,16,4,256]{3,2,1,0:T(4,128)S(1)}, u32[]{:S(2)}, u32[]{:S(2)}) collective-permute-start(f32[2,16,4,256]{3,2,1,0:T(4,128)} %refs_0_.1), channel_id=1, source_target_pairs={{1,0},{0,1},{3,2},{2,3},{5,4},{4,5},{7,6},{6,7},{9,8},{8,9},{11,10... | collective-permute-start | bytes 393224 | tf_op jit(solution)/shard_map/ppermute | solution.py:438
  3.0 3.6 %prepare.1 = (f32[2,2,64,4096]{3,2,1,0:T(8,128)S(1)}, f32[64,4096]{1,0:T(8,128)S(1)}, f32[80,64]{1,0:T(8,128)S(1)}, f32[48,64]{1,0:T(8,128)S(1)}, f32[128,96]{1,0:T(8,128)S(1)}) custom-call(s32[32]{0:T(128)} %bitcast.7, bf16[32,2,2,128,128]{4,3,2,1,0:T(8,128)(2,1)} %bitcast.6, s32[4,4096]{1,0:T(4,128)} %refs_7_.1), custom_call_target="tpu_custom_call" | custom-call | tf_op jit(solution)/shard_map/prepare/pallas_call | solution.py:148
  6.8 5.2 %sweep.2 = (f32[88,256]{1,0:T(8,128)S(1)}, f32[88,256]{1,0:T(8,128)S(1)}, f32[128,512]{1,0:T(8,128)S(1)}, bf16[192,8192]{1,0:T(8,128)(2,1)S(1)}, bf16[512,8192]{1,0:T(8,128)(2,1)S(1)}) custom-call(f32[2,16,4,256]{3,2,1,0:T(4,128)S(1)} %copy-done.2, f32[2,16,4,256]{3,2,1,0:T(4,128)S(1)} %collective-permute-done.refs_1_, s32[2,4096]{1,0:T(2,128)S(1)} %copy-done.3, ...), custom_call_target="tpu_custom_call" | custom-call | tf_op jit(solution)/shard_map/sweep/pallas_call | solution.py:371
  12.0 0.1 collective-permute-start.1
  12.1 1.3 %collective-permute-done.1 = f32[88,256]{1,0:T(8,128)S(1)} collective-permute-done((f32[88,256]{1,0:T(8,128)S(1)}, f32[88,256]{1,0:T(8,128)S(1)}, u32[]{:S(2)}, u32[]{:S(2)}) %collective-permute-start.1) | collective-permute-done | bytes 90144 | tf_op jit(solution)/shard_map/ppermute | solution.py:432
  13.3 1.8 %collective-permute-start.2 = (f32[88,256]{1,0:T(8,128)S(1)}, f32[88,256]{1,0:T(8,128)S(1)}, u32[]{:S(2)}, u32[]{:S(2)}) collective-permute-start(f32[88,256]{1,0:T(8,128)S(1)} %add.42), channel_id=1, source_target_pairs={{1,0},{0,1},{3,2},{2,3},{5,4},{4,5},{7,6},{6,7},{9,8},{8,9},{11,10... | collective-permute-start | bytes 270344 | tf_op jit(solution)/shard_map/ppermute | solution.py:438
  15.2 1.9 %own_moments.2 = (f32[88,256]{1,0:T(8,128)S(1)}, f32[88,256]{1,0:T(8,128)S(1)}) custom-call(bf16[512,8192]{1,0:T(8,128)(2,1)S(1)} %get-tuple-element.33.picks_ref.refs_4_, bf16[192,8192]{1,0:T(8,128)(2,1)S(1)} %get-tuple-element.37.terms_ref, f32[128,512]{1,0:T(8,128)S(1)} %get-tuple-element.31.current_ref.refs_0_, ...), custom_call_target="tpu_custom_call" | custom-call | flops 805306368 | bytes 7340032 | tf_op jit(solution)/shard_map/own_moments/pallas_call | solution.py:344
  17.1 1.0 %collective-permute-done.2 = f32[88,256]{1,0:T(8,128)S(1)} collective-permute-done((f32[88,256]{1,0:T(8,128)S(1)}, f32[88,256]{1,0:T(8,128)S(1)}, u32[]{:S(2)}, u32[]{:S(2)}) %collective-permute-start.2) | collective-permute-done | bytes 90144 | tf_op jit(solution)/shard_map/ppermute | solution.py:438
  18.1 0.3 collective-permute-done.3
  18.4 2.7 %collective-permute-start.6 = (f32[88,256]{1,0:T(8,128)S(1)}, f32[88,256]{1,0:T(8,128)S(1)}, u32[]{:S(2)}, u32[]{:S(2)}) collective-permute-start(f32[88,256]{1,0:T(8,128)S(1)} %add.44), channel_id=1, source_target_pairs={{0,8},{2,10},{4,12},{6,14},{8,0},{10,2},{12,4},{14,6},{1,9},{3,11}... | collective-permute-start | bytes 270344 | tf_op jit(solution)/shard_map/ppermute | solution.py:448
  21.1 1.3 %collective-permute-start.5 = (f32[88,256]{1,0:T(8,128)S(1)}, f32[88,256]{1,0:T(8,128)S(1)}, u32[]{:S(2)}, u32[]{:S(2)}) collective-permute-start(f32[88,256]{1,0:T(8,128)S(1)} %add.44), channel_id=1, source_target_pairs={{0,12},{2,14},{4,8},{6,10},{8,4},{10,6},{12,0},{14,2},{1,13},{3,15... | collective-permute-start | bytes 270344 | tf_op jit(solution)/shard_map/ppermute | solution.py:448
  22.4 0.2 collective-permute-start.4
  22.6 6.1 %collective-permute-done.6 = f32[88,256]{1,0:T(8,128)S(1)} collective-permute-done((f32[88,256]{1,0:T(8,128)S(1)}, f32[88,256]{1,0:T(8,128)S(1)}, u32[]{:S(2)}, u32[]{:S(2)}) %collective-permute-start.6) | collective-permute-done | bytes 90144 | tf_op jit(solution)/shard_map/ppermute | solution.py:448
  28.7 0.6 %collective-permute-done.4 = f32[88,256]{1,0:T(8,128)S(1)} collective-permute-done((f32[88,256]{1,0:T(8,128)S(1)}, f32[88,256]{1,0:T(8,128)S(1)}, u32[]{:S(2)}, u32[]{:S(2)}) %collective-permute-start.4) | collective-permute-done | bytes 90144 | tf_op jit(solution)/shard_map/ppermute | solution.py:448
  29.5 0.5 collective-permute-start.7
  30.0 0.2 collective-permute-start.9
  30.2 1.5 %collective-permute-start.8 = (f32[48,256]{1,0:T(8,128)S(1)}, f32[48,256]{1,0:T(8,128)S(1)}, u32[]{:S(2)}, u32[]{:S(2)}) collective-permute-start(f32[48,256]{1,0:T(8,128)S(1)} %constant_dynamic-update-slice_fusion), channel_id=1, source_target_pairs={{0,2},{2,0},{4,6},{6,4},{8,10},{10,8},{12,14},{14,12},{1,3},{3,1},... | collective-permute-start | bytes 147464 | tf_op jit(solution)/shard_map/ppermute | solution.py:432
  31.7 2.4 %collective-permute-done.7 = f32[48,256]{1,0:T(8,128)S(1)} collective-permute-done((f32[48,256]{1,0:T(8,128)S(1)}, f32[48,256]{1,0:T(8,128)S(1)}, u32[]{:S(2)}, u32[]{:S(2)}) %collective-permute-start.7) | collective-permute-done | bytes 49184 | tf_op jit(solution)/shard_map/ppermute | solution.py:438
  34.1 4.8 %sweep.3 = (f32[88,256]{1,0:T(8,128)S(1)}, f32[88,256]{1,0:T(8,128)S(1)}, f32[128,512]{1,0:T(8,128)S(1)}, bf16[192,8192]{1,0:T(8,128)(2,1)S(1)}) custom-call(f32[128,512]{1,0:T(8,128)S(1)} %get-tuple-element.31.current_ref.refs_0_, f32[128,96]{1,0:T(8,128)S(1)} %get-tuple-element.32.refs_1_.fit_ref, f32[48,512]{1,0:T(8,128)S(1)} %pad_maximum_fusion.refs_2_, ...), custom_call_target="tpu_custom_call" | custom-call | tf_op jit(solution)/shard_map/sweep/pallas_call | solution.py:371
  38.9 0.4 collective-permute-start.10
  39.3 1.0 %collective-permute-done.10 = f32[88,256]{1,0:T(8,128)S(1)} collective-permute-done((f32[88,256]{1,0:T(8,128)S(1)}, f32[88,256]{1,0:T(8,128)S(1)}, u32[]{:S(2)}, u32[]{:S(2)}) %collective-permute-start.10) | collective-permute-done | bytes 90144 | tf_op jit(solution)/shard_map/ppermute | solution.py:432
  40.3 1.1 %collective-permute-start.11 = (f32[88,256]{1,0:T(8,128)S(1)}, f32[88,256]{1,0:T(8,128)S(1)}, u32[]{:S(2)}, u32[]{:S(2)}) collective-permute-start(f32[88,256]{1,0:T(8,128)S(1)} %add.49), channel_id=1, source_target_pairs={{1,0},{0,1},{3,2},{2,3},{5,4},{4,5},{7,6},{6,7},{9,8},{8,9},{11,10... | collective-permute-start | bytes 270344 | tf_op jit(solution)/shard_map/ppermute | solution.py:438
  41.4 1.9 %own_moments.3 = (f32[88,256]{1,0:T(8,128)S(1)}, f32[88,256]{1,0:T(8,128)S(1)}) custom-call(bf16[512,8192]{1,0:T(8,128)(2,1)S(1)} %get-tuple-element.33.picks_ref.refs_4_, bf16[192,8192]{1,0:T(8,128)(2,1)S(1)} %get-tuple-element.45.terms_ref, f32[128,512]{1,0:T(8,128)S(1)} %get-tuple-element.41.current_ref.before_ref, ...), custom_call_target="tpu_custom_call" | custom-call | flops 805306368 | bytes 7340032 | tf_op jit(solution)/shard_map/own_moments/pallas_call | solution.py:344
  43.4 1.8 %collective-permute-done.11 = f32[88,256]{1,0:T(8,128)S(1)} collective-permute-done((f32[88,256]{1,0:T(8,128)S(1)}, f32[88,256]{1,0:T(8,128)S(1)}, u32[]{:S(2)}, u32[]{:S(2)}) %collective-permute-start.11) | collective-permute-done | bytes 90144 | tf_op jit(solution)/shard_map/ppermute | solution.py:438
  45.2 3.4 %collective-permute-start.15 = (f32[88,256]{1,0:T(8,128)S(1)}, f32[88,256]{1,0:T(8,128)S(1)}, u32[]{:S(2)}, u32[]{:S(2)}) collective-permute-start(f32[88,256]{1,0:T(8,128)S(1)} %add.51), channel_id=1, source_target_pairs={{0,8},{2,10},{4,12},{6,14},{8,0},{10,2},{12,4},{14,6},{1,9},{3,11}... | collective-permute-start | bytes 270344 | tf_op jit(solution)/shard_map/ppermute | solution.py:448
  48.6 0.4 collective-permute-start.14
  49.1 0.2 collective-permute-start.13
  49.3 5.6 %collective-permute-done.15 = f32[88,256]{1,0:T(8,128)S(1)} collective-permute-done((f32[88,256]{1,0:T(8,128)S(1)}, f32[88,256]{1,0:T(8,128)S(1)}, u32[]{:S(2)}, u32[]{:S(2)}) %collective-permute-start.15) | collective-permute-done | bytes 90144 | tf_op jit(solution)/shard_map/ppermute | solution.py:448
  54.9 0.6 %collective-permute-done.14 = f32[88,256]{1,0:T(8,128)S(1)} collective-permute-done((f32[88,256]{1,0:T(8,128)S(1)}, f32[88,256]{1,0:T(8,128)S(1)}, u32[]{:S(2)}, u32[]{:S(2)}) %collective-permute-start.14) | collective-permute-done | bytes 90144 | tf_op jit(solution)/shard_map/ppermute | solution.py:448
  55.5 0.9 %collective-permute-done.13 = f32[88,256]{1,0:T(8,128)S(1)} collective-permute-done((f32[88,256]{1,0:T(8,128)S(1)}, f32[88,256]{1,0:T(8,128)S(1)}, u32[]{:S(2)}, u32[]{:S(2)}) %collective-permute-start.13) | collective-permute-done | bytes 90144 | tf_op jit(solution)/shard_map/ppermute | solution.py:448
  56.7 1.2 %collective-permute-done.16.other_ref = f32[48,256]{1,0:T(8,128)S(1)} collective-permute-done((f32[48,256]{1,0:T(8,128)S(1)}, f32[48,256]{1,0:T(8,128)S(1)}, u32[]{:S(2)}, u32[]{:S(2)}) %collective-permute-start.16) | collective-permute-done | bytes 49184 | tf_op jit(solution)/shard_map/ppermute | solution.py:432
  57.9 0.9 %finish.1 = f32[2,16,4,256]{3,2,1,0:T(4,128)} custom-call(f32[128,512]{1,0:T(8,128)S(1)} %get-tuple-element.41.current_ref.before_ref, f32[128,96]{1,0:T(8,128)S(1)} %get-tuple-element.32.refs_1_.fit_ref, f32[48,256]{1,0:T(8,128)S(1)} %constant_dynamic-update-slice_fusion.6.own_ref, f32[48,256]{1,0:T(8,128)S(1)} %collective-permute-done.16.other_ref), custom_call_target="tpu_custom_call" | custom-call | tf_op jit(solution)/shard_map/finish/pallas_call | solution.py:398
  (38 shorter events, 0.7 us)
Async XLA Ops:
  0.0 6.7 %copy-start.2 = (f32[2,16,4,256]{3,2,1,0:T(4,128)S(1)}, f32[2,16,4,256]{3,2,1,0:T(4,128)}, u32[]{:S(2)}) copy-start(f32[2,16,4,256]{3,2,1,0:T(4,128)} %refs_0_.1) | copy-start | bytes 393220
  0.0 6.7 %copy-start.1 = (s32[4,4096]{1,0:T(4,128)S(1)}, s32[4,4096]{1,0:T(4,128)}, u32[]{:S(2)}) copy-start(s32[4,4096]{1,0:T(4,128)} %refs_7_.1) | copy-start | bytes 196612
  0.0 6.7 %copy-start = (f32[2,2,4,4096]{3,2,1,0:T(4,128)S(1)}, f32[2,2,4,4096]{3,2,1,0:T(4,128)}, u32[]{:S(2)}) copy-start(f32[2,2,4,4096]{3,2,1,0:T(4,128)} %refs_8_.1) | copy-start | bytes 786436
  0.0 6.7 %copy-start.3 = (s32[2,4096]{1,0:T(2,128)S(1)}, s32[2,4096]{1,0:T(2,128)}, u32[]{:S(2)}) copy-start(s32[2,4096]{1,0:T(2,128)} %refs_2_.1) | copy-start | bytes 98308
  0.0 6.7 %collective-permute-start = (f32[2,16,4,256]{3,2,1,0:T(4,128)}, f32[2,16,4,256]{3,2,1,0:T(4,128)S(1)}, u32[]{:S(2)}, u32[]{:S(2)}) collective-permute-start(f32[2,16,4,256]{3,2,1,0:T(4,128)} %refs_0_.1), channel_id=1, source_target_pairs={{1,0},{0,1},{3,2},{2,3},{5,4},{4,5},{7,6},{6,7},{9,8},{8,9},{11,10... | collective-permute-start | bytes 393224 | tf_op jit(solution)/shard_map/ppermute | solution.py:438
  12.0 1.4 %collective-permute-start.1 = (f32[88,256]{1,0:T(8,128)S(1)}, f32[88,256]{1,0:T(8,128)S(1)}, u32[]{:S(2)}, u32[]{:S(2)}) collective-permute-start(f32[88,256]{1,0:T(8,128)S(1)} %get-tuple-element.35), channel_id=1, source_target_pairs={{0,2},{2,0},{4,6},{6,4},{8,10},{10,8},{12,14},{14,12},{1,3},{3,1},... | collective-permute-start | bytes 270344 | tf_op jit(solution)/shard_map/ppermute | solution.py:432
  13.3 4.7 %collective-permute-start.2 = (f32[88,256]{1,0:T(8,128)S(1)}, f32[88,256]{1,0:T(8,128)S(1)}, u32[]{:S(2)}, u32[]{:S(2)}) collective-permute-start(f32[88,256]{1,0:T(8,128)S(1)} %add.42), channel_id=1, source_target_pairs={{1,0},{0,1},{3,2},{2,3},{5,4},{4,5},{7,6},{6,7},{9,8},{8,9},{11,10... | collective-permute-start | bytes 270344 | tf_op jit(solution)/shard_map/ppermute | solution.py:438
  17.0 1.4 %collective-permute-start.3 = (f32[88,256]{1,0:T(8,128)S(1)}, f32[88,256]{1,0:T(8,128)S(1)}, u32[]{:S(2)}, u32[]{:S(2)}) collective-permute-start(f32[88,256]{1,0:T(8,128)S(1)} %get-tuple-element.40), channel_id=1, source_target_pairs={{0,2},{2,0},{4,6},{6,4},{8,10},{10,8},{12,14},{14,12},{1,3},{3,1},... | collective-permute-start | bytes 270344 | tf_op jit(solution)/shard_map/ppermute | solution.py:432
  18.4 10.3 %collective-permute-start.6 = (f32[88,256]{1,0:T(8,128)S(1)}, f32[88,256]{1,0:T(8,128)S(1)}, u32[]{:S(2)}, u32[]{:S(2)}) collective-permute-start(f32[88,256]{1,0:T(8,128)S(1)} %add.44), channel_id=1, source_target_pairs={{0,8},{2,10},{4,12},{6,14},{8,0},{10,2},{12,4},{14,6},{1,9},{3,11}... | collective-permute-start | bytes 270344 | tf_op jit(solution)/shard_map/ppermute | solution.py:448
  21.1 7.6 %collective-permute-start.5 = (f32[88,256]{1,0:T(8,128)S(1)}, f32[88,256]{1,0:T(8,128)S(1)}, u32[]{:S(2)}, u32[]{:S(2)}) collective-permute-start(f32[88,256]{1,0:T(8,128)S(1)} %add.44), channel_id=1, source_target_pairs={{0,12},{2,14},{4,8},{6,10},{8,4},{10,6},{12,0},{14,2},{1,13},{3,15... | collective-permute-start | bytes 270344 | tf_op jit(solution)/shard_map/ppermute | solution.py:448
  22.4 6.9 %collective-permute-start.4 = (f32[88,256]{1,0:T(8,128)S(1)}, f32[88,256]{1,0:T(8,128)S(1)}, u32[]{:S(2)}, u32[]{:S(2)}) collective-permute-start(f32[88,256]{1,0:T(8,128)S(1)} %add.44), channel_id=1, source_target_pairs={{0,4},{2,6},{4,0},{6,2},{8,12},{10,14},{12,8},{14,10},{1,5},{3,7},... | collective-permute-start | bytes 270344 | tf_op jit(solution)/shard_map/ppermute | solution.py:448
  29.5 4.6 %collective-permute-start.7 = (f32[48,256]{1,0:T(8,128)S(1)}, f32[48,256]{1,0:T(8,128)S(1)}, u32[]{:S(2)}, u32[]{:S(2)}) collective-permute-start(f32[48,256]{1,0:T(8,128)S(1)} %constant_dynamic-update-slice_fusion), channel_id=1, source_target_pairs={{1,0},{0,1},{3,2},{2,3},{5,4},{4,5},{7,6},{6,7},{9,8},{8,9},{11,10... | collective-permute-start | bytes 147464 | tf_op jit(solution)/shard_map/ppermute | solution.py:438
  30.0 4.1 %collective-permute-start.9 = (f32[48,256]{1,0:T(8,128)S(1)}, f32[48,256]{1,0:T(8,128)S(1)}, u32[]{:S(2)}, u32[]{:S(2)}) collective-permute-start(f32[48,256]{1,0:T(8,128)S(1)} %constant_dynamic-update-slice_fusion), channel_id=1, source_target_pairs={{3,0},{2,1},{1,2},{0,3},{7,4},{6,5},{5,6},{4,7},{11,8},{10,9},{9,1... | collective-permute-start | bytes 147464 | tf_op jit(solution)/shard_map/ppermute | solution.py:442
  30.2 3.9 %collective-permute-start.8 = (f32[48,256]{1,0:T(8,128)S(1)}, f32[48,256]{1,0:T(8,128)S(1)}, u32[]{:S(2)}, u32[]{:S(2)}) collective-permute-start(f32[48,256]{1,0:T(8,128)S(1)} %constant_dynamic-update-slice_fusion), channel_id=1, source_target_pairs={{0,2},{2,0},{4,6},{6,4},{8,10},{10,8},{12,14},{14,12},{1,3},{3,1},... | collective-permute-start | bytes 147464 | tf_op jit(solution)/shard_map/ppermute | solution.py:432
  38.9 1.4 %collective-permute-start.10 = (f32[88,256]{1,0:T(8,128)S(1)}, f32[88,256]{1,0:T(8,128)S(1)}, u32[]{:S(2)}, u32[]{:S(2)}) collective-permute-start(f32[88,256]{1,0:T(8,128)S(1)} %get-tuple-element.43), channel_id=1, source_target_pairs={{0,2},{2,0},{4,6},{6,4},{8,10},{10,8},{12,14},{14,12},{1,3},{3,1},... | collective-permute-start | bytes 270344 | tf_op jit(solution)/shard_map/ppermute | solution.py:432
  40.3 4.9 %collective-permute-start.11 = (f32[88,256]{1,0:T(8,128)S(1)}, f32[88,256]{1,0:T(8,128)S(1)}, u32[]{:S(2)}, u32[]{:S(2)}) collective-permute-start(f32[88,256]{1,0:T(8,128)S(1)} %add.49), channel_id=1, source_target_pairs={{1,0},{0,1},{3,2},{2,3},{5,4},{4,5},{7,6},{6,7},{9,8},{8,9},{11,10... | collective-permute-start | bytes 270344 | tf_op jit(solution)/shard_map/ppermute | solution.py:438
  43.3 1.9 %collective-permute-start.12 = (f32[88,256]{1,0:T(8,128)S(1)}, f32[88,256]{1,0:T(8,128)S(1)}, u32[]{:S(2)}, u32[]{:S(2)}) collective-permute-start(f32[88,256]{1,0:T(8,128)S(1)} %get-tuple-element.48), channel_id=1, source_target_pairs={{0,2},{2,0},{4,6},{6,4},{8,10},{10,8},{12,14},{14,12},{1,3},{3,1},... | collective-permute-start | bytes 270344 | tf_op jit(solution)/shard_map/ppermute | solution.py:432
  45.2 9.7 %collective-permute-start.15 = (f32[88,256]{1,0:T(8,128)S(1)}, f32[88,256]{1,0:T(8,128)S(1)}, u32[]{:S(2)}, u32[]{:S(2)}) collective-permute-start(f32[88,256]{1,0:T(8,128)S(1)} %add.51), channel_id=1, source_target_pairs={{0,8},{2,10},{4,12},{6,14},{8,0},{10,2},{12,4},{14,6},{1,9},{3,11}... | collective-permute-start | bytes 270344 | tf_op jit(solution)/shard_map/ppermute | solution.py:448
  48.6 6.9 %collective-permute-start.14 = (f32[88,256]{1,0:T(8,128)S(1)}, f32[88,256]{1,0:T(8,128)S(1)}, u32[]{:S(2)}, u32[]{:S(2)}) collective-permute-start(f32[88,256]{1,0:T(8,128)S(1)} %add.51), channel_id=1, source_target_pairs={{0,12},{2,14},{4,8},{6,10},{8,4},{10,6},{12,0},{14,2},{1,13},{3,15... | collective-permute-start | bytes 270344 | tf_op jit(solution)/shard_map/ppermute | solution.py:448
  49.1 7.4 %collective-permute-start.13 = (f32[88,256]{1,0:T(8,128)S(1)}, f32[88,256]{1,0:T(8,128)S(1)}, u32[]{:S(2)}, u32[]{:S(2)}) collective-permute-start(f32[88,256]{1,0:T(8,128)S(1)} %add.51), channel_id=1, source_target_pairs={{0,4},{2,6},{4,0},{6,2},{8,12},{10,14},{12,8},{14,10},{1,5},{3,7},... | collective-permute-start | bytes 270344 | tf_op jit(solution)/shard_map/ppermute | solution.py:448
  56.6 1.3 %collective-permute-start.16 = (f32[48,256]{1,0:T(8,128)S(1)}, f32[48,256]{1,0:T(8,128)S(1)}, u32[]{:S(2)}, u32[]{:S(2)}) collective-permute-start(f32[48,256]{1,0:T(8,128)S(1)} %constant_dynamic-update-slice_fusion.6.own_ref), channel_id=1, source_target_pairs={{0,2},{2,0},{4,6},{6,4},{8,10},{10,8},{12,14},{14,12},{1,3},{3,1},... | collective-permute-start | bytes 147464 | tf_op jit(solution)/shard_map/ppermute | solution.py:432

commit v5 on v4

--- a/solution.py
+++ b/solution.py
@@ -484,8 +484,9 @@
         kept = lax.optimization_barrier(kept) + other_core(other)
         coefs = solve(over_chips(kept))
         if number < ITERS - 1:
-            across = [from_later(coefs, k, True) for k in range(1, blocks)]
-            along = [from_later(coefs, k) for k in range(1, blocks)]
+            short = coefs.astype(BF16)
+            across = [from_later(short, k, True).astype(F32) for k in range(1, blocks)]
+            along = [from_later(short, k).astype(F32) for k in range(1, blocks)]
             beside = other_core(coefs)
             inputs = [current, fit, jnp.concatenate([coefs] + along, axis=1), jnp.concatenate([beside] + across, axis=1), picks]
         else:

time: 59 us -> 58.5 us (level)
    ppermute x4, waiting for transfers between devices: 5.22 us -> 4.34 us  [from_later(): lax.ppermute(value, 'bl', [((j + k) % count, j) for j in range(count)])]
  transfers between devices with their start and end apart: 17 -> 17, of which waited for: 13 -> 12; matrix products, arithmetic and copies ran while one was open for 0% -> 0% of each run, Pallas kernels for 13% -> 13%
where the time goes in v5:
time: 58.5 us; the launch traced here: 58.4 us
  waiting for transfers between devices  22.4 us (38%)
  Pallas kernels  18.4 us (31%)
  starting transfers between devices  17 us (29%)
    ppermute x6, waiting for transfers between devices, over_chips(): lax.ppermute(v, 'chan', [(j, j ^ 2 * k) for j in range(count)])  14.1 us
    pallas_call x2, Pallas kernels, sweep(): pl.pallas_call(partial(sweep_kernel, first, blocks, owned, SWEEP_TILE), i...  10.1 us
    ppermute x6, starting transfers between devices, over_chips(): lax.ppermute(v, 'chan', [(j, j ^ 2 * k) for j in range(count)])  8.21 us
    ppermute x4, starting transfers between devices, from_later(): lax.ppermute(value, 'bl', [((j + k) % count, j) for j in range(count)])  6.67 us
    ppermute x4, waiting for transfers between devices, from_later(): lax.ppermute(value, 'bl', [((j + k) % count, j) for j in range(count)])  4.34 us
    ppermute x6, waiting for transfers between devices, other_core(): return lax.ppermute(value, 'chan', [(j, j ^ 1) for j in range(count)])  3.99 us
    pallas_call x2, Pallas kernels, own_moments(): pl.pallas_call(partial(own_kernel, blocks, OWN_CHUNK), in_specs=[vmem] *...  3.74 us
    pallas_call x1, Pallas kernels, prepare(): pl.pallas_call(partial(prep_kernel, total, channels, chunk), in_specs=[pl...  3.65 us
  transfers between devices with their start and end apart: 17, of which 12 were waited for; matrix products, arithmetic and copies ran while one was open for 0% of the time, Pallas kernels for 13%

profile of v5, /device:TPU:0, one launch (start us, length us, event | category | flops | bytes accessed | tf_op | source)
XLA Modules:
  0.0 58.4 jit_solution(10984058736784799919)
XLA Ops:
  0.0 3.0 %collective-permute-start = (f32[2,16,4,256]{3,2,1,0:T(4,128)}, f32[2,16,4,256]{3,2,1,0:T(4,128)S(1)}, u32[]{:S(2)}, u32[]{:S(2)}) collective-permute-start(f32[2,16,4,256]{3,2,1,0:T(4,128)} %refs_0_.1), channel_id=1, source_target_pairs={{1,0},{0,1},{3,2},{2,3},{5,4},{4,5},{7,6},{6,7},{9,8},{8,9},{11,10... | collective-permute-start | bytes 393224 | tf_op jit(solution)/shard_map/ppermute | solution.py:438
  3.0 3.6 %prepare.1 = (f32[2,2,64,4096]{3,2,1,0:T(8,128)S(1)}, f32[64,4096]{1,0:T(8,128)S(1)}, f32[80,64]{1,0:T(8,128)S(1)}, f32[48,64]{1,0:T(8,128)S(1)}, f32[128,96]{1,0:T(8,128)S(1)}) custom-call(s32[32]{0:T(128)} %bitcast.7, bf16[32,2,2,128,128]{4,3,2,1,0:T(8,128)(2,1)} %bitcast.6, s32[4,4096]{1,0:T(4,128)} %refs_7_.1), custom_call_target="tpu_custom_call" | custom-call | tf_op jit(solution)/shard_map/prepare/pallas_call | solution.py:148
  6.8 5.2 %sweep.2 = (f32[88,256]{1,0:T(8,128)S(1)}, f32[88,256]{1,0:T(8,128)S(1)}, f32[128,512]{1,0:T(8,128)S(1)}, bf16[192,8192]{1,0:T(8,128)(2,1)S(1)}, bf16[512,8192]{1,0:T(8,128)(2,1)S(1)}) custom-call(f32[2,16,4,256]{3,2,1,0:T(4,128)S(1)} %copy-done.2, f32[2,16,4,256]{3,2,1,0:T(4,128)S(1)} %collective-permute-done.refs_1_, s32[2,4096]{1,0:T(2,128)S(1)} %copy-done.3, ...), custom_call_target="tpu_custom_call" | custom-call | tf_op jit(solution)/shard_map/sweep/pallas_call | solution.py:371
  12.1 1.3 %collective-permute-done.1 = f32[88,256]{1,0:T(8,128)S(1)} collective-permute-done((f32[88,256]{1,0:T(8,128)S(1)}, f32[88,256]{1,0:T(8,128)S(1)}, u32[]{:S(2)}, u32[]{:S(2)}) %collective-permute-start.1) | collective-permute-done | bytes 90144 | tf_op jit(solution)/shard_map/ppermute | solution.py:432
  13.3 1.8 %collective-permute-start.2 = (f32[88,256]{1,0:T(8,128)S(1)}, f32[88,256]{1,0:T(8,128)S(1)}, u32[]{:S(2)}, u32[]{:S(2)}) collective-permute-start(f32[88,256]{1,0:T(8,128)S(1)} %add.42), channel_id=1, source_target_pairs={{1,0},{0,1},{3,2},{2,3},{5,4},{4,5},{7,6},{6,7},{9,8},{8,9},{11,10... | collective-permute-start | bytes 270344 | tf_op jit(solution)/shard_map/ppermute | solution.py:438
  15.2 1.9 %own_moments.2 = (f32[88,256]{1,0:T(8,128)S(1)}, f32[88,256]{1,0:T(8,128)S(1)}) custom-call(bf16[512,8192]{1,0:T(8,128)(2,1)S(1)} %get-tuple-element.33.picks_ref.refs_4_, bf16[192,8192]{1,0:T(8,128)(2,1)S(1)} %get-tuple-element.37.terms_ref, f32[128,512]{1,0:T(8,128)S(1)} %get-tuple-element.31.current_ref.refs_0_, ...), custom_call_target="tpu_custom_call" | custom-call | flops 805306368 | bytes 7340032 | tf_op jit(solution)/shard_map/own_moments/pallas_call | solution.py:344
  17.1 1.0 %collective-permute-done.2 = f32[88,256]{1,0:T(8,128)S(1)} collective-permute-done((f32[88,256]{1,0:T(8,128)S(1)}, f32[88,256]{1,0:T(8,128)S(1)}, u32[]{:S(2)}, u32[]{:S(2)}) %collective-permute-start.2) | collective-permute-done | bytes 90144 | tf_op jit(solution)/shard_map/ppermute | solution.py:438
  18.1 0.3 collective-permute-done.3
  18.4 2.7 %collective-permute-start.6 = (f32[88,256]{1,0:T(8,128)S(1)}, f32[88,256]{1,0:T(8,128)S(1)}, u32[]{:S(2)}, u32[]{:S(2)}) collective-permute-start(f32[88,256]{1,0:T(8,128)S(1)} %add.44), channel_id=1, source_target_pairs={{0,8},{2,10},{4,12},{6,14},{8,0},{10,2},{12,4},{14,6},{1,9},{3,11}... | collective-permute-start | bytes 270344 | tf_op jit(solution)/shard_map/ppermute | solution.py:448
  21.1 1.3 %collective-permute-start.5 = (f32[88,256]{1,0:T(8,128)S(1)}, f32[88,256]{1,0:T(8,128)S(1)}, u32[]{:S(2)}, u32[]{:S(2)}) collective-permute-start(f32[88,256]{1,0:T(8,128)S(1)} %add.44), channel_id=1, source_target_pairs={{0,12},{2,14},{4,8},{6,10},{8,4},{10,6},{12,0},{14,2},{1,13},{3,15... | collective-permute-start | bytes 270344 | tf_op jit(solution)/shard_map/ppermute | solution.py:448
  22.4 0.2 collective-permute-start.4
  22.6 6.1 %collective-permute-done.6 = f32[88,256]{1,0:T(8,128)S(1)} collective-permute-done((f32[88,256]{1,0:T(8,128)S(1)}, f32[88,256]{1,0:T(8,128)S(1)}, u32[]{:S(2)}, u32[]{:S(2)}) %collective-permute-start.6) | collective-permute-done | bytes 90144 | tf_op jit(solution)/shard_map/ppermute | solution.py:448
  28.7 0.6 %collective-permute-done.4 = f32[88,256]{1,0:T(8,128)S(1)} collective-permute-done((f32[88,256]{1,0:T(8,128)S(1)}, f32[88,256]{1,0:T(8,128)S(1)}, u32[]{:S(2)}, u32[]{:S(2)}) %collective-permute-start.4) | collective-permute-done | bytes 90144 | tf_op jit(solution)/shard_map/ppermute | solution.py:448
  29.5 0.5 collective-permute-start.7
  30.0 0.2 collective-permute-start.9
  30.2 1.5 %collective-permute-start.8 = (f32[48,256]{1,0:T(8,128)S(1)}, f32[48,256]{1,0:T(8,128)S(1)}, u32[]{:S(2)}, u32[]{:S(2)}) collective-permute-start(f32[48,256]{1,0:T(8,128)S(1)} %constant_dynamic-update-slice_fusion), channel_id=1, source_target_pairs={{0,2},{2,0},{4,6},{6,4},{8,10},{10,8},{12,14},{14,12},{1,3},{3,1},... | collective-permute-start | bytes 147464 | tf_op jit(solution)/shard_map/ppermute | solution.py:432
  31.7 1.8 %collective-permute-done.7 = bf16[48,256]{1,0:T(8,128)(2,1)S(1)} collective-permute-done((bf16[48,256]{1,0:T(8,128)(2,1)S(1)}, bf16[48,256]{1,0:T(8,128)(2,1)S(1)}, u32[]{:S(2)}, u32[]{:S(2)}) %collective-permute-start.7) | collective-permute-done | bytes 24608 | tf_op jit(solution)/shard_map/ppermute | solution.py:438
  33.6 4.8 %sweep.3 = (f32[88,256]{1,0:T(8,128)S(1)}, f32[88,256]{1,0:T(8,128)S(1)}, f32[128,512]{1,0:T(8,128)S(1)}, bf16[192,8192]{1,0:T(8,128)(2,1)S(1)}) custom-call(f32[128,512]{1,0:T(8,128)S(1)} %get-tuple-element.31.current_ref.refs_0_, f32[128,96]{1,0:T(8,128)S(1)} %get-tuple-element.32.refs_1_.fit_ref, f32[48,512]{1,0:T(8,128)S(1)} %pad_maximum_fusion.refs_2_, ...), custom_call_target="tpu_custom_call" | custom-call | tf_op jit(solution)/shard_map/sweep/pallas_call | solution.py:371
  38.4 0.1 collective-permute-start.10
  38.6 1.2 %collective-permute-done.10 = f32[88,256]{1,0:T(8,128)S(1)} collective-permute-done((f32[88,256]{1,0:T(8,128)S(1)}, f32[88,256]{1,0:T(8,128)S(1)}, u32[]{:S(2)}, u32[]{:S(2)}) %collective-permute-start.10) | collective-permute-done | bytes 90144 | tf_op jit(solution)/shard_map/ppermute | solution.py:432
  39.8 1.3 %collective-permute-start.11 = (f32[88,256]{1,0:T(8,128)S(1)}, f32[88,256]{1,0:T(8,128)S(1)}, u32[]{:S(2)}, u32[]{:S(2)}) collective-permute-start(f32[88,256]{1,0:T(8,128)S(1)} %add.49), channel_id=1, source_target_pairs={{1,0},{0,1},{3,2},{2,3},{5,4},{4,5},{7,6},{6,7},{9,8},{8,9},{11,10... | collective-permute-start | bytes 270344 | tf_op jit(solution)/shard_map/ppermute | solution.py:438
  41.1 1.9 %own_moments.3 = (f32[88,256]{1,0:T(8,128)S(1)}, f32[88,256]{1,0:T(8,128)S(1)}) custom-call(bf16[512,8192]{1,0:T(8,128)(2,1)S(1)} %get-tuple-element.33.picks_ref.refs_4_, bf16[192,8192]{1,0:T(8,128)(2,1)S(1)} %get-tuple-element.45.terms_ref, f32[128,512]{1,0:T(8,128)S(1)} %get-tuple-element.41.current_ref.before_ref, ...), custom_call_target="tpu_custom_call" | custom-call | flops 805306368 | bytes 7340032 | tf_op jit(solution)/shard_map/own_moments/pallas_call | solution.py:344
  43.0 0.1 collective-permute-start.12
  43.1 1.5 %collective-permute-done.11 = f32[88,256]{1,0:T(8,128)S(1)} collective-permute-done((f32[88,256]{1,0:T(8,128)S(1)}, f32[88,256]{1,0:T(8,128)S(1)}, u32[]{:S(2)}, u32[]{:S(2)}) %collective-permute-start.11) | collective-permute-done | bytes 90144 | tf_op jit(solution)/shard_map/ppermute | solution.py:438
  44.6 3.3 %collective-permute-start.15 = (f32[88,256]{1,0:T(8,128)S(1)}, f32[88,256]{1,0:T(8,128)S(1)}, u32[]{:S(2)}, u32[]{:S(2)}) collective-permute-start(f32[88,256]{1,0:T(8,128)S(1)} %add.51), channel_id=1, source_target_pairs={{0,8},{2,10},{4,12},{6,14},{8,0},{10,2},{12,4},{14,6},{1,9},{3,11}... | collective-permute-start | bytes 270344 | tf_op jit(solution)/shard_map/ppermute | solution.py:448
  47.9 0.5 collective-permute-start.14
  48.4 0.2 collective-permute-start.13
  48.6 6.0 %collective-permute-done.15 = f32[88,256]{1,0:T(8,128)S(1)} collective-permute-done((f32[88,256]{1,0:T(8,128)S(1)}, f32[88,256]{1,0:T(8,128)S(1)}, u32[]{:S(2)}, u32[]{:S(2)}) %collective-permute-start.15) | collective-permute-done | bytes 90144 | tf_op jit(solution)/shard_map/ppermute | solution.py:448
  54.6 0.4 collective-permute-done.14
  55.0 1.0 %collective-permute-done.13 = f32[88,256]{1,0:T(8,128)S(1)} collective-permute-done((f32[88,256]{1,0:T(8,128)S(1)}, f32[88,256]{1,0:T(8,128)S(1)}, u32[]{:S(2)}, u32[]{:S(2)}) %collective-permute-start.13) | collective-permute-done | bytes 90144 | tf_op jit(solution)/shard_map/ppermute | solution.py:448
  56.3 1.2 %collective-permute-done.16.other_ref = f32[48,256]{1,0:T(8,128)S(1)} collective-permute-done((f32[48,256]{1,0:T(8,128)S(1)}, f32[48,256]{1,0:T(8,128)S(1)}, u32[]{:S(2)}, u32[]{:S(2)}) %collective-permute-start.16) | collective-permute-done | bytes 49184 | tf_op jit(solution)/shard_map/ppermute | solution.py:432
  57.5 0.9 %finish.1 = f32[2,16,4,256]{3,2,1,0:T(4,128)} custom-call(f32[128,512]{1,0:T(8,128)S(1)} %get-tuple-element.41.current_ref.before_ref, f32[128,96]{1,0:T(8,128)S(1)} %get-tuple-element.32.refs_1_.fit_ref, f32[48,256]{1,0:T(8,128)S(1)} %constant_dynamic-update-slice_fusion.6.own_ref, f32[48,256]{1,0:T(8,128)S(1)} %collective-permute-done.16.other_ref), custom_call_target="tpu_custom_call" | custom-call | tf_op jit(solution)/shard_map/finish/pallas_call | solution.py:398
  (41 shorter events, 0.7 us)
Async XLA Ops:
  0.0 6.7 %copy-start.2 = (f32[2,16,4,256]{3,2,1,0:T(4,128)S(1)}, f32[2,16,4,256]{3,2,1,0:T(4,128)}, u32[]{:S(2)}) copy-start(f32[2,16,4,256]{3,2,1,0:T(4,128)} %refs_0_.1) | copy-start | bytes 393220
  0.0 6.7 %copy-start.1 = (s32[4,4096]{1,0:T(4,128)S(1)}, s32[4,4096]{1,0:T(4,128)}, u32[]{:S(2)}) copy-start(s32[4,4096]{1,0:T(4,128)} %refs_7_.1) | copy-start | bytes 196612
  0.0 6.7 %copy-start = (f32[2,2,4,4096]{3,2,1,0:T(4,128)S(1)}, f32[2,2,4,4096]{3,2,1,0:T(4,128)}, u32[]{:S(2)}) copy-start(f32[2,2,4,4096]{3,2,1,0:T(4,128)} %refs_8_.1) | copy-start | bytes 786436
  0.0 6.7 %copy-start.3 = (s32[2,4096]{1,0:T(2,128)S(1)}, s32[2,4096]{1,0:T(2,128)}, u32[]{:S(2)}) copy-start(s32[2,4096]{1,0:T(2,128)} %refs_2_.1) | copy-start | bytes 98308
  0.0 6.7 %collective-permute-start = (f32[2,16,4,256]{3,2,1,0:T(4,128)}, f32[2,16,4,256]{3,2,1,0:T(4,128)S(1)}, u32[]{:S(2)}, u32[]{:S(2)}) collective-permute-start(f32[2,16,4,256]{3,2,1,0:T(4,128)} %refs_0_.1), channel_id=1, source_target_pairs={{1,0},{0,1},{3,2},{2,3},{5,4},{4,5},{7,6},{6,7},{9,8},{8,9},{11,10... | collective-permute-start | bytes 393224 | tf_op jit(solution)/shard_map/ppermute | solution.py:438
  12.0 1.4 %collective-permute-start.1 = (f32[88,256]{1,0:T(8,128)S(1)}, f32[88,256]{1,0:T(8,128)S(1)}, u32[]{:S(2)}, u32[]{:S(2)}) collective-permute-start(f32[88,256]{1,0:T(8,128)S(1)} %get-tuple-element.35), channel_id=1, source_target_pairs={{0,2},{2,0},{4,6},{6,4},{8,10},{10,8},{12,14},{14,12},{1,3},{3,1},... | collective-permute-start | bytes 270344 | tf_op jit(solution)/shard_map/ppermute | solution.py:432
  13.3 4.7 %collective-permute-start.2 = (f32[88,256]{1,0:T(8,128)S(1)}, f32[88,256]{1,0:T(8,128)S(1)}, u32[]{:S(2)}, u32[]{:S(2)}) collective-permute-start(f32[88,256]{1,0:T(8,128)S(1)} %add.42), channel_id=1, source_target_pairs={{1,0},{0,1},{3,2},{2,3},{5,4},{4,5},{7,6},{6,7},{9,8},{8,9},{11,10... | collective-permute-start | bytes 270344 | tf_op jit(solution)/shard_map/ppermute | solution.py:438
  17.0 1.4 %collective-permute-start.3 = (f32[88,256]{1,0:T(8,128)S(1)}, f32[88,256]{1,0:T(8,128)S(1)}, u32[]{:S(2)}, u32[]{:S(2)}) collective-permute-start(f32[88,256]{1,0:T(8,128)S(1)} %get-tuple-element.40), channel_id=1, source_target_pairs={{0,2},{2,0},{4,6},{6,4},{8,10},{10,8},{12,14},{14,12},{1,3},{3,1},... | collective-permute-start | bytes 270344 | tf_op jit(solution)/shard_map/ppermute | solution.py:432
  18.4 10.3 %collective-permute-start.6 = (f32[88,256]{1,0:T(8,128)S(1)}, f32[88,256]{1,0:T(8,128)S(1)}, u32[]{:S(2)}, u32[]{:S(2)}) collective-permute-start(f32[88,256]{1,0:T(8,128)S(1)} %add.44), channel_id=1, source_target_pairs={{0,8},{2,10},{4,12},{6,14},{8,0},{10,2},{12,4},{14,6},{1,9},{3,11}... | collective-permute-start | bytes 270344 | tf_op jit(solution)/shard_map/ppermute | solution.py:448
  21.1 7.6 %collective-permute-start.5 = (f32[88,256]{1,0:T(8,128)S(1)}, f32[88,256]{1,0:T(8,128)S(1)}, u32[]{:S(2)}, u32[]{:S(2)}) collective-permute-start(f32[88,256]{1,0:T(8,128)S(1)} %add.44), channel_id=1, source_target_pairs={{0,12},{2,14},{4,8},{6,10},{8,4},{10,6},{12,0},{14,2},{1,13},{3,15... | collective-permute-start | bytes 270344 | tf_op jit(solution)/shard_map/ppermute | solution.py:448
  22.4 6.9 %collective-permute-start.4 = (f32[88,256]{1,0:T(8,128)S(1)}, f32[88,256]{1,0:T(8,128)S(1)}, u32[]{:S(2)}, u32[]{:S(2)}) collective-permute-start(f32[88,256]{1,0:T(8,128)S(1)} %add.44), channel_id=1, source_target_pairs={{0,4},{2,6},{4,0},{6,2},{8,12},{10,14},{12,8},{14,10},{1,5},{3,7},... | collective-permute-start | bytes 270344 | tf_op jit(solution)/shard_map/ppermute | solution.py:448
  29.5 4.1 %collective-permute-start.7 = (bf16[48,256]{1,0:T(8,128)(2,1)S(1)}, bf16[48,256]{1,0:T(8,128)(2,1)S(1)}, u32[]{:S(2)}, u32[]{:S(2)}) collective-permute-start(bf16[48,256]{1,0:T(8,128)(2,1)S(1)} %convert_element_type.9), channel_id=1, source_target_pairs={{1,0},{0,1},{3,2},{2,3},{5,4},{4,5},{7,6},{6,7},{9,8},{8,9},{11,10... | collective-permute-start | bytes 73736 | tf_op jit(solution)/shard_map/ppermute | solution.py:438
  30.0 3.5 %collective-permute-start.9 = (bf16[48,256]{1,0:T(8,128)(2,1)S(1)}, bf16[48,256]{1,0:T(8,128)(2,1)S(1)}, u32[]{:S(2)}, u32[]{:S(2)}) collective-permute-start(bf16[48,256]{1,0:T(8,128)(2,1)S(1)} %convert_element_type.9), channel_id=1, source_target_pairs={{3,0},{2,1},{1,2},{0,3},{7,4},{6,5},{5,6},{4,7},{11,8},{10,9},{9,1... | collective-permute-start | bytes 73736 | tf_op jit(solution)/shard_map/ppermute | solution.py:442
  30.2 3.4 %collective-permute-start.8 = (f32[48,256]{1,0:T(8,128)S(1)}, f32[48,256]{1,0:T(8,128)S(1)}, u32[]{:S(2)}, u32[]{:S(2)}) collective-permute-start(f32[48,256]{1,0:T(8,128)S(1)} %constant_dynamic-update-slice_fusion), channel_id=1, source_target_pairs={{0,2},{2,0},{4,6},{6,4},{8,10},{10,8},{12,14},{14,12},{1,3},{3,1},... | collective-permute-start | bytes 147464 | tf_op jit(solution)/shard_map/ppermute | solution.py:432
  38.4 1.4 %collective-permute-start.10 = (f32[88,256]{1,0:T(8,128)S(1)}, f32[88,256]{1,0:T(8,128)S(1)}, u32[]{:S(2)}, u32[]{:S(2)}) collective-permute-start(f32[88,256]{1,0:T(8,128)S(1)} %get-tuple-element.43), channel_id=1, source_target_pairs={{0,2},{2,0},{4,6},{6,4},{8,10},{10,8},{12,14},{14,12},{1,3},{3,1},... | collective-permute-start | bytes 270344 | tf_op jit(solution)/shard_map/ppermute | solution.py:432
  39.8 4.7 %collective-permute-start.11 = (f32[88,256]{1,0:T(8,128)S(1)}, f32[88,256]{1,0:T(8,128)S(1)}, u32[]{:S(2)}, u32[]{:S(2)}) collective-permute-start(f32[88,256]{1,0:T(8,128)S(1)} %add.49), channel_id=1, source_target_pairs={{1,0},{0,1},{3,2},{2,3},{5,4},{4,5},{7,6},{6,7},{9,8},{8,9},{11,10... | collective-permute-start | bytes 270344 | tf_op jit(solution)/shard_map/ppermute | solution.py:438
  43.0 1.6 %collective-permute-start.12 = (f32[88,256]{1,0:T(8,128)S(1)}, f32[88,256]{1,0:T(8,128)S(1)}, u32[]{:S(2)}, u32[]{:S(2)}) collective-permute-start(f32[88,256]{1,0:T(8,128)S(1)} %get-tuple-element.48), channel_id=1, source_target_pairs={{0,2},{2,0},{4,6},{6,4},{8,10},{10,8},{12,14},{14,12},{1,3},{3,1},... | collective-permute-start | bytes 270344 | tf_op jit(solution)/shard_map/ppermute | solution.py:432
  44.6 10.0 %collective-permute-start.15 = (f32[88,256]{1,0:T(8,128)S(1)}, f32[88,256]{1,0:T(8,128)S(1)}, u32[]{:S(2)}, u32[]{:S(2)}) collective-permute-start(f32[88,256]{1,0:T(8,128)S(1)} %add.51), channel_id=1, source_target_pairs={{0,8},{2,10},{4,12},{6,14},{8,0},{10,2},{12,4},{14,6},{1,9},{3,11}... | collective-permute-start | bytes 270344 | tf_op jit(solution)/shard_map/ppermute | solution.py:448
  47.9 7.1 %collective-permute-start.14 = (f32[88,256]{1,0:T(8,128)S(1)}, f32[88,256]{1,0:T(8,128)S(1)}, u32[]{:S(2)}, u32[]{:S(2)}) collective-permute-start(f32[88,256]{1,0:T(8,128)S(1)} %add.51), channel_id=1, source_target_pairs={{0,12},{2,14},{4,8},{6,10},{8,4},{10,6},{12,0},{14,2},{1,13},{3,15... | collective-permute-start | bytes 270344 | tf_op jit(solution)/shard_map/ppermute | solution.py:448
  48.4 7.6 %collective-permute-start.13 = (f32[88,256]{1,0:T(8,128)S(1)}, f32[88,256]{1,0:T(8,128)S(1)}, u32[]{:S(2)}, u32[]{:S(2)}) collective-permute-start(f32[88,256]{1,0:T(8,128)S(1)} %add.51), channel_id=1, source_target_pairs={{0,4},{2,6},{4,0},{6,2},{8,12},{10,14},{12,8},{14,10},{1,5},{3,7},... | collective-permute-start | bytes 270344 | tf_op jit(solution)/shard_map/ppermute | solution.py:448
  56.2 1.3 %collective-permute-start.16 = (f32[48,256]{1,0:T(8,128)S(1)}, f32[48,256]{1,0:T(8,128)S(1)}, u32[]{:S(2)}, u32[]{:S(2)}) collective-permute-start(f32[48,256]{1,0:T(8,128)S(1)} %constant_dynamic-update-slice_fusion.6.own_ref), channel_id=1, source_target_pairs={{0,2},{2,0},{4,6},{6,4},{8,10},{10,8},{12,14},{14,12},{1,3},{3,1},... | collective-permute-start | bytes 147464 | tf_op jit(solution)/shard_map/ppermute | solution.py:432
